TPU v7x, 128 devices: a whole 4x4x4 slice. The times are simulated.
128 devices in a mesh: dp: 8 (over z, x_hi), fsdp: 16 (over x_lo, y, core).
Axes of the slice: x: 4 (x_hi: 2, x_lo: 2; x = x_hi * 2 + x_lo), y: 4, z: 4, core: 2. Of those that a mesh axis runs over, the one named last changes fastest.
Arguments:
- tokens: bfloat16 [65536, 768], P(('dp', 'fsdp')), may hold values from -6 to 6
- chip_lengths: int32 [256], P(('dp', 'fsdp')), may hold values from 64 to 256, as said below
- chip_ids: int32 [256], P(('dp', 'fsdp')), may hold values from 0 to 31, as said below
- positions: int32 [65536], P(('dp', 'fsdp')), may hold values from -1 to 1023, as said below
- ln1_gain: bfloat16 [768], P(('dp', 'fsdp')), may hold values from 0.099609375 to 1.8984375
- ln1_bias: bfloat16 [768], P(('dp', 'fsdp')), may hold values from -3 to 3
- qkv_weight: bfloat16 [768, 2304], P(('dp', 'fsdp')), may hold values from -0.21875 to 0.21875
- out_weight: bfloat16 [768, 768], P(('dp', 'fsdp')), may hold values from -0.875 to 0.875
- ln2_gain: bfloat16 [768], P(('dp', 'fsdp')), may hold values from 0.099609375 to 1.8984375
- ln2_bias: bfloat16 [768], P(('dp', 'fsdp')), may hold values from -3 to 3
- fc1_weight: bfloat16 [768, 3072], P(('dp', 'fsdp')), may hold values from -0.21875 to 0.21875
- fc1_bias: bfloat16 [3072], P(('dp', 'fsdp')), may hold values from -3 to 3
- fc2_weight: bfloat16 [3072, 768], P(('dp', 'fsdp')), may hold values from -0.109375 to 0.109375
- fc2_bias: bfloat16 [768], P(('dp', 'fsdp')), may hold values from -3 to 3
- dec_weight: bfloat16 [768, 512], P(('dp', 'fsdp')), may hold values from -0.21875 to 0.21875
- dec_bias: bfloat16 [512], P(('dp', 'fsdp')), may hold values from -3 to 3
- mask_token: bfloat16 [512], P(('dp', 'fsdp')), may hold values from -4 to 4
- grid_cotangent: bfloat16 [256, 1024, 512], P('dp', 'fsdp'), may hold values from -6 to 6
Outputs:
- full_grid: bfloat16 [256, 1024, 512], P('dp', 'fsdp')
- tokens_grad: float32 [65536, 768], P(('dp', 'fsdp'))
- ln1_gain_grad: float32 [768], P(('dp', 'fsdp'))
- ln1_bias_grad: float32 [768], P(('dp', 'fsdp'))
- qkv_weight_grad: float32 [768, 2304], P(('dp', 'fsdp'))
- out_weight_grad: float32 [768, 768], P(('dp', 'fsdp'))
- ln2_gain_grad: float32 [768], P(('dp', 'fsdp'))
- ln2_bias_grad: float32 [768], P(('dp', 'fsdp'))
- fc1_weight_grad: float32 [768, 3072], P(('dp', 'fsdp'))
- fc1_bias_grad: float32 [3072], P(('dp', 'fsdp'))
- fc2_weight_grad: float32 [3072, 768], P(('dp', 'fsdp'))
- fc2_bias_grad: float32 [768], P(('dp', 'fsdp'))
- dec_weight_grad: float32 [768, 512], P(('dp', 'fsdp'))
- dec_bias_grad: float32 [512], P(('dp', 'fsdp'))
- mask_token_grad: float32 [512], P(('dp', 'fsdp'))
Inputs may be any that keep to these rules, and one draw needn't show every extreme that they name: `chip_lengths`: each slot holds one chip of 256 or 64 visible patches; every pack has at least one of each kind; a chip's rows are 2 plus its visible patches. `chip_ids`: within each group of 32 slots (one index of dp) the values are a permutation. `positions`: each chip's first two rows (class and time-location tokens) and the padding rows after the last chip have -1; the other rows of a chip hold distinct cells below 4 times its length.
All inputs are finite; a program needn't handle non-finite values.
Results may differ from a plain program's by a relative error of at most 0.018.
Values may be sent and summed in bfloat16 or wider, within the bound.
A program may use at most 192 MiB of HBM per device.

v0:
```python
from functools import partial

import jax
import jax.numpy as jnp
from jax import lax
from jax.sharding import PartitionSpec as P

D = 768
HEADS = 12
HEAD_DIM = 64
DEC = 512
GRID = 1024


NORM_EPS = 1e-06


def normalize(values):
    center = values - jnp.mean(values, axis=-1, keepdims=True)
    spread = jnp.mean(center * center, axis=-1, keepdims=True)
    return center * lax.rsqrt(spread + NORM_EPS)


def ln_affine(values, gain, bias):
    return normalize(values) * gain + bias


def left_product(left, right):
    return lax.dot_general(
        left, right, (((0,), (0,)), ((), ())), preferred_element_type=jnp.float32
    )


def right_product(left, right):
    return lax.dot_general(
        left, right, (((1,), (1,)), ((), ())), preferred_element_type=jnp.float32
    )


def pack_layout(chip_lengths, positions):
    row_count = positions.shape[0]
    slot_count = chip_lengths.shape[0]
    ends = jnp.cumsum(chip_lengths + 2)
    row_index = jnp.arange(row_count, dtype=jnp.int32)
    segment = jnp.sum((row_index[:, None] >= ends[None, :]).astype(jnp.int32), axis=1)
    target = jnp.where(positions >= 0, segment * GRID + positions, -1)
    cell_index = jnp.arange(slot_count * GRID, dtype=jnp.int32)
    hits = cell_index[:, None] == target[None, :]
    fill_table = hits.astype(jnp.bfloat16)
    covered = jnp.any(hits, axis=1)
    valid = cell_index % GRID < jnp.repeat(4 * chip_lengths, GRID)
    empty_cells = (valid & jnp.logical_not(covered)).astype(jnp.bfloat16)
    return (segment, fill_table, empty_cells)


def layer_forward(weights, tokens, segment):
    gain_one = weights[0].astype(jnp.float32)
    bias_one = weights[1].astype(jnp.float32)
    gain_two = weights[4].astype(jnp.float32)
    bias_two = weights[5].astype(jnp.float32)
    inputs = tokens.astype(jnp.float32)
    token_count = tokens.shape[0]
    normed = ln_affine(inputs, gain_one, bias_one).astype(jnp.bfloat16)
    packed_qkv = jnp.dot(normed, weights[2], preferred_element_type=jnp.float32).astype(
        jnp.bfloat16
    )
    queries = packed_qkv[:, :D].reshape(token_count, HEADS, HEAD_DIM)
    key_heads = packed_qkv[:, D : 2 * D].reshape(token_count, HEADS, HEAD_DIM)
    value_heads = packed_qkv[:, 2 * D :].reshape(token_count, HEADS, HEAD_DIM)
    scores = jnp.einsum(
        "qhd,khd->hqk", queries, key_heads, preferred_element_type=jnp.float32
    ) * HEAD_DIM ** (-0.5)
    same_chip = segment[:, None] == segment[None, :]
    scores = jnp.where(same_chip[None], scores, -1e30)
    peak = jnp.max(scores, axis=-1, keepdims=True)
    raised = jnp.exp(scores - peak)
    attn_probs = raised / jnp.sum(raised, axis=-1, keepdims=True)
    probs_low = attn_probs.astype(jnp.bfloat16)
    mixed = jnp.einsum("hqk,khd->qhd", probs_low, value_heads, preferred_element_type=jnp.float32)
    mixed = mixed.reshape(token_count, D).astype(jnp.bfloat16)
    after_attn = inputs + jnp.dot(mixed, weights[3], preferred_element_type=jnp.float32)
    normed_two = ln_affine(after_attn, gain_two, bias_two).astype(jnp.bfloat16)
    pre_act = jnp.dot(normed_two, weights[6], preferred_element_type=jnp.float32) + weights[
        7
    ].astype(jnp.float32)
    activated = jax.nn.gelu(pre_act, approximate=False).astype(jnp.bfloat16)
    after_mlp = (
        after_attn
        + jnp.dot(activated, weights[8], preferred_element_type=jnp.float32)
        + weights[9].astype(jnp.float32)
    )
    return (
        inputs,
        normed,
        queries,
        key_heads,
        value_heads,
        attn_probs,
        probs_low,
        mixed,
        after_attn,
        normed_two,
        pre_act,
        activated,
        after_mlp,
    )


def body(
    tokens,
    chip_lengths,
    chip_ids,
    positions,
    ln1_gain,
    ln1_bias,
    qkv_weight,
    out_weight,
    ln2_gain,
    ln2_bias,
    fc1_weight,
    fc1_bias,
    fc2_weight,
    fc2_bias,
    dec_weight,
    dec_bias,
    mask_token,
    grid_cotangent,
):
    gathered = (
        lax.all_gather(ln1_gain, ("dp", "fsdp"), axis=0, tiled=True),
        lax.all_gather(ln1_bias, ("dp", "fsdp"), axis=0, tiled=True),
        lax.all_gather(qkv_weight, ("dp", "fsdp"), axis=0, tiled=True),
        lax.all_gather(out_weight, ("dp", "fsdp"), axis=0, tiled=True),
        lax.all_gather(ln2_gain, ("dp", "fsdp"), axis=0, tiled=True),
        lax.all_gather(ln2_bias, ("dp", "fsdp"), axis=0, tiled=True),
        lax.all_gather(fc1_weight, ("dp", "fsdp"), axis=0, tiled=True),
        lax.all_gather(fc1_bias, ("dp", "fsdp"), axis=0, tiled=True),
        lax.all_gather(fc2_weight, ("dp", "fsdp"), axis=0, tiled=True),
        lax.all_gather(fc2_bias, ("dp", "fsdp"), axis=0, tiled=True),
        lax.all_gather(dec_weight, ("dp", "fsdp"), axis=0, tiled=True),
        lax.all_gather(dec_bias, ("dp", "fsdp"), axis=0, tiled=True),
        lax.all_gather(mask_token, ("dp", "fsdp"), axis=0, tiled=True),
    )
    segment, fill_table, empty_cells = pack_layout(chip_lengths, positions)
    forward_saved = layer_forward(gathered, tokens, segment)
    dec_input = forward_saved[12].astype(jnp.bfloat16)
    projected = (
        jnp.dot(dec_input, gathered[10], preferred_element_type=jnp.float32)
        + gathered[11].astype(jnp.float32)
    ).astype(jnp.bfloat16)
    cell_values = jnp.dot(fill_table, projected, preferred_element_type=jnp.float32)
    cell_values = (
        cell_values
        + empty_cells.astype(jnp.float32)[:, None] * gathered[12].astype(jnp.float32)[None, :]
    )
    slot_count = chip_lengths.shape[0]
    cell_values = cell_values.astype(jnp.bfloat16).reshape(slot_count, GRID, DEC)
    fsdp_size = lax.axis_size("fsdp")
    chip_tags = jnp.broadcast_to(chip_ids.astype(jnp.bfloat16)[:, None], (slot_count, fsdp_size))
    arrived, arrived_tags = (
        lax.all_to_all(cell_values, "fsdp", split_axis=1, concat_axis=0, tiled=True),
        lax.all_to_all(chip_tags, "fsdp", split_axis=1, concat_axis=0, tiled=True),
    )
    group_size = arrived.shape[0]
    owner_rows = arrived_tags[:, 0].astype(jnp.int32)
    placement = (jnp.arange(group_size, dtype=jnp.int32)[:, None] == owner_rows[None, :]).astype(
        jnp.bfloat16
    )
    full_grid = jnp.dot(
        placement, arrived.reshape(group_size, -1), preferred_element_type=jnp.float32
    )
    full_grid = full_grid.astype(jnp.bfloat16).reshape(arrived.shape)
    returned = left_product(placement, grid_cotangent.reshape(group_size, -1))
    returned = returned.astype(jnp.bfloat16).reshape(grid_cotangent.shape)
    grid_grad = lax.all_to_all(returned, "fsdp", split_axis=0, concat_axis=1, tiled=True)
    weights = (
        lax.all_gather(ln1_gain, ("dp", "fsdp"), axis=0, tiled=True),
        lax.all_gather(ln1_bias, ("dp", "fsdp"), axis=0, tiled=True),
        lax.all_gather(qkv_weight, ("dp", "fsdp"), axis=0, tiled=True),
        lax.all_gather(out_weight, ("dp", "fsdp"), axis=0, tiled=True),
        lax.all_gather(ln2_gain, ("dp", "fsdp"), axis=0, tiled=True),
        lax.all_gather(ln2_bias, ("dp", "fsdp"), axis=0, tiled=True),
        lax.all_gather(fc1_weight, ("dp", "fsdp"), axis=0, tiled=True),
        lax.all_gather(fc1_bias, ("dp", "fsdp"), axis=0, tiled=True),
        lax.all_gather(fc2_weight, ("dp", "fsdp"), axis=0, tiled=True),
        lax.all_gather(fc2_bias, ("dp", "fsdp"), axis=0, tiled=True),
        lax.all_gather(dec_weight, ("dp", "fsdp"), axis=0, tiled=True),
        lax.all_gather(dec_bias, ("dp", "fsdp"), axis=0, tiled=True),
        lax.all_gather(mask_token, ("dp", "fsdp"), axis=0, tiled=True),
    )
    (
        inputs,
        normed,
        queries,
        key_heads,
        value_heads,
        attn_probs,
        probs_low,
        mixed,
        after_attn,
        normed_two,
        pre_act,
        activated,
        after_mlp,
    ) = layer_forward(weights, tokens, segment)
    token_count = tokens.shape[0]
    gain_one = weights[0].astype(jnp.float32)
    bias_one = weights[1].astype(jnp.float32)
    gain_two = weights[4].astype(jnp.float32)
    bias_two = weights[5].astype(jnp.float32)
    flat_grad = grid_grad.reshape(slot_count * GRID, DEC)
    proj_grad = left_product(fill_table, flat_grad).astype(jnp.bfloat16)
    mask_grad = jnp.dot(empty_cells, flat_grad, preferred_element_type=jnp.float32)
    dec_w_grad = left_product(after_mlp.astype(jnp.bfloat16), proj_grad)
    dec_b_grad = jnp.sum(proj_grad.astype(jnp.float32), axis=0)
    mlp_grad = right_product(proj_grad, weights[10])
    fc2_input = mlp_grad.astype(jnp.bfloat16)
    fc2_w_grad = left_product(activated, fc2_input)
    fc2_b_grad = jnp.sum(fc2_input.astype(jnp.float32), axis=0)
    act_grad = right_product(fc2_input, weights[8])
    unused_value, gelu_pull = jax.vjp(partial(jax.nn.gelu, approximate=False), pre_act)
    pre_grad = gelu_pull(act_grad)[0].astype(jnp.bfloat16)
    fc1_w_grad = left_product(normed_two, pre_grad)
    fc1_b_grad = jnp.sum(pre_grad.astype(jnp.float32), axis=0)
    norm_two_grad = right_product(pre_grad, weights[6])
    unused_two, norm_two_pull = jax.vjp(ln_affine, after_attn, gain_two, bias_two)
    attn_res_grad, ln2_g_grad, ln2_b_grad = norm_two_pull(norm_two_grad)
    resid_grad = mlp_grad + attn_res_grad
    out_input = resid_grad.astype(jnp.bfloat16)
    out_w_grad = left_product(mixed, out_input)
    mixed_grad = (
        right_product(out_input, weights[3])
        .astype(jnp.bfloat16)
        .reshape(token_count, HEADS, HEAD_DIM)
    )
    prob_grad = jnp.einsum(
        "qhd,khd->hqk", mixed_grad, value_heads, preferred_element_type=jnp.float32
    )
    value_grad = jnp.einsum(
        "hqk,qhd->khd", probs_low, mixed_grad, preferred_element_type=jnp.float32
    )
    inner_sum = jnp.sum(prob_grad * attn_probs, axis=-1, keepdims=True)
    score_grad = (attn_probs * (prob_grad - inner_sum)).astype(jnp.bfloat16)
    scale_factor = HEAD_DIM ** (-0.5)
    query_grad = scale_factor * jnp.einsum(
        "hqk,khd->qhd", score_grad, key_heads, preferred_element_type=jnp.float32
    )
    key_grad = scale_factor * jnp.einsum(
        "hqk,qhd->khd", score_grad, queries, preferred_element_type=jnp.float32
    )
    qkv_grad = jnp.concatenate(
        [
            query_grad.reshape(token_count, D),
            key_grad.reshape(token_count, D),
            value_grad.reshape(token_count, D),
        ],
        axis=1,
    ).astype(jnp.bfloat16)
    qkv_w_grad = left_product(normed, qkv_grad)
    normed_grad = right_product(qkv_grad, weights[2])
    unused_one, norm_one_pull = jax.vjp(ln_affine, inputs, gain_one, bias_one)
    input_part, ln1_g_grad, ln1_b_grad = norm_one_pull(normed_grad)
    tokens_grad = resid_grad + input_part
    shares = (
        lax.psum_scatter(ln1_g_grad, ("dp", "fsdp"), scatter_dimension=0, tiled=True),
        lax.psum_scatter(ln1_b_grad, ("dp", "fsdp"), scatter_dimension=0, tiled=True),
        lax.psum_scatter(qkv_w_grad, ("dp", "fsdp"), scatter_dimension=0, tiled=True),
        lax.psum_scatter(out_w_grad, ("dp", "fsdp"), scatter_dimension=0, tiled=True),
        lax.psum_scatter(ln2_g_grad, ("dp", "fsdp"), scatter_dimension=0, tiled=True),
        lax.psum_scatter(ln2_b_grad, ("dp", "fsdp"), scatter_dimension=0, tiled=True),
        lax.psum_scatter(fc1_w_grad, ("dp", "fsdp"), scatter_dimension=0, tiled=True),
        lax.psum_scatter(fc1_b_grad, ("dp", "fsdp"), scatter_dimension=0, tiled=True),
        lax.psum_scatter(fc2_w_grad, ("dp", "fsdp"), scatter_dimension=0, tiled=True),
        lax.psum_scatter(fc2_b_grad, ("dp", "fsdp"), scatter_dimension=0, tiled=True),
        lax.psum_scatter(dec_w_grad, ("dp", "fsdp"), scatter_dimension=0, tiled=True),
        lax.psum_scatter(dec_b_grad, ("dp", "fsdp"), scatter_dimension=0, tiled=True),
        lax.psum_scatter(mask_grad, ("dp", "fsdp"), scatter_dimension=0, tiled=True),
    )
    return (
        full_grid,
        tokens_grad,
        shares[0],
        shares[1],
        shares[2],
        shares[3],
        shares[4],
        shares[5],
        shares[6],
        shares[7],
        shares[8],
        shares[9],
        shares[10],
        shares[11],
        shares[12],
    )


def solution(mesh):
    placed = (
        P(("dp", "fsdp"), None),
        P(("dp", "fsdp")),
        P(("dp", "fsdp")),
        P(("dp", "fsdp")),
        P(("dp", "fsdp")),
        P(("dp", "fsdp")),
        P(("dp", "fsdp"), None),
        P(("dp", "fsdp"), None),
        P(("dp", "fsdp")),
        P(("dp", "fsdp")),
        P(("dp", "fsdp"), None),
        P(("dp", "fsdp")),
        P(("dp", "fsdp"), None),
        P(("dp", "fsdp")),
        P(("dp", "fsdp"), None),
        P(("dp", "fsdp")),
        P(("dp", "fsdp")),
        P("dp", "fsdp", None),
    )
    return jax.shard_map(
        body,
        mesh=mesh,
        in_specs=placed,
        out_specs=(
            P("dp", "fsdp", None),
            P(("dp", "fsdp"), None),
            P(("dp", "fsdp")),
            P(("dp", "fsdp")),
            P(("dp", "fsdp"), None),
            P(("dp", "fsdp"), None),
            P(("dp", "fsdp")),
            P(("dp", "fsdp")),
            P(("dp", "fsdp"), None),
            P(("dp", "fsdp")),
            P(("dp", "fsdp"), None),
            P(("dp", "fsdp")),
            P(("dp", "fsdp"), None),
            P(("dp", "fsdp")),
            P(("dp", "fsdp")),
        ),
        check_vma=False,
    )
```

profile of v0, /device:TPU:1, one launch (start us, length us, event | category | flops | bytes accessed | tf_op | source)
XLA Modules:
  0.0 1364.9 jit_solution(11628175462667294958)
XLA Ops:
  10.7 6.9 all-to-all-start
  27.6 5.0 all-to-all-start.2
  35.1 57.5 %all-gather.3 = bf16[128,6,512]{2,1,0:T(8,128)(2,1)S(1)} all-gather(bf16[1,6,512]{2,1,0:T(8,128)(2,1)S(1)} %bitcast.125), channel_id=1, replica_groups=mesh['dp'=8,'fsdp'=16] {'dp','fsdp'}, dimensions={0}, use_global_device_ids=true | all-gather | bytes 792576 | tf_op jit(solution)/shard_map/all_gather | solution.py:140
  94.6 64.2 %all-reduce.25 = (bf16[512]{0:T(512)(128)(2,1)}, bf16[768]{0:T(1024)(128)(2,1)S(1)}, bf16[768]{0:T(1024)(128)(2,1)S(1)}, bf16[768]{0:T(1024)(128)(2,1)S(1)}, bf1...) all-reduce(bf16[512]{0:T(512)(128)(2,1)S(1)} %dynamic-update-slice., ...), channel_id=1, replica_groups=mesh['dp'=8,'fsdp'=16] {'dp','fsdp'}, use_global_device_ids=true, to_apply=%add.7 | all-reduce | flops 7936 | bytes 31744
  167.9 6.6 reshape.295
  174.5 4.2 convolution_convert_fusion.2
  186.5 10.2 fusion.83
  196.7 6.1 fusion.35
  205.2 17.9 %all-gather.15.cloned.1.call-done = bf16[128,6,3072]{2,1,0:T(8,128)(2,1)} async-done(((bf16[1,6,3072]{2,1,0:T(8,128)(2,1)}), bf16[128,6,3072]{2,1,0:T(8,128)(2,1)}) %all-gather.15.cloned.1.call-update) | async-done | bytes 4718608 | tf_op jit(solution)/shard_map/all_gather | solution.py:136
  223.1 7.8 reshape.299
  230.9 20.3 %multiply_convert_fusion.1 = (bf16[512,3072]{1,0:T(8,128)(2,1)}, f32[512,3072]{1,0:T(8,128)}, f32[512,3072]{1,0:T(8,128)}) fusion(f32[3072]{0:T(1024)S(1)} %convert_element_type.162, bf16[768,3072]{1,0:T(8,128)(2,1)} %reshape.299, f32[512,768]{1,0:T(8,128)S(1)} %copy-done.7, f32[768]{0:T(1024)S(1)} %convert_element_type.160, ...), kind=kOutput, calls=%fused_computation.12 | convolution fusion | flops 2521694208 | bytes 22042624 | tf_op jit(solution)/shard_map/dot_general | solution.py:83
  251.1 39.7 %all-gather.9.cloned.1.call-done = bf16[3072,768]{1,0:T(8,128)(2,1)} async-done(((bf16[24,768]{1,0:T(8,128)(2,1)}), bf16[3072,768]{1,0:T(8,128)(2,1)}) %all-gather.9.cloned.1.call-update) | async-done | bytes 4718608 | tf_op jit(solution)/shard_map/all_gather | solution.py:138
  290.9 9.4 convert_reduce_fusion
  309.7 8.2 fusion.64
  319.3 10.4 multiply_reduce_fusion
  331.4 7.7 multiply_convert_fusion
  339.1 5.1 add_convert_fusion.2
  353.4 6.0 fusion.45
  359.4 5.6 fusion.75
  365.0 366.0 %fusion.78 = (f32[8,2304]{1,0:T(8,128)S(1)}, f32[8,768]{1,0:T(8,128)S(1)}, f32[8,3072]{1,0:T(8,128)S(1)}, f32[8,512]{1,0:T(8,128)S(1)}) fusion(f32[768,2304]{1,0:T(8,128)} %fusion.45, f32[768,768]{1,0:T(8,128)} %fusion.48, f32[768,3072]{1,0:T(8,128)} %fusion.75, f32[768,512]{1,0:T(8,128)} %fusion.86), kind=kCustom, calls=%all-reduce-scatter.4 | all-reduce-scatter fusion | flops 6815745 | bytes 20660224
  742.8 13.2 collective-permute-start.118
  756.1 7.0 collective-permute-start.117
  782.0 5.1 collective-permute-start.108
  789.4 4.1 collective-permute-start.106
  862.8 4.2 collective-permute-start.42
  903.6 4.4 collective-permute-start.25
  911.9 4.3 collective-permute-start.22
  920.8 4.2 collective-permute-start.19
  944.0 4.2 collective-permute-start.11
  957.0 6.7 fusion.77
  967.1 4.1 collective-permute-start.5
  978.0 4.3 add_convert_fusion.1
  982.4 5.1 copy.79
  987.4 5.8 all-to-all-start.1
  993.3 5.8 collective-permute-start.2
  1006.0 12.5 collective-permute-done.2
  1018.5 4.6 collective-permute-start.93
  1036.9 7.7 collective-permute-start.85
  1063.8 62.6 %all-reduce.24 = (f32[768]{0:T(1024)S(1)}, f32[768]{0:T(1024)S(1)}, f32[768]{0:T(1024)S(1)}, f32[768]{0:T(1024)S(1)}, f32[3072]{0:T(1024)S(1)}, /*index=5*/f32[768]{0:T(1024)S(1)}, f32[512]{0:T(512)S(1)}, f32[512]{0:T(512)S(1)}) all-reduce(f32[768]{0:T(1024)} %get-tuple-element.17, ...), channel_id=2, replica_groups=mesh['dp'=8,'fsdp'=16] {'dp','fsdp'}, use_global_device_ids=true, to_apply=%region_15.16.clone | all-reduce | flops 7936 | bytes 63488
  1131.1 25.9 %concatenate.8 = f32[262,512]{1,0:T(8,128)S(1)} concatenate(f32[6,512]{1,0:T(8,128)} %copy-done.91, f32[8,512]{1,0:T(8,128)} %copy-done.89, f32[8,512]{1,0:T(8,128)} %copy-done.90, f32[8,512]{1,0:T(8,128)} %copy-done.92, f32[8,512]{1,0:T(8,128)} %copy-done.93, f32[8,512]{1,0:T(8,128)} %copy-done.94, f32[8,512]{1,0:T(8,128)} %copy-done.95, f32[8,512]{1,0:T(8,128)} %copy-done.96, ...), dimensions={0} | concatenate | bytes 1073152
  1164.4 4.4 collective-permute-start.76
  1172.7 6.5 collective-permute-start.74
  1179.8 27.2 %concatenate.6 = f32[262,768]{1,0:T(8,128)S(1)} concatenate(f32[6,768]{1,0:T(8,128)} %copy-done.55, f32[8,768]{1,0:T(8,128)} %copy-done.56, f32[8,768]{1,0:T(8,128)} %copy-done.57, f32[8,768]{1,0:T(8,128)} %copy-done.58, f32[8,768]{1,0:T(8,128)} %copy-done.59, f32[8,768]{1,0:T(8,128)} %copy-done.60, f32[8,768]{1,0:T(8,128)} %copy-done.61, f32[8,768]{1,0:T(8,128)} %copy-done.62, ...), dimensions={0} | concatenate | bytes 1609728
  1214.9 4.8 collective-permute-start.70
  1219.7 4.9 collective-permute-start.69
  1225.2 54.0 %concatenate.5 = f32[262,2304]{1,0:T(8,128)} concatenate(f32[6,2304]{1,0:T(8,128)} %copy-done.32, f32[8,2304]{1,0:T(8,128)} %copy-done.29, f32[8,2304]{1,0:T(8,128)} %copy-done.30, f32[8,2304]{1,0:T(8,128)} %copy-done.31, f32[8,2304]{1,0:T(8,128)} %copy-done.33, f32[8,2304]{1,0:T(8,128)} %copy-done.34, f32[8,2304]{1,0:T(8,128)} %copy-done.35, f32[8,2304]{1,0:T(8,128)} %copy-done.36, ...), dimensions={0} | concatenate | bytes 4829184
  1285.7 4.3 collective-permute-start.66
  1296.9 53.5 %concatenate.7 = f32[262,3072]{1,0:T(8,128)} concatenate(f32[6,3072]{1,0:T(8,128)S(1)} %collective-permute-done.95, f32[8,3072]{1,0:T(8,128)S(1)} %collective-permute-done.94, f32[8,3072]{1,0:T(8,128)S(1)} %collective-permute-done.93, f32[8,3072]{1,0:T(8,128)S(1)} %collective-permute-done.92, f32[8,3072]{1,0:T(8,128)S(1)} %collective-permute-done.91, ...), dimensions={0} | concatenate | bytes 6438912
  (641 shorter events, 326.8 us)
Async XLA Ops:
  7.2 157.5 %all-gather.13.cloned.1.call-start = ((), (), s32[]{:S(2)}) async-start(), calls=%async_computation.7 | async-start | bytes 1585152 | tf_op jit(solution)/shard_map/all_gather | solution.py:133
  7.9 160.0 %all-gather.11.cloned.1.call-start = ((), (), s32[]{:S(2)}) async-start(), calls=%async_computation.6 | async-start | bytes 4755456 | tf_op jit(solution)/shard_map/all_gather | solution.py:132
  8.7 214.5 %all-gather.15.cloned.1.call-start = ((), (), s32[]{:S(2)}) async-start(), calls=%async_computation.8 | async-start | bytes 6340608 | tf_op jit(solution)/shard_map/all_gather | solution.py:136
  27.6 131.8 %all-to-all-start.2 = ((bf16[32,64,512]{2,1,0:T(8,128)(2,1)}), bf16[32,64,512]{2,1,0:T(8,128)(2,1)}, u32[]{:S(2)}, u32[]{:S(2)}) async-start(bf16[32,64,512]{2,1,0:T(8,128)(2,1)} %bitcast.97), calls=%async_computation.2 | async-start | bytes 4194304 | tf_op jit(solution)/shard_map/all_to_all | solution.py:175
  32.6 258.2 %all-gather.9.cloned.1.call-start = ((), (), s32[]{:S(2)}) async-start(), calls=%async_computation.4 | async-start | bytes 4755456 | tf_op jit(solution)/shard_map/all_gather | solution.py:138
  33.2 1324.9 %reduce-scatter.10.cloned.1.call-start = ((), (), s32[]{:S(2)}) async-start(), calls=%async_computation.5 | async-start | bytes 9510912 | tf_op jit(solution)/shard_map/reduce_scatter | solution.py:273
  737.6 18.5 %collective-permute-start.122 = (f32[8,512]{1,0:T(8,128)S(1)}, f32[8,512]{1,0:T(8,128)S(1)}, u32[]{:S(2)}, u32[]{:S(2)}) collective-permute-start(f32[8,512]{1,0:T(8,128)S(1)} %get-tuple-element.45), channel_id=1, source_target_pairs={{0,27},{1,28},{2,29},{3,30},{4,31},{5,32},{6,33},{7,34},{8,35},{9,... | collective-permute-start | bytes 49160
  738.9 24.2 %collective-permute-start.121 = (f32[8,512]{1,0:T(8,128)S(1)}, f32[8,512]{1,0:T(8,128)S(1)}, u32[]{:S(2)}, u32[]{:S(2)}) collective-permute-start(f32[8,512]{1,0:T(8,128)S(1)} %get-tuple-element.45), channel_id=1, source_target_pairs={{0,26},{1,27},{2,28},{3,29},{4,30},{5,31},{6,32},{7,33},{8,34},{9,... | collective-permute-start | bytes 49160
  740.2 25.7 %collective-permute-start.120 = (f32[8,512]{1,0:T(8,128)S(1)}, f32[8,512]{1,0:T(8,128)S(1)}, u32[]{:S(2)}, u32[]{:S(2)}) collective-permute-start(f32[8,512]{1,0:T(8,128)S(1)} %get-tuple-element.45), channel_id=1, source_target_pairs={{0,25},{1,26},{2,27},{3,28},{4,29},{5,30},{6,31},{7,32},{8,33},{9,... | collective-permute-start | bytes 49160
  741.5 25.7 %collective-permute-start.119 = (f32[8,512]{1,0:T(8,128)S(1)}, f32[8,512]{1,0:T(8,128)S(1)}, u32[]{:S(2)}, u32[]{:S(2)}) collective-permute-start(f32[8,512]{1,0:T(8,128)S(1)} %get-tuple-element.45), channel_id=1, source_target_pairs={{0,24},{1,25},{2,26},{3,27},{4,28},{5,29},{6,30},{7,31},{8,32},{9,... | collective-permute-start | bytes 49160
  742.8 27.7 %collective-permute-start.118 = (f32[8,512]{1,0:T(8,128)S(1)}, f32[8,512]{1,0:T(8,128)S(1)}, u32[]{:S(2)}, u32[]{:S(2)}) collective-permute-start(f32[8,512]{1,0:T(8,128)S(1)} %get-tuple-element.45), channel_id=1, source_target_pairs={{0,23},{1,24},{2,25},{3,26},{4,27},{5,28},{6,29},{7,30},{8,31},{9,... | collective-permute-start | bytes 49160
  808.8 19.3 %collective-permute-start.63 = (f32[6,768]{1,0:T(8,128)S(1)}, f32[6,768]{1,0:T(8,128)S(1)}, u32[]{:S(2)}, u32[]{:S(2)}) collective-permute-start(f32[6,768]{1,0:T(8,128)S(1)} %slice.19), channel_id=1, source_target_pairs={{0,32},{1,33},{2,34},{3,35},{4,36},{5,37},{6,38},{7,39},{8,40},{9,... | collective-permute-start | bytes 55304
  934.7 17.3 %collective-permute-start.14 = (f32[8,2304]{1,0:T(8,128)S(1)}, f32[8,2304]{1,0:T(8,128)S(1)}, u32[]{:S(2)}, u32[]{:S(2)}) collective-permute-start(f32[8,2304]{1,0:T(8,128)S(1)} %get-tuple-element.42), channel_id=1, source_target_pairs={{0,15},{1,16},{2,17},{3,18},{4,19},{5,20},{6,21},{7,22},{8,23},{9,... | collective-permute-start | bytes 221192
  936.1 17.1 %collective-permute-start.13 = (f32[8,2304]{1,0:T(8,128)S(1)}, f32[8,2304]{1,0:T(8,128)S(1)}, u32[]{:S(2)}, u32[]{:S(2)}) collective-permute-start(f32[8,2304]{1,0:T(8,128)S(1)} %get-tuple-element.42), channel_id=1, source_target_pairs={{0,14},{1,15},{2,16},{3,17},{4,18},{5,19},{6,20},{7,21},{8,22},{9,... | collective-permute-start | bytes 221192
  940.7 22.9 %collective-permute-start.12 = (f32[8,2304]{1,0:T(8,128)S(1)}, f32[8,2304]{1,0:T(8,128)S(1)}, u32[]{:S(2)}, u32[]{:S(2)}) collective-permute-start(f32[8,2304]{1,0:T(8,128)S(1)} %get-tuple-element.42), channel_id=1, source_target_pairs={{0,13},{1,14},{2,15},{3,16},{4,17},{5,18},{6,19},{7,20},{8,21},{9,... | collective-permute-start | bytes 221192
  944.0 21.6 %collective-permute-start.11 = (f32[8,2304]{1,0:T(8,128)S(1)}, f32[8,2304]{1,0:T(8,128)S(1)}, u32[]{:S(2)}, u32[]{:S(2)}) collective-permute-start(f32[8,2304]{1,0:T(8,128)S(1)} %get-tuple-element.42), channel_id=1, source_target_pairs={{0,12},{1,13},{2,14},{3,15},{4,16},{5,17},{6,18},{7,19},{8,20},{9,... | collective-permute-start | bytes 221192
  948.2 18.9 %collective-permute-start.10 = (f32[8,2304]{1,0:T(8,128)S(1)}, f32[8,2304]{1,0:T(8,128)S(1)}, u32[]{:S(2)}, u32[]{:S(2)}) collective-permute-start(f32[8,2304]{1,0:T(8,128)S(1)} %get-tuple-element.42), channel_id=1, source_target_pairs={{0,11},{1,12},{2,13},{3,14},{4,15},{5,16},{6,17},{7,18},{8,19},{9,... | collective-permute-start | bytes 221192
  951.9 19.3 %collective-permute-start.9 = (f32[8,2304]{1,0:T(8,128)S(1)}, f32[8,2304]{1,0:T(8,128)S(1)}, u32[]{:S(2)}, u32[]{:S(2)}) collective-permute-start(f32[8,2304]{1,0:T(8,128)S(1)} %get-tuple-element.42), channel_id=1, source_target_pairs={{0,10},{1,11},{2,12},{3,13},{4,14},{5,15},{6,16},{7,17},{8,18},{9,... | collective-permute-start | bytes 221192
  953.9 20.5 %collective-permute-start.8 = (f32[8,2304]{1,0:T(8,128)S(1)}, f32[8,2304]{1,0:T(8,128)S(1)}, u32[]{:S(2)}, u32[]{:S(2)}) collective-permute-start(f32[8,2304]{1,0:T(8,128)S(1)} %get-tuple-element.42), channel_id=1, source_target_pairs={{0,9},{1,10},{2,11},{3,12},{4,13},{5,14},{6,15},{7,16},{8,17},{9,1... | collective-permute-start | bytes 221192
  963.6 29.7 %collective-permute-start.7 = (f32[8,2304]{1,0:T(8,128)S(1)}, f32[8,2304]{1,0:T(8,128)S(1)}, u32[]{:S(2)}, u32[]{:S(2)}) collective-permute-start(f32[8,2304]{1,0:T(8,128)S(1)} %get-tuple-element.42), channel_id=1, source_target_pairs={{0,8},{1,9},{2,10},{3,11},{4,12},{5,13},{6,14},{7,15},{8,16},{9,17... | collective-permute-start | bytes 221192
  965.6 33.6 %collective-permute-start.6 = (f32[8,2304]{1,0:T(8,128)S(1)}, f32[8,2304]{1,0:T(8,128)S(1)}, u32[]{:S(2)}, u32[]{:S(2)}) collective-permute-start(f32[8,2304]{1,0:T(8,128)S(1)} %get-tuple-element.42), channel_id=1, source_target_pairs={{0,7},{1,8},{2,9},{3,10},{4,11},{5,12},{6,13},{7,14},{8,15},{9,16}... | collective-permute-start | bytes 221192
  967.1 34.3 %collective-permute-start.5 = (f32[8,2304]{1,0:T(8,128)S(1)}, f32[8,2304]{1,0:T(8,128)}, u32[]{:S(2)}, u32[]{:S(2)}) collective-permute-start(f32[8,2304]{1,0:T(8,128)S(1)} %get-tuple-element.42), channel_id=1, source_target_pairs={{0,6},{1,7},{2,8},{3,9},{4,10},{5,11},{6,12},{7,13},{8,14},{9,15},... | collective-permute-start | bytes 221192
  971.3 32.1 %collective-permute-start.4 = (f32[8,2304]{1,0:T(8,128)S(1)}, f32[8,2304]{1,0:T(8,128)}, u32[]{:S(2)}, u32[]{:S(2)}) collective-permute-start(f32[8,2304]{1,0:T(8,128)S(1)} %get-tuple-element.42), channel_id=1, source_target_pairs={{0,5},{1,6},{2,7},{3,8},{4,9},{5,10},{6,11},{7,12},{8,13},{9,14},{... | collective-permute-start | bytes 221192
  974.4 30.3 %collective-permute-start.3 = (f32[8,2304]{1,0:T(8,128)S(1)}, f32[8,2304]{1,0:T(8,128)}, u32[]{:S(2)}, u32[]{:S(2)}) collective-permute-start(f32[8,2304]{1,0:T(8,128)S(1)} %get-tuple-element.42), channel_id=1, source_target_pairs={{0,4},{1,5},{2,6},{3,7},{4,8},{5,9},{6,10},{7,11},{8,12},{9,13},{1... | collective-permute-start | bytes 221192
  987.4 364.6 %all-to-all-start.1 = ((bf16[2,1024,512]{2,0,1:T(2,128)(2,1)}), bf16[2,1024,512]{2,0,1:T(2,128)(2,1)}, u32[]{:S(2)}, u32[]{:S(2)}) async-start(bf16[2,1024,512]{2,0,1:T(2,128)(2,1)} %copy.79), calls=%async_computation.1 | async-start | bytes 4194304 | tf_op jit(solution)/shard_map/all_to_all | solution.py:161
  993.3 25.2 %collective-permute-start.2 = (f32[8,2304]{1,0:T(8,128)S(1)}, f32[8,2304]{1,0:T(8,128)}, u32[]{:S(2)}, u32[]{:S(2)}) collective-permute-start(f32[8,2304]{1,0:T(8,128)S(1)} %get-tuple-element.42), channel_id=1, source_target_pairs={{0,3},{1,4},{2,5},{3,6},{4,7},{5,8},{6,9},{7,10},{8,11},{9,12},{10... | collective-permute-start | bytes 221192
  999.1 24.0 %collective-permute-start.1 = (f32[8,2304]{1,0:T(8,128)S(1)}, f32[8,2304]{1,0:T(8,128)}, u32[]{:S(2)}, u32[]{:S(2)}) collective-permute-start(f32[8,2304]{1,0:T(8,128)S(1)} %get-tuple-element.42), channel_id=1, source_target_pairs={{0,2},{1,3},{2,4},{3,5},{4,6},{5,7},{6,8},{7,9},{8,10},{9,11},{10,... | collective-permute-start | bytes 221192
  1001.4 23.5 %collective-permute-start = (f32[8,2304]{1,0:T(8,128)S(1)}, f32[8,2304]{1,0:T(8,128)}, u32[]{:S(2)}, u32[]{:S(2)}) collective-permute-start(f32[8,2304]{1,0:T(8,128)S(1)} %get-tuple-element.42), channel_id=1, source_target_pairs={{0,1},{1,2},{2,3},{3,4},{4,5},{5,6},{6,7},{7,8},{8,9},{9,10},{10,1... | collective-permute-start | bytes 221192
  1003.3 24.9 %collective-permute-start.94 = (f32[8,3072]{1,0:T(8,128)S(1)}, f32[8,3072]{1,0:T(8,128)S(1)}, u32[]{:S(2)}, u32[]{:S(2)}) collective-permute-start(f32[8,3072]{1,0:T(8,128)S(1)} %get-tuple-element.44), channel_id=1, source_target_pairs={{0,31},{1,32},{2,33},{3,34},{4,35},{5,36},{6,37},{7,38},{8,39},{9,... | collective-permute-start | bytes 294920
  1004.7 21.6 %collective-permute-start.95 = (f32[6,3072]{1,0:T(8,128)S(1)}, f32[6,3072]{1,0:T(8,128)S(1)}, u32[]{:S(2)}, u32[]{:S(2)}) collective-permute-start(f32[6,3072]{1,0:T(8,128)S(1)} %slice.20), channel_id=1, source_target_pairs={{0,32},{1,33},{2,34},{3,35},{4,36},{5,37},{6,38},{7,39},{8,40},{9,... | collective-permute-start | bytes 221192
  1035.0 17.2 %collective-permute-start.86 = (f32[8,3072]{1,0:T(8,128)S(1)}, f32[8,3072]{1,0:T(8,128)S(1)}, u32[]{:S(2)}, u32[]{:S(2)}) collective-permute-start(f32[8,3072]{1,0:T(8,128)S(1)} %get-tuple-element.44), channel_id=1, source_target_pairs={{0,23},{1,24},{2,25},{3,26},{4,27},{5,28},{6,29},{7,30},{8,31},{9,... | collective-permute-start | bytes 294920
  1036.9 17.4 %collective-permute-start.85 = (f32[8,3072]{1,0:T(8,128)S(1)}, f32[8,3072]{1,0:T(8,128)S(1)}, u32[]{:S(2)}, u32[]{:S(2)}) collective-permute-start(f32[8,3072]{1,0:T(8,128)S(1)} %get-tuple-element.44), channel_id=1, source_target_pairs={{0,22},{1,23},{2,24},{3,25},{4,26},{5,27},{6,28},{7,29},{8,30},{9,... | collective-permute-start | bytes 294920
  1046.2 110.8 %collective-permute-start.83 = (f32[8,3072]{1,0:T(8,128)S(1)}, f32[8,3072]{1,0:T(8,128)}, u32[]{:S(2)}, u32[]{:S(2)}) collective-permute-start(f32[8,3072]{1,0:T(8,128)S(1)} %get-tuple-element.44), channel_id=1, source_target_pairs={{0,20},{1,21},{2,22},{3,23},{4,24},{5,25},{6,26},{7,27},{8,28},{9,... | collective-permute-start | bytes 294920
  1048.1 112.7 %collective-permute-start.82 = (f32[8,3072]{1,0:T(8,128)S(1)}, f32[8,3072]{1,0:T(8,128)}, u32[]{:S(2)}, u32[]{:S(2)}) collective-permute-start(f32[8,3072]{1,0:T(8,128)S(1)} %get-tuple-element.44), channel_id=1, source_target_pairs={{0,19},{1,20},{2,21},{3,22},{4,23},{5,24},{6,25},{7,26},{8,27},{9,... | collective-permute-start | bytes 294920
  1052.2 112.2 %collective-permute-start.81 = (f32[8,3072]{1,0:T(8,128)S(1)}, f32[8,3072]{1,0:T(8,128)}, u32[]{:S(2)}, u32[]{:S(2)}) collective-permute-start(f32[8,3072]{1,0:T(8,128)S(1)} %get-tuple-element.44), channel_id=1, source_target_pairs={{0,18},{1,19},{2,20},{3,21},{4,22},{5,23},{6,24},{7,25},{8,26},{9,... | collective-permute-start | bytes 294920
  1054.3 114.5 %collective-permute-start.80 = (f32[8,3072]{1,0:T(8,128)S(1)}, f32[8,3072]{1,0:T(8,128)}, u32[]{:S(2)}, u32[]{:S(2)}) collective-permute-start(f32[8,3072]{1,0:T(8,128)S(1)} %get-tuple-element.44), channel_id=1, source_target_pairs={{0,17},{1,18},{2,19},{3,20},{4,21},{5,22},{6,23},{7,24},{8,25},{9,... | collective-permute-start | bytes 294920
  1057.7 115.0 %collective-permute-start.79 = (f32[8,3072]{1,0:T(8,128)S(1)}, f32[8,3072]{1,0:T(8,128)}, u32[]{:S(2)}, u32[]{:S(2)}) collective-permute-start(f32[8,3072]{1,0:T(8,128)S(1)} %get-tuple-element.44), channel_id=1, source_target_pairs={{0,16},{1,17},{2,18},{3,19},{4,20},{5,21},{6,22},{7,23},{8,24},{9,... | collective-permute-start | bytes 294920
  1157.0 50.1 %collective-permute-start.78 = (f32[8,3072]{1,0:T(8,128)S(1)}, f32[8,3072]{1,0:T(8,128)S(1)}, u32[]{:S(2)}, u32[]{:S(2)}) collective-permute-start(f32[8,3072]{1,0:T(8,128)S(1)} %get-tuple-element.44), channel_id=1, source_target_pairs={{0,15},{1,16},{2,17},{3,18},{4,19},{5,20},{6,21},{7,22},{8,23},{9,... | collective-permute-start | bytes 294920
  1160.9 47.7 %collective-permute-start.77 = (f32[8,3072]{1,0:T(8,128)S(1)}, f32[8,3072]{1,0:T(8,128)S(1)}, u32[]{:S(2)}, u32[]{:S(2)}) collective-permute-start(f32[8,3072]{1,0:T(8,128)S(1)} %get-tuple-element.44), channel_id=1, source_target_pairs={{0,14},{1,15},{2,16},{3,17},{4,18},{5,19},{6,20},{7,21},{8,22},{9,... | collective-permute-start | bytes 294920
  1164.4 47.8 %collective-permute-start.76 = (f32[8,3072]{1,0:T(8,128)S(1)}, f32[8,3072]{1,0:T(8,128)S(1)}, u32[]{:S(2)}, u32[]{:S(2)}) collective-permute-start(f32[8,3072]{1,0:T(8,128)S(1)} %get-tuple-element.44), channel_id=1, source_target_pairs={{0,13},{1,14},{2,15},{3,16},{4,17},{5,18},{6,19},{7,20},{8,21},{9,... | collective-permute-start | bytes 294920
  1168.8 46.1 %collective-permute-start.75 = (f32[8,3072]{1,0:T(8,128)S(1)}, f32[8,3072]{1,0:T(8,128)S(1)}, u32[]{:S(2)}, u32[]{:S(2)}) collective-permute-start(f32[8,3072]{1,0:T(8,128)S(1)} %get-tuple-element.44), channel_id=1, source_target_pairs={{0,12},{1,13},{2,14},{3,15},{4,16},{5,17},{6,18},{7,19},{8,20},{9,... | collective-permute-start | bytes 294920
  1172.7 46.9 %collective-permute-start.74 = (f32[8,3072]{1,0:T(8,128)S(1)}, f32[8,3072]{1,0:T(8,128)S(1)}, u32[]{:S(2)}, u32[]{:S(2)}) collective-permute-start(f32[8,3072]{1,0:T(8,128)S(1)} %get-tuple-element.44), channel_id=1, source_target_pairs={{0,11},{1,12},{2,13},{3,14},{4,15},{5,16},{6,17},{7,18},{8,19},{9,... | collective-permute-start | bytes 294920
  1207.1 72.1 %collective-permute-start.73 = (f32[8,3072]{1,0:T(8,128)S(1)}, f32[8,3072]{1,0:T(8,128)S(1)}, u32[]{:S(2)}, u32[]{:S(2)}) collective-permute-start(f32[8,3072]{1,0:T(8,128)S(1)} %get-tuple-element.44), channel_id=1, source_target_pairs={{0,10},{1,11},{2,12},{3,13},{4,14},{5,15},{6,16},{7,17},{8,18},{9,... | collective-permute-start | bytes 294920
  1208.6 73.6 %collective-permute-start.72 = (f32[8,3072]{1,0:T(8,128)S(1)}, f32[8,3072]{1,0:T(8,128)S(1)}, u32[]{:S(2)}, u32[]{:S(2)}) collective-permute-start(f32[8,3072]{1,0:T(8,128)S(1)} %get-tuple-element.44), channel_id=1, source_target_pairs={{0,9},{1,10},{2,11},{3,12},{4,13},{5,14},{6,15},{7,16},{8,17},{9,1... | collective-permute-start | bytes 294920
  1212.2 73.5 %collective-permute-start.71 = (f32[8,3072]{1,0:T(8,128)S(1)}, f32[8,3072]{1,0:T(8,128)S(1)}, u32[]{:S(2)}, u32[]{:S(2)}) collective-permute-start(f32[8,3072]{1,0:T(8,128)S(1)} %get-tuple-element.44), channel_id=1, source_target_pairs={{0,8},{1,9},{2,10},{3,11},{4,12},{5,13},{6,14},{7,15},{8,16},{9,17... | collective-permute-start | bytes 294920
  1214.9 75.2 %collective-permute-start.70 = (f32[8,3072]{1,0:T(8,128)S(1)}, f32[8,3072]{1,0:T(8,128)S(1)}, u32[]{:S(2)}, u32[]{:S(2)}) collective-permute-start(f32[8,3072]{1,0:T(8,128)S(1)} %get-tuple-element.44), channel_id=1, source_target_pairs={{0,7},{1,8},{2,9},{3,10},{4,11},{5,12},{6,13},{7,14},{8,15},{9,16}... | collective-permute-start | bytes 294920
  1219.7 72.6 %collective-permute-start.69 = (f32[8,3072]{1,0:T(8,128)S(1)}, f32[8,3072]{1,0:T(8,128)S(1)}, u32[]{:S(2)}, u32[]{:S(2)}) collective-permute-start(f32[8,3072]{1,0:T(8,128)S(1)} %get-tuple-element.44), channel_id=1, source_target_pairs={{0,6},{1,7},{2,8},{3,9},{4,10},{5,11},{6,12},{7,13},{8,14},{9,15},... | collective-permute-start | bytes 294920
  1279.2 17.7 %collective-permute-start.68 = (f32[8,3072]{1,0:T(8,128)S(1)}, f32[8,3072]{1,0:T(8,128)S(1)}, u32[]{:S(2)}, u32[]{:S(2)}) collective-permute-start(f32[8,3072]{1,0:T(8,128)S(1)} %get-tuple-element.44), channel_id=1, source_target_pairs={{0,5},{1,6},{2,7},{3,8},{4,9},{5,10},{6,11},{7,12},{8,13},{9,14},{... | collective-permute-start | bytes 294920
  (233 other events, 10326.6 us)
Sparse Core Ops, SparseCore 0:
  10.8 75.7 all-gather.12
  89.7 64.4 all-gather.10
  157.4 65.6 all-gather.14
  226.1 64.7 all-gather.8
  318.1 219.6 reduce-scatter.9
where the time goes:
time: 1380 us; the launch traced here: 1360 us
  blocking collectives  550 us (40%)
  starting transfers between devices  357 us (26%)
  local copies, waits for them, and re-layouts  226 us (16%)
  matrix products  120 us (9%)
  waiting for transfers between devices  76 us (6%)
  other arithmetic  18.2 us (1%)
  between operations  17.9 us (1%)
    unnamed x3, blocking collectives  493 us
    unnamed x128, starting transfers between devices  339 us
    unnamed x336, local copies, waits for them, and re-layouts  206 us
    all_gather x1, blocking collectives, body(): lax.all_gather(dec_weight, ('dp', 'fsdp'), axis=0, tiled=True)  57.5 us
    all_gather x1, waiting for transfers between devices, body(): lax.all_gather(fc2_weight, ('dp', 'fsdp'), axis=0, tiled=True)  39.7 us
    dot_general x7, matrix products, left_product(): lax.dot_general(left, right, (((0,), (0,)), ((), ())), preferred_element_...  28 us
  transfers between devices with their start and end apart: 136, of which 5 were waited for; matrix products, arithmetic and copies ran while one was open for 51% of the time, Pallas kernels for 0%

commit v1 on v0

--- a/solution.py
+++ b/solution.py
@@ -1,10 +1,14 @@
+import functools
+import numpy as np
+import jax, jax.numpy as jnp
+from jax import lax
+from jax.experimental import pallas as pl
+from jax.experimental.pallas import tpu as pltpu
+from jax.sharding import PartitionSpec as P
+
 from functools import partial
 
-import jax
-import jax.numpy as jnp
-from jax import lax
-from jax.sharding import PartitionSpec as P
-
+ROWS = 336
 D = 768
 HEADS = 12
 HEAD_DIM = 64
@@ -40,7 +44,8 @@
 def pack_layout(chip_lengths, positions):
     row_count = positions.shape[0]
     slot_count = chip_lengths.shape[0]
-    ends = jnp.cumsum(chip_lengths + 2)
+    first = chip_lengths[0] + 2
+    ends = jnp.stack([first, first + chip_lengths[1] + 2])
     row_index = jnp.arange(row_count, dtype=jnp.int32)
     segment = jnp.sum((row_index[:, None] >= ends[None, :]).astype(jnp.int32), axis=1)
     target = jnp.where(positions >= 0, segment * GRID + positions, -1)
@@ -106,6 +111,379 @@
     )
 
 
+MESH = pl.DeviceIdType.MESH
+LW = 384
+SROWS = 80
+
+def coords():
+    dp = lax.axis_index("dp"); fs = lax.axis_index("fsdp")
+    z = dp // 2
+    x = (dp % 2) * 2 + fs // 8
+    y = (fs % 8) // 2
+    c = fs % 2
+    return z, x, y, c
+
+def dev(z, x, y, c):
+    return (z * 2 + x // 2, (x % 2) * 8 + y * 2 + c)
+
+def perm_matrix():
+    m = np.zeros((624, 640), np.float32)
+    for d in range(8):
+        for u in range(8):
+            for j in range(6):
+                m[48 * u + 6 * d + j, d * 80 + 6 * u + j] = 1
+        for j in range(6):
+            m[48 * 8 + 6 * d + j, d * 80 + 72 + j] = 1
+        for i in range(24):
+            m[432 + 24 * d + i, d * 80 + 48 + i] = 1
+    return m
+
+ALL = slice(None)
+
+def ag_chunks():
+    return [
+        [("g", "zx", (0, 2), (0, 1), (1, 2)), ("g", "xz", (2, 4), (2, 3), (3, 4))],
+        [("g", "zx", (4, 6), (4, 5), (5, 6)), ("g", "xz", (6, 8), (6, 7), (7, 8))],
+        [("g2", "zx", (0, 96), (0, 48), (48, 96)), ("g2", "xz", (96, 192), (96, 144), (144, 192))],
+        [("g", "zx", (8, 9), (8, 9), None)],
+    ]
+
+def ag_kernel(s_ref, p_ref, g_ref, g2_ref, s1, ss1, rs1, loc, ssem, rsem):
+    z, x, y, c = coords()
+    zp, zm, zo = (z + 1) % 4, (z + 3) % 4, (z + 2) % 4
+    xp, xm, xo = (x + 1) % 4, (x + 3) % 4, (x + 2) % 4
+    o = 1 - c
+    bar = pltpu.get_barrier_semaphore()
+    targets = [dev(zp, x, y, c), dev(zm, x, y, c), dev(z, xp, y, c), dev(z, xm, y, c)]
+    group = []
+    for dy in range(4):
+        for dc in range(2):
+            if dy or dc:
+                group.append((dy, dc, dev(z, x, (y + dy) % 4, (c + dc) % 2)))
+    for t in targets + [g[2] for g in group]:
+        pl.semaphore_signal(bar, inc=1, device_id=t, device_id_type=MESH)
+    pl.semaphore_wait(bar, len(targets) + len(group))
+
+    me = 2 * y + c
+    own = pltpu.make_async_copy(s_ref.at[c], s1.at[me], loc)
+    own.start()
+    firsts = []
+    for i, (dy, dc, t) in enumerate(group):
+        cp = pltpu.make_async_remote_copy(s_ref.at[(c + dc) % 2], s1.at[me], ss1.at[i], rs1.at[i], device_id=t, device_id_type=MESH)
+        cp.start()
+        src = 2 * ((y + 4 - dy) % 4) + (c + dc) % 2
+        rc = pltpu.make_async_remote_copy(s_ref.at[c], s1.at[src], ss1.at[i], rs1.at[i], device_id=t, device_id_type=MESH)
+        firsts.append((cp, rc))
+    own.wait()
+    for cp, rc in firsts:
+        rc.wait_recv()
+
+    flat = s1[...].reshape(640, LW)
+    def relay(lo, hi):
+        r = jnp.dot(p_ref[lo:hi, :], flat, preferred_element_type=jnp.float32)
+        return r.astype(jnp.bfloat16)
+
+    def place(p):
+        if p == 0: g_ref[c, 0:4, z, x] = relay(0, 192).reshape(4, 48, LW)
+        if p == 1: g_ref[c, 4:8, z, x] = relay(192, 384).reshape(4, 48, LW)
+        if p == 2: g2_ref[c, z, x] = relay(432, 624)
+        if p == 3: g_ref[c, 8, z, x] = relay(384, 432)
+
+    def view(arr, h, part, zs, xs):
+        if arr == "g":
+            return g_ref.at[h, part[0]:part[1], zs, xs]
+        return g2_ref.at[h, zs, xs, part[0]:part[1]]
+
+    sends = []
+    def mk(k, i, src, dst, to):
+        return pltpu.make_async_remote_copy(src, dst, ssem.at[k, i], rsem.at[k, i], device_id=to, device_id_type=MESH)
+    def send(k, i, v, to):
+        cp = mk(k, i, v, v, to); cp.start(); sends.append(cp)
+    def recv(k, i, v):
+        mk(k, i, v, v, dev(z, x, y, o)).wait_recv()
+
+    def steps(k, chunk):
+        arr, order, full, fa, fb = chunk
+        if order == "zx":
+            d1p, d1m, d2p, d2m = targets
+            p1, m1, o1, p2, m2, o2, s1_, s2_ = zp, zm, zo, xp, xm, xo, z, x
+            V = lambda part, a, b, h=c: view(arr, h, part, a, b)
+        else:
+            d2p, d2m, d1p, d1m = targets
+            p1, m1, o1, p2, m2, o2, s1_, s2_ = xp, xm, xo, zp, zm, zo, x, z
+            V = lambda part, a, b, h=c: view(arr, h, part, b, a)
+        sib = dev(z, x, y, o)
+        def st0():
+            send(k, 0, V(full, s1_, s2_), d1p)
+            send(k, 1, V(full, s1_, s2_), d1m)
+        def st1():
+            recv(k, 0, V(full, m1, s2_))
+            send(k, 2, V(fa, m1, s2_), d1p)
+            recv(k, 1, V(full, p1, s2_))
+            if fb is not None: send(k, 3, V(fb, p1, s2_), d1m)
+        def st2():
+            recv(k, 2, V(fa, o1, s2_))
+            if fb is not None: recv(k, 3, V(fb, o1, s2_))
+            send(k, 4, V(full, ALL, s2_), d2p)
+            send(k, 5, V(full, ALL, s2_), d2m)
+            send(k, 8, V(full, ALL, s2_), sib)
+        def st3():
+            recv(k, 4, V(full, ALL, m2))
+            send(k, 6, V(fa, ALL, m2), d2p)
+            send(k, 9, V(full, ALL, m2), sib)
+            recv(k, 5, V(full, ALL, p2))
+            if fb is not None: send(k, 7, V(fb, ALL, p2), d2m)
+            send(k, 10, V(full, ALL, p2), sib)
+        def st4():
+            recv(k, 6, V(fa, ALL, o2))
+            if fb is not None: recv(k, 7, V(fb, ALL, o2))
+            send(k, 11, V(full, ALL, o2), sib)
+        def st5():
+            recv(k, 8, V(full, ALL, s2_, o))
+            recv(k, 9, V(full, ALL, m2, o))
+            recv(k, 10, V(full, ALL, p2, o))
+            recv(k, 11, V(full, ALL, o2, o))
+        return [st0, st1, st2, st3, st4, st5]
+
+    pieces = []
+    k = 0
+    for p, cl in enumerate(ag_chunks()):
+        lst = []
+        for ch in cl:
+            lst.append(steps(k, ch)); k += 1
+        pieces.append(lst)
+    for t in range(len(pieces) + 5):
+        for p, lst in enumerate(pieces):
+            s = t - p
+            if s == 0: place(p)
+            if 0 <= s < 6:
+                for ch in lst: ch[s]()
+    for cp, rc in firsts: cp.wait_send()
+    for cp in sends: cp.wait_send()
+
+def ag_call(s, pm):
+    nk = sum(len(c) for c in ag_chunks())
+    return pl.pallas_call(
+        ag_kernel,
+        out_shape=(jax.ShapeDtypeStruct((2, 9, 4, 4, 48, LW), jnp.bfloat16), jax.ShapeDtypeStruct((2, 4, 4, 192, LW), jnp.bfloat16)),
+        in_specs=[pl.BlockSpec(memory_space=pltpu.VMEM)] * 2,
+        out_specs=[pl.BlockSpec(memory_space=pltpu.VMEM)] * 2,
+        scratch_shapes=[
+            pltpu.VMEM((8, SROWS, LW), jnp.bfloat16),
+            pltpu.SemaphoreType.DMA((7,)), pltpu.SemaphoreType.DMA((7,)), pltpu.SemaphoreType.DMA(()),
+            pltpu.SemaphoreType.DMA((nk, 12)), pltpu.SemaphoreType.DMA((nk, 12)),
+        ],
+        compiler_params=pltpu.CompilerParams(collective_id=0, has_side_effects=True, vmem_limit_bytes=58 * 2**20),
+        cost_estimate=pl.CostEstimate(flops=10**9, bytes_accessed=3 * 10**7, transcendentals=0),
+        name="gather_weights",
+    )(s, pm)
+
+def half_split(w, h):
+    n = w.shape[1] // 2
+    return w[:, h * n:(h + 1) * n]
+
+def pack_half(h, qkv, out, fc1, fc2, dec, vec):
+    def units(w):
+        n = w.shape[1] // LW
+        return w.reshape(6, n, LW).transpose(1, 0, 2).reshape(6 * n, LW)
+    rows = [units(half_split(qkv, h)), units(half_split(out, h)), units(half_split(fc1, h)), half_split(fc2, h),
+            jnp.concatenate([half_split(dec, h), vec[h]], axis=1), jnp.zeros((2, LW), jnp.bfloat16)]
+    return jnp.concatenate(rows, axis=0)
+
+def pack_vec(ln1_g, ln1_b, ln2_g, ln2_b, fc2_b, fc1_b, dec_b, mask):
+    cols = [ln1_g[:, None], ln1_b[:, None], ln2_g[:, None], ln2_b[:, None], fc2_b[:, None], fc1_b.reshape(6, 4),
+            jnp.pad(dec_b, (0, 2))[:, None], jnp.pad(mask, (0, 2))[:, None]]
+    v = jnp.concatenate(cols, axis=1)
+    return jnp.pad(v, ((0, 0), (0, 128 - v.shape[1])))
+
+def unpack_weights(g, g2):
+    def w(u0, u1):
+        a = g[:, u0:u1].reshape(2, u1 - u0, 768, LW)
+        return a.transpose(2, 0, 1, 3).reshape(768, 2 * (u1 - u0) * LW)
+    qkv, out, fc1 = w(0, 3), w(3, 4), w(4, 8)
+    fc2 = g2.reshape(2, 3072, LW).transpose(1, 0, 2).reshape(3072, 768)
+    dv = g[:, 8].reshape(2, 768, LW)
+    dec = dv[:, :, :256].transpose(1, 0, 2).reshape(768, 512)
+    v = dv[0, :, 256:]
+    vecs = (v[:, 0], v[:, 1], v[:, 2], v[:, 3], v[:, 4], v[:, 5:9].reshape(3072),
+            v[:, 9].reshape(128, 6)[:, :4].reshape(512), v[:, 10].reshape(128, 6)[:, :4].reshape(512))
+    return qkv, out, fc1, fc2, dec, vecs
+
+
+def rs_kernel(g_ref, g2_ref, pt_ref, o_ref, sg, sg2, acc, acc2, xa, xa2, xb, xb2, fs, f1, ssem, rsem, ss1, rs1, loc):
+    z, x, y, c = coords()
+    zp, zm, zo = (z + 1) % 4, (z + 3) % 4, (z + 2) % 4
+    xp, xm, xo = (x + 1) % 4, (x + 3) % 4, (x + 2) % 4
+    o = 1 - c
+    bar = pltpu.get_barrier_semaphore()
+    targets = [dev(zp, x, y, c), dev(zm, x, y, c), dev(z, xp, y, c), dev(z, xm, y, c)]
+    sib = dev(z, x, y, o)
+    group = []
+    for dy in range(4):
+        for dc in range(2):
+            if dy or dc:
+                group.append((dy, dc, dev(z, x, (y + dy) % 4, (c + dc) % 2)))
+    for t in targets + [g[2] for g in group]:
+        pl.semaphore_signal(bar, inc=1, device_id=t, device_id_type=MESH)
+    pl.semaphore_wait(bar, len(targets) + len(group))
+
+    sends = []
+    def send(k, i, src, dst, to):
+        cp = pltpu.make_async_remote_copy(src, dst, ssem.at[k, i], rsem.at[k, i], device_id=to, device_id_type=MESH)
+        cp.start(); sends.append(cp)
+    def recv(k, i, v):
+        pltpu.make_async_remote_copy(v, v, ssem.at[k, i], rsem.at[k, i], device_id=sib, device_id_type=MESH).wait_recv()
+    f32, bf = jnp.float32, jnp.bfloat16
+
+    def steps(k, chunk):
+        arr, order, full, fa, fb = chunk
+        zx = order == "zx"
+        if zx:
+            d1p, d1m, d2p, d2m = targets
+            p1, m1, o1, p2, m2, o2, s1_, s2_ = zp, zm, zo, xp, xm, xo, z, x
+        else:
+            d2p, d2m, d1p, d1m = targets
+            p1, m1, o1, p2, m2, o2, s1_, s2_ = xp, xm, xo, zp, zm, zo, x, z
+        def idx(part, a, b):
+            zs, xs = (a, b) if zx else (b, a)
+            r = pl.ds(part[0], part[1] - part[0])
+            return (r, zs, xs) if arr == "g" else (zs, xs, r)
+        A = acc if arr == "g" else acc2
+        def inp(h, part, a, b):
+            src = g_ref if arr == "g" else g2_ref
+            return src.at[(h,) + idx(part, a, b)]
+        SG = sg if arr == "g" else sg2
+        def xav(way, part):
+            r = slice(part[0], part[1])
+            return xa.at[way, r] if arr == "g" else xa2.at[way, :, r]
+        def xbv(way, part):
+            r = slice(part[0], part[1])
+            return xb.at[way, r] if arr == "g" else xb2.at[way, r]
+        def add(part, a, b, recvd):
+            i = idx(part, a, b)
+            A[i] = (A[i].astype(f32) + recvd[...].astype(f32)).astype(bf)
+        def st0():
+            send(k, 8, inp(o, full, ALL, ALL), SG.at[idx(full, ALL, ALL)], sib)
+        def st1():
+            recv(k, 8, SG.at[idx(full, ALL, ALL)])
+            def one(j, _):
+                i = idx(full, j, ALL)
+                A[i] = (inp(c, full, j, ALL)[...].astype(f32) + SG[i].astype(f32)).astype(bf)
+                return 0
+            lax.fori_loop(0, 4, one, 0)
+            send(k, 0, A.at[idx(fa, ALL, o2)], xav(0, fa), d2p)
+            if fb is not None: send(k, 1, A.at[idx(fb, ALL, o2)], xav(0, fb), d2m)
+        def st2():
+            recv(k, 0, xav(0, fa)); add(fa, ALL, p2, xav(0, fa))
+            send(k, 2, A.at[idx(full, ALL, p2)], xav(1, full), d2p)
+            if fb is not None:
+                recv(k, 1, xav(0, fb)); add(fb, ALL, m2, xav(0, fb))
+            send(k, 3, A.at[idx(full, ALL, m2)], xav(2, full), d2m)
+        def st3():
+            recv(k, 2, xav(1, full)); recv(k, 3, xav(2, full))
+            i = idx(full, ALL, s2_)
+            A[i] = (A[i].astype(f32) + xav(1, full)[...].astype(f32) + xav(2, full)[...].astype(f32)).astype(bf)
+            send(k, 4, A.at[idx(fa, o1, s2_)], xbv(0, fa), d1p)
+            if fb is not None: send(k, 5, A.at[idx(fb, o1, s2_)], xbv(0, fb), d1m)
+        def st4():
+            recv(k, 4, xbv(0, fa)); add(fa, p1, s2_, xbv(0, fa))
+            send(k, 6, A.at[idx(full, p1, s2_)], xbv(1, full), d1p)
+            if fb is not None:
+                recv(k, 5, xbv(0, fb)); add(fb, m1, s2_, xbv(0, fb))
+            send(k, 7, A.at[idx(full, m1, s2_)], xbv(2, full), d1m)
+        def st5():
+            recv(k, 6, xbv(1, full)); recv(k, 7, xbv(2, full))
+            i = idx(full, s1_, s2_)
+            A[i] = (A[i].astype(f32) + xbv(1, full)[...].astype(f32) + xbv(2, full)[...].astype(f32)).astype(bf)
+        return [st0, st1, st2, st3, st4, st5]
+
+    pieces = []
+    k = 0
+    for cl in ag_chunks():
+        lst = []
+        for ch in cl:
+            lst.append(steps(k, ch)); k += 1
+        pieces.append(lst)
+    pieces = pieces[::-1]
+    for t in range(len(pieces) + 5):
+        for p, lst in enumerate(pieces):
+            s = t - p
+            if 0 <= s < 6:
+                for ch in lst: ch[s]()
+    blk = jnp.concatenate([acc[:, z, x].reshape(432, LW), acc2[z, x]], axis=0)
+    r = jnp.dot(pt_ref[...], blk, preferred_element_type=f32).astype(bf)
+    fs[...] = r.reshape(8, SROWS, LW)
+    me = 2 * y + c
+    own = pltpu.make_async_copy(fs.at[me], f1.at[me], loc)
+    own.start()
+    lasts = []
+    for i, (dy, dc, t) in enumerate(group):
+        dst = 2 * ((y + dy) % 4) + (c + dc) % 2
+        cp = pltpu.make_async_remote_copy(fs.at[dst], f1.at[me], ss1.at[i], rs1.at[i], device_id=t, device_id_type=MESH)
+        cp.start()
+        src = 2 * ((y + 4 - dy) % 4) + (c + dc) % 2
+        rc = pltpu.make_async_remote_copy(fs.at[me], f1.at[src], ss1.at[i], rs1.at[i], device_id=t, device_id_type=MESH)
+        lasts.append((cp, rc))
+    own.wait()
+    for cp, rc in lasts: rc.wait_recv()
+    for h in range(2):
+        t = f1[h].astype(f32)
+        for yy in range(1, 4): t = t + f1[2 * yy + h].astype(f32)
+        o_ref[h] = t
+    for cp, rc in lasts: cp.wait_send()
+    for cp in sends: cp.wait_send()
+
+def rs_call(g, g2, pt):
+    nk = sum(len(c) for c in ag_chunks())
+    V, bf = pltpu.VMEM, jnp.bfloat16
+    return pl.pallas_call(
+        rs_kernel,
+        out_shape=jax.ShapeDtypeStruct((2, SROWS, LW), jnp.float32),
+        in_specs=[pl.BlockSpec(memory_space=pltpu.VMEM)] * 3,
+        out_specs=pl.BlockSpec(memory_space=pltpu.VMEM),
+        scratch_shapes=[
+            V((9, 4, 4, 48, LW), bf), V((4, 4, 192, LW), bf),
+            V((9, 4, 4, 48, LW), bf), V((4, 4, 192, LW), bf),
+            V((3, 9, 4, 48, LW), bf), V((3, 4, 192, LW), bf),
+            V((3, 9, 48, LW), bf), V((3, 192, LW), bf),
+            V((8, SROWS, LW), bf), V((8, SROWS, LW), bf),
+            pltpu.SemaphoreType.DMA((nk, 9)), pltpu.SemaphoreType.DMA((nk, 9)),
+            pltpu.SemaphoreType.DMA((7,)), pltpu.SemaphoreType.DMA((7,)), pltpu.SemaphoreType.DMA(()),
+        ],
+        compiler_params=pltpu.CompilerParams(collective_id=1, has_side_effects=True, vmem_limit_bytes=60 * 2**20),
+        cost_estimate=pl.CostEstimate(flops=10**9, bytes_accessed=3 * 10**7, transcendentals=0),
+        name="scatter_grads",
+    )(g, g2, pt)
+
+def pack_grads(qkv, out, fc1, fc2, dec, vec):
+    bf = jnp.bfloat16
+    def u(w):
+        w = w.astype(bf)
+        n = w.shape[1] // LW // 2
+        return w.reshape(768, 2, n, LW).transpose(1, 2, 0, 3)
+    d = dec.astype(bf).reshape(768, 2, 256).transpose(1, 0, 2)
+    v = jnp.stack([vec.astype(bf), jnp.zeros_like(vec, bf)])
+    dv = jnp.concatenate([d, v], axis=2)[:, None]
+    g = jnp.concatenate([u(qkv), u(out), u(fc1), dv], axis=1).reshape(2, 9, 4, 4, 48, LW)
+    g2 = fc2.astype(bf).reshape(3072, 2, LW).transpose(1, 0, 2).reshape(2, 4, 4, 192, LW)
+    return g, g2
+
+def pack_vec_full(ln1_g, ln1_b, ln2_g, ln2_b, fc2_b, fc1_b, dec_b, mask):
+    p4 = lambda v: jnp.pad(v.reshape(128, 4), ((0, 0), (0, 2))).reshape(768, 1)
+    cols = [ln1_g[:, None], ln1_b[:, None], ln2_g[:, None], ln2_b[:, None], fc2_b[:, None], fc1_b.reshape(768, 4), p4(dec_b), p4(mask)]
+    v = jnp.concatenate(cols, axis=1)
+    return jnp.pad(v, ((0, 0), (0, 128 - v.shape[1])))
+
+def unpack_grads(r):
+    def u(a, n):
+        return a.reshape(2, n, 6, LW).transpose(2, 0, 1, 3).reshape(6, 2 * n * LW)
+    qkv, out, fc1 = u(r[:, 0:18], 3), u(r[:, 18:24], 1), u(r[:, 24:48], 4)
+    fc2 = r[:, 48:72].transpose(1, 0, 2).reshape(24, 768)
+    dec = r[:, 72:78, :256].transpose(1, 0, 2).reshape(6, 512)
+    v = r[0, 72:78, 256:]
+    return qkv, out, fc1, fc2, dec, (v[:, 0], v[:, 1], v[:, 2], v[:, 3], v[:, 4], v[:, 5:9].reshape(24), v[:4, 9], v[:4, 10])
+
+
 def body(
     tokens,
     chip_lengths,
@@ -126,20 +504,17 @@
     mask_token,
     grid_cotangent,
 ):
+    all_tokens = tokens
+    tokens = tokens[:ROWS]
+    positions = positions[:ROWS]
+    vec = pack_vec(ln1_gain, ln1_bias, ln2_gain, ln2_bias, fc2_bias, fc1_bias, dec_bias, mask_token)
+    packed = jnp.stack(
+        [pack_half(h, qkv_weight, out_weight, fc1_weight, fc2_weight, dec_weight, [vec, jnp.zeros_like(vec)]) for h in range(2)]
+    )
+    perm = jnp.asarray(perm_matrix(), jnp.bfloat16)
+    w_qkv, w_out, w_fc1, w_fc2, w_dec, vecs = unpack_weights(*ag_call(packed, perm))
     gathered = (
-        lax.all_gather(ln1_gain, ("dp", "fsdp"), axis=0, tiled=True),
-        lax.all_gather(ln1_bias, ("dp", "fsdp"), axis=0, tiled=True),
-        lax.all_gather(qkv_weight, ("dp", "fsdp"), axis=0, tiled=True),
-        lax.all_gather(out_weight, ("dp", "fsdp"), axis=0, tiled=True),
-        lax.all_gather(ln2_gain, ("dp", "fsdp"), axis=0, tiled=True),
-        lax.all_gather(ln2_bias, ("dp", "fsdp"), axis=0, tiled=True),
-        lax.all_gather(fc1_weight, ("dp", "fsdp"), axis=0, tiled=True),
-        lax.all_gather(fc1_bias, ("dp", "fsdp"), axis=0, tiled=True),
-        lax.all_gather(fc2_weight, ("dp", "fsdp"), axis=0, tiled=True),
-        lax.all_gather(fc2_bias, ("dp", "fsdp"), axis=0, tiled=True),
-        lax.all_gather(dec_weight, ("dp", "fsdp"), axis=0, tiled=True),
-        lax.all_gather(dec_bias, ("dp", "fsdp"), axis=0, tiled=True),
-        lax.all_gather(mask_token, ("dp", "fsdp"), axis=0, tiled=True),
+        vecs[0], vecs[1], w_qkv, w_out, vecs[2], vecs[3], w_fc1, vecs[5], w_fc2, vecs[4], w_dec, vecs[6], vecs[7],
     )
     segment, fill_table, empty_cells = pack_layout(chip_lengths, positions)
     forward_saved = layer_forward(gathered, tokens, segment)
@@ -173,21 +548,7 @@
     returned = left_product(placement, grid_cotangent.reshape(group_size, -1))
     returned = returned.astype(jnp.bfloat16).reshape(grid_cotangent.shape)
     grid_grad = lax.all_to_all(returned, "fsdp", split_axis=0, concat_axis=1, tiled=True)
-    weights = (
-        lax.all_gather(ln1_gain, ("dp", "fsdp"), axis=0, tiled=True),
-        lax.all_gather(ln1_bias, ("dp", "fsdp"), axis=0, tiled=True),
-        lax.all_gather(qkv_weight, ("dp", "fsdp"), axis=0, tiled=True),
-        lax.all_gather(out_weight, ("dp", "fsdp"), axis=0, tiled=True),
-        lax.all_gather(ln2_gain, ("dp", "fsdp"), axis=0, tiled=True),
-        lax.all_gather(ln2_bias, ("dp", "fsdp"), axis=0, tiled=True),
-        lax.all_gather(fc1_weight, ("dp", "fsdp"), axis=0, tiled=True),
-        lax.all_gather(fc1_bias, ("dp", "fsdp"), axis=0, tiled=True),
-        lax.all_gather(fc2_weight, ("dp", "fsdp"), axis=0, tiled=True),
-        lax.all_gather(fc2_bias, ("dp", "fsdp"), axis=0, tiled=True),
-        lax.all_gather(dec_weight, ("dp", "fsdp"), axis=0, tiled=True),
-        lax.all_gather(dec_bias, ("dp", "fsdp"), axis=0, tiled=True),
-        lax.all_gather(mask_token, ("dp", "fsdp"), axis=0, tiled=True),
-    )
+    weights = gathered
     (
         inputs,
         normed,
@@ -202,7 +563,7 @@
         pre_act,
         activated,
         after_mlp,
-    ) = layer_forward(weights, tokens, segment)
+    ) = forward_saved
     token_count = tokens.shape[0]
     gain_one = weights[0].astype(jnp.float32)
     bias_one = weights[1].astype(jnp.float32)
@@ -261,37 +622,26 @@
     unused_one, norm_one_pull = jax.vjp(ln_affine, inputs, gain_one, bias_one)
     input_part, ln1_g_grad, ln1_b_grad = norm_one_pull(normed_grad)
     tokens_grad = resid_grad + input_part
-    shares = (
-        lax.psum_scatter(ln1_g_grad, ("dp", "fsdp"), scatter_dimension=0, tiled=True),
-        lax.psum_scatter(ln1_b_grad, ("dp", "fsdp"), scatter_dimension=0, tiled=True),
-        lax.psum_scatter(qkv_w_grad, ("dp", "fsdp"), scatter_dimension=0, tiled=True),
-        lax.psum_scatter(out_w_grad, ("dp", "fsdp"), scatter_dimension=0, tiled=True),
-        lax.psum_scatter(ln2_g_grad, ("dp", "fsdp"), scatter_dimension=0, tiled=True),
-        lax.psum_scatter(ln2_b_grad, ("dp", "fsdp"), scatter_dimension=0, tiled=True),
-        lax.psum_scatter(fc1_w_grad, ("dp", "fsdp"), scatter_dimension=0, tiled=True),
-        lax.psum_scatter(fc1_b_grad, ("dp", "fsdp"), scatter_dimension=0, tiled=True),
-        lax.psum_scatter(fc2_w_grad, ("dp", "fsdp"), scatter_dimension=0, tiled=True),
-        lax.psum_scatter(fc2_b_grad, ("dp", "fsdp"), scatter_dimension=0, tiled=True),
-        lax.psum_scatter(dec_w_grad, ("dp", "fsdp"), scatter_dimension=0, tiled=True),
-        lax.psum_scatter(dec_b_grad, ("dp", "fsdp"), scatter_dimension=0, tiled=True),
-        lax.psum_scatter(mask_grad, ("dp", "fsdp"), scatter_dimension=0, tiled=True),
-    )
+    tokens_grad = jnp.pad(tokens_grad, ((0, all_tokens.shape[0] - ROWS), (0, 0)))
+    vec_grad = pack_vec_full(ln1_g_grad, ln1_b_grad, ln2_g_grad, ln2_b_grad, fc2_b_grad, fc1_b_grad, dec_b_grad, mask_grad)
+    g, g2 = pack_grads(qkv_w_grad, out_w_grad, fc1_w_grad, fc2_w_grad, dec_w_grad, vec_grad)
+    s_qkv, s_out, s_fc1, s_fc2, s_dec, s_vec = unpack_grads(rs_call(g, g2, perm.T))
     return (
         full_grid,
         tokens_grad,
-        shares[0],
-        shares[1],
-        shares[2],
-        shares[3],
-        shares[4],
-        shares[5],
-        shares[6],
-        shares[7],
-        shares[8],
-        shares[9],
-        shares[10],
-        shares[11],
-        shares[12],
+        s_vec[0],
+        s_vec[1],
+        s_qkv,
+        s_out,
+        s_vec[2],
+        s_vec[3],
+        s_fc1,
+        s_vec[5],
+        s_fc2,
+        s_vec[4],
+        s_dec,
+        s_vec[6],
+        s_vec[7],
     )
 
 

time: 1380 us -> 454 us (0.33)
  blocking collectives: 550 us -> 0 us
  starting transfers between devices: 357 us -> 17.5 us
  Pallas kernels: 0 us -> 147 us
  local copies, waits for them, and re-layouts: 226 us -> 135 us
  matrix products: 120 us -> 74.3 us
  waiting for transfers between devices: 76 us -> 40.5 us
  between operations: 17.9 us -> 3.35 us
    unnamed x3 -> x0, blocking collectives: 493 us -> none
    unnamed x128 -> x0, starting transfers between devices: 339 us -> none
    unnamed x336 -> x127, local copies, waits for them, and re-layouts: 206 us -> 16.6 us
    pallas_call x0 -> x2, Pallas kernels: none -> 147 us  [the longest x1 74.2 us: ag_call(): pl.pallas_call(ag_kernel, out_shape=(jax.ShapeDtypeStruct((2, 9, 4, 4, 48...]
    all_gather x4 -> x0, waiting for transfers between devices: 57.7 us -> none  [the longest x1 39.7 us: body(): lax.all_gather(fc2_weight, ('dp', 'fsdp'), axis=0, tiled=True)]
    all_gather x1 -> x0, blocking collectives: 57.5 us -> none  [body(): lax.all_gather(dec_weight, ('dp', 'fsdp'), axis=0, tiled=True)]
    reshape x0 -> x23, local copies, waits for them, and re-layouts: none -> 49.3 us  [the longest x3 16.3 us: u(): return w.reshape(768, 2, n, LW).transpose(1, 2, 0, 3)]
    all_to_all x1, waiting for transfers between devices: 0.01 us -> 21.7 us  [body(): lax.all_to_all(returned, 'fsdp', split_axis=0, concat_axis=1, tiled=True)]
  transfers between devices with their start and end apart: 136 -> 3, of which waited for: 5 -> 2; matrix products, arithmetic and copies ran while one was open for 51% -> 27% of each run, Pallas kernels for 0% -> 17%
where the time goes in v1:
time: 454 us; the launch traced here: 446 us
  Pallas kernels  147 us (32%)
  local copies, waits for them, and re-layouts  135 us (30%)
  matrix products  74.3 us (16%)
  waiting for transfers between devices  40.5 us (9%)
  other arithmetic  27.4 us (6%)
  starting transfers between devices  17.5 us (4%)
    pallas_call x1, Pallas kernels, ag_call(): pl.pallas_call(ag_kernel, out_shape=(jax.ShapeDtypeStruct((2, 9, 4, 4, 48...  74.2 us
    pallas_call x1, Pallas kernels, rs_call(): pl.pallas_call(rs_kernel, out_shape=jax.ShapeDtypeStruct((2, SROWS, LW),...  73.3 us
    all_to_all x1, waiting for transfers between devices, body(): lax.all_to_all(returned, 'fsdp', split_axis=0, concat_axis=1, tiled=True)  21.7 us
    dot_general x7, matrix products, left_product(): lax.dot_general(left, right, (((0,), (0,)), ((), ())), preferred_element_...  20.2 us
    all_to_all x1, waiting for transfers between devices, body(): lax.all_to_all(cell_values, 'fsdp', split_axis=1, concat_axis=0, tiled=True)  18.8 us
    unnamed x127, local copies, waits for them, and re-layouts  16.6 us
    reshape x3, local copies, waits for them, and re-layouts, u(): return w.reshape(768, 2, n, LW).transpose(1, 2, 0, 3)  16.3 us
    dot_general x1, matrix products, layer_forward(): jnp.dot(normed_two, weights[6], preferred_element_type=jnp.float32)  14.1 us
  transfers between devices with their start and end apart: 3, of which 2 were waited for; matrix products, arithmetic and copies ran while one was open for 27% of the time, Pallas kernels for 17%

profile of v1, /device:TPU:1, one launch (start us, length us, event | category | flops | bytes accessed | tf_op | source)
XLA Modules:
  0.0 445.9 jit_solution(14361349014724588623)
XLA Ops:
  1.9 6.9 %all-to-all-start = ((bf16[2,16,1]{0,2,1:T(2,128)(2,1)}), bf16[2,16,1]{0,2,1:T(2,128)(2,1)}, u32[]{:S(2)}, u32[]{:S(2)}) async-start(bf16[2,16,1]{0,2,1:T(2,128)(2,1)} %broadcast_in_dim.57), calls=%async_computation | async-start | bytes 16384 | tf_op jit(solution)/shard_map/all_to_all | solution.py:537
  22.1 74.2 %gather_weights.1 = (bf16[2,9,4,4,48,384]{5,4,3,2,1,0:T(8,128)(2,1)}, bf16[2,4,4,192,384]{4,3,2,1,0:T(8,128)(2,1)}) custom-call(bf16[2,80,384]{2,1,0:T(8,128)(2,1)} %pad_maximum_fusion.4.s_ref, bf16[624,640]{1,0:T(8,128)(2,1)} %constant.125.clone.p_ref), custom_call_target="tpu_custom_call" | custom-call | flops 1000000000 | bytes 30000000 | tf_op jit(solution)/shard_map/gather_weights/pallas_call | solution.py:266
  96.2 2.9 fusion.83
  101.5 2.4 slice.159
  103.9 5.0 %slice.166 = bf16[2,4,4,4,48,384]{5,4,3,2,1,0:T(8,128)(2,1)} slice(bf16[2,9,4,4,48,384]{5,4,3,2,1,0:T(8,128)(2,1)} %get-tuple-element.17), slice={[0:2], [4:8], [0:4], [0:4], [0:48], [0:384]} | slice | bytes 9437184 | tf_op jit(solution)/shard_map/slice | solution.py:301
  114.2 6.7 %copy.216 = bf16[2,3072,384]{1,2,0:T(8,128)(2,1)} copy(bf16[2,3072,384]{2,1,0:T(8,128)(2,1)} %bitcast.198) | data formatting | bytes 9437184 | tf_op jit(solution)/shard_map/reshape | solution.py:304
  120.9 2.4 copy.213
  123.3 2.3 copy.249
  137.0 6.7 %copy.214 = bf16[2,4,768,384]{2,3,1,0:T(8,128)(2,1)} copy(bf16[2,4,768,384]{3,2,1,0:T(8,128)(2,1)} %bitcast.167) | data formatting | bytes 9437184 | tf_op jit(solution)/shard_map/reshape | solution.py:301
  143.7 3.9 copy.208
  147.7 3.7 convolution_convert_fusion.5
  152.4 4.8 %fusion.92 = (f32[12,336]{1,0:T(8,128)S(1)}, f32[12,336,336]{1,2,0:T(8,128)}) fusion(pred[336,336]{0,1:T(8,128)(4,1)S(1)} %copy-done.21, bf16[336,12,64]{0,2,1:T(8,128)(2,1)S(1)} %bitcast.213, bf16[336,12,64]{0,2,1:T(8,128)(2,1)S(1)} %bitcast.211), kind=kOutput, calls=%fused_computation.178 | convolution fusion | flops 178827600 | bytes 6580224 | tf_op jit(solution)/shard_map/sub | solution.py:81
  157.3 3.6 fusion.26
  162.1 14.1 %multiply_convert_fusion.1 = (bf16[336,3072]{1,0:T(8,128)(2,1)S(1)}, f32[336,3072]{1,0:T(8,128)}, f32[336,3072]{1,0:T(8,128)}) fusion(f32[3072]{0:T(1024)S(1)} %copy-done.30, bf16[768,3072]{0,1:T(8,128)(2,1)S(1)} %bitcast.193, f32[336,768]{1,0:T(8,128)S(1)} %get-tuple-element.68, f32[768]{0:T(1024)S(1)} %copy-done.33, f32[768]{0:T(1024)S(1)} %copy-done.29, ...), kind=kOutput, calls=%fused_computation.17 | convolution fusion | flops 1654861824 | bytes 16093824 | tf_op jit(solution)/shard_map/dot_general | solution.py:88
  176.3 2.6 fusion.33
  179.0 4.1 add_convert_fusion
  183.1 5.1 %copy.218 = bf16[2,1024,512]{2,0,1:T(2,128)(2,1)} copy(bf16[2,1024,512]{2,1,0:T(8,128)(2,1)} %bitcast.219) | data formatting | bytes 4194304 | tf_op jit(solution)/shard_map/reshape | solution.py:532
  188.1 4.3 all-to-all-start.1
  192.5 4.1 copy.255
  197.4 2.3 convolution_convert_fusion
  199.8 2.0 copy.256
  201.8 18.8 %all-to-all-done.1 = bf16[2,1024,512]{2,0,1:T(2,128)(2,1)} async-done(((bf16[2,1024,512]{2,0,1:T(2,128)(2,1)}), bf16[2,1024,512]{2,0,1:T(2,128)(2,1)}, u32[]{:S(2)}, u32[]{:S(2)}) %all-to-all-start.1) | async-done | bytes 2097184 | tf_op jit(solution)/shard_map/all_to_all | solution.py:536
  220.6 6.3 %all-to-all-start.2 = ((bf16[32,64,512]{2,1,0:T(8,128)(2,1)}), bf16[32,64,512]{2,1,0:T(8,128)(2,1)}, u32[]{:S(2)}, u32[]{:S(2)}) async-start(bf16[32,64,512]{2,1,0:T(8,128)(2,1)} %bitcast.176), calls=%async_computation.2 | async-start | bytes 4194304 | tf_op jit(solution)/shard_map/all_to_all | solution.py:550
  227.0 1.9 copy.219
  231.0 2.0 copy.254
  233.1 21.7 %all-to-all-done.2 = bf16[32,64,512]{2,1,0:T(8,128)(2,1)} async-done(((bf16[32,64,512]{2,1,0:T(8,128)(2,1)}), bf16[32,64,512]{2,1,0:T(8,128)(2,1)}, u32[]{:S(2)}, u32[]{:S(2)}) %all-to-all-start.2) | async-done | bytes 2097184 | tf_op jit(solution)/shard_map/all_to_all | solution.py:550
  254.8 2.0 copy.221
  261.6 3.2 fusion.94
  264.9 2.0 multiply_reduce_fusion.2
  268.9 1.8 convolution_convert_fusion.6
  270.7 4.8 %convolution_convert_fusion.3 = bf16[768,3072]{1,0:T(8,128)(2,1)} fusion(bf16[336,3072]{1,0:T(8,128)(2,1)S(1)} %get-tuple-element.77, f32[336,768]{1,0:T(8,128)S(1)} %get-tuple-element.68, f32[768]{0:T(1024)S(1)} %copy-done.33, f32[768]{0:T(1024)S(1)} %copy-done.29, f32[336]{0:T(512)S(1)} %fusion.67, f32[336]{0:T(512)S(1)} %broadcast_multiply_fusion), kind=kOutput, calls=%fused_computation.10 | convolution fusion | flops 1589096448 | bytes 7824000 | tf_op jit(solution)/shard_map/dot_general | solution.py:33
  275.5 4.6 %convolution_convert_fusion.2 = bf16[3072,768]{0,1:T(8,128)(2,1)} fusion(bf16[336,3072]{1,0:T(8,128)(2,1)S(1)} %copy-done.46, f32[336,768]{1,0:T(8,128)S(1)} %get-tuple-element.75), kind=kOutput, calls=%fused_computation.9 | convolution fusion | flops 1588064256 | bytes 7815168 | tf_op jit(solution)/shard_map/dot_general | solution.py:33
  280.4 4.8 %fusion.29 = bf16[12,64,336]{2,1,0:T(8,128)(2,1)} fusion(bf16[336,12,64]{0,2,1:T(8,128)(2,1)S(1)} %bitcast.222, f32[12,336,336]{1,2,0:T(8,128)} %get-tuple-element.66, f32[12,336]{1,0:T(8,128)S(1)} %get-tuple-element.65), kind=kOutput, calls=%fused_computation.65 | convolution fusion | flops 176375808 | bytes 6467328 | tf_op jit(solution)/shard_map/hqk,qhd->khd/dot_general | solution.py:600
  285.2 4.0 multiply_reduce_fusion
  292.7 2.4 fusion.80
  295.1 4.1 convolution_convert_fusion.4
  299.5 4.0 copy.231
  303.5 4.2 dot_general.107
  307.7 2.8 multiply_reduce_fusion.1
  311.2 2.3 copy.230
  315.2 9.6 %reshape.454 = bf16[768,2,4,384]{3,2,1,0:T(4,128)(2,1)} reshape(bf16[768,3072]{1,0:T(8,128)(2,1)} %convolution_convert_fusion.3) | data formatting | bytes 9437184 | tf_op jit(solution)/shard_map/reshape | solution.py:463
  324.8 5.0 %copy.229 = bf16[768,2,4,384]{3,0,2,1:T(8,128)(2,1)} copy(bf16[768,2,4,384]{3,2,1,0:T(4,128)(2,1)} %reshape.454) | data formatting | bytes 9437184 | tf_op jit(solution)/shard_map/reshape | solution.py:463
  329.8 6.7 %copy.234 = bf16[3072,2,384]{2,0,1:T(8,128)(2,1)} copy(bf16[3072,2,384]{0,2,1:T(8,128)(2,1)} %bitcast.197) | data formatting | bytes 9437184 | tf_op jit(solution)/shard_map/reshape | solution.py:468
  337.5 5.8 %copy.226 = bf16[768,2304]{0,1:T(8,128)(2,1)} copy(bf16[768,2304]{1,0:T(8,128)(2,1)} %convolution_convert_fusion.4) | data formatting | bytes 7077888 | tf_op jit(solution)/shard_map/convert_element_type | solution.py:461
  343.3 6.1 %copy.227 = bf16[2,3,768,384]{3,2,1,0:T(8,128)(2,1)} copy(bf16[2,3,768,384]{2,3,1,0:T(8,128)(2,1)} %bitcast.170) | data formatting | bytes 7077888 | tf_op jit(solution)/shard_map/transpose | solution.py:463
  350.7 9.0 %pad_maximum_fusion.g_ref = bf16[2,9,4,4,48,384]{5,4,3,2,1,0:T(8,128)(2,1)} fusion(bf16[2,1,4,4,48,384]{5,4,3,2,1,0:T(8,128)(2,1)S(1)} %bitcast.202, bf16[2,4,4,4,48,384]{5,4,3,2,1,0:T(8,128)(2,1)} %bitcast.168, bf16[2,1,4,4,48,384]{5,4,3,2,1,0:T(8,128)(2,1)S(1)} %bitcast.201, bf16[2,3,4,4,48,384]{5,4,3,2,1,0:T(8,128)(2,1)} %bitcast.171), kind=kLoop, calls=%fused_computation.3 | loop fusion | flops 15925248 | bytes 21233664 | tf_op jit(solution)/shard_map/concatenate | solution.py:467
  359.7 73.3 %scatter_grads.1 = f32[2,80,384]{2,1,0:T(8,128)} custom-call(bf16[2,9,4,4,48,384]{5,4,3,2,1,0:T(8,128)(2,1)} %pad_maximum_fusion.g_ref, bf16[2,4,4,192,384]{4,3,2,1,0:T(8,128)(2,1)} %bitcast.166, bf16[640,624]{1,0:T(8,128)(2,1)} %constant.159.pt_ref), custom_call_target="tpu_custom_call" | custom-call | flops 1000000000 | bytes 30000000 | tf_op jit(solution)/shard_map/scatter_grads/pallas_call | solution.py:439
  443.0 2.5 pad.34
  (245 shorter events, 62.9 us)
Async XLA Ops:
  1.9 186.2 %all-to-all-start = ((bf16[2,16,1]{0,2,1:T(2,128)(2,1)}), bf16[2,16,1]{0,2,1:T(2,128)(2,1)}, u32[]{:S(2)}, u32[]{:S(2)}) async-start(bf16[2,16,1]{0,2,1:T(2,128)(2,1)} %broadcast_in_dim.57), calls=%async_computation | async-start | bytes 16384 | tf_op jit(solution)/shard_map/all_to_all | solution.py:537
  103.9 7.3 %copy-start.35 = (s32[512]{0:T(512)S(1)}, s32[512]{0:T(512)}, u32[]{:S(2)}) copy-start(s32[512]{0:T(512)} %param.22) | copy-start | bytes 6148
  103.9 8.4 %copy-start.1 = (bf16[512,768]{1,0:T(8,128)(2,1)S(1)}, bf16[512,768]{1,0:T(8,128)(2,1)}, u32[]{:S(2)}) copy-start(bf16[512,768]{1,0:T(8,128)(2,1)} %param.19) | copy-start | bytes 2359300
  103.9 9.7 %copy-start.41 = (s32[2]{0:T(128)S(1)}, s32[2]{0:T(128)}, u32[]{:S(2)}) copy-start(s32[2]{0:T(128)} %get-tuple-element.82) | copy-start | bytes 28
  111.1 2.4 copy-start.36
  143.7 4.0 copy-start.23
  143.7 4.0 copy-start.25
  143.7 4.0 copy-start.31
  151.8 5.4 %copy-start.11 = (bf16[336,768]{0,1:T(8,128)(2,1)}, bf16[336,768]{0,1:T(8,128)(2,1)S(1)}, u32[]{:S(2)}) copy-start(bf16[336,768]{0,1:T(8,128)(2,1)S(1)} %copy.211) | copy-start | bytes 1548292
  152.1 5.1 %copy-start.13 = (bf16[336,768]{0,1:T(8,128)(2,1)}, bf16[336,768]{0,1:T(8,128)(2,1)S(1)}, u32[]{:S(2)}) copy-start(bf16[336,768]{0,1:T(8,128)(2,1)S(1)} %copy.210) | copy-start | bytes 1548292
  152.4 4.8 %copy-start.18 = (bf16[336,768]{0,1:T(8,128)(2,1)}, bf16[336,768]{0,1:T(8,128)(2,1)S(1)}, u32[]{:S(2)}) copy-start(bf16[336,768]{0,1:T(8,128)(2,1)S(1)} %copy.209) | copy-start | bytes 1548292
  157.2 4.8 %slice-start.6 = ((s8[4718592]{0:T(1024)(128)(4,1)}), s8[4194304]{0:T(1024)(128)(4,1)S(1)}, s32[]{:S(2)}) async-start(s8[4718592]{0:T(1024)(128)(4,1)} %bitcast.191), calls=%async_computation.9 | async-start | bytes 8388608
  157.2 3.7 copy-start
  157.2 3.7 copy-start.2
  157.3 4.9 %slice-start.7 = ((s8[4718592]{0:T(1024)(128)(4,1)}), s8[524288]{0:T(1024)(128)(4,1)S(1)}, s32[]{:S(2)}) async-start(s8[4718592]{0:T(1024)(128)(4,1)} %bitcast.191), calls=%async_computation.10 | async-start | bytes 1048576
  160.9 15.3 %slice-start.2 = ((s8[4718592]{0:T(1024)(128)(4,1)}), s8[4194304]{0:T(1024)(128)(4,1)S(1)}, s32[]{:S(2)}) async-start(s8[4718592]{0:T(1024)(128)(4,1)} %bitcast.185), calls=%async_computation.5 | async-start | bytes 8388608
  162.1 14.1 %slice-start.3 = ((s8[4718592]{0:T(1024)(128)(4,1)}), s8[524288]{0:T(1024)(128)(4,1)S(1)}, s32[]{:S(2)}) async-start(s8[4718592]{0:T(1024)(128)(4,1)} %bitcast.185), calls=%async_computation.6 | async-start | bytes 1048576
  162.1 14.1 %copy-start.34 = (f32[768]{0:T(1024)S(1)}, f32[768]{0:T(1024)}, u32[]{:S(2)}) copy-start(f32[768]{0:T(1024)} %get-tuple-element.28) | copy-start | bytes 9220
  176.3 2.7 copy-start.45
  176.3 2.7 copy-start.10
  176.3 2.7 copy-start.37
  176.3 2.6 copy-start.39
  176.3 2.6 copy-start.40
  188.1 32.4 %all-to-all-start.1 = ((bf16[2,1024,512]{2,0,1:T(2,128)(2,1)}), bf16[2,1024,512]{2,0,1:T(2,128)(2,1)}, u32[]{:S(2)}, u32[]{:S(2)}) async-start(bf16[2,1024,512]{2,0,1:T(2,128)(2,1)} %copy.218), calls=%async_computation.1 | async-start | bytes 4194304 | tf_op jit(solution)/shard_map/all_to_all | solution.py:536
  199.7 27.2 %copy-start.42 = (s32[2]{0:T(128)S(1)}, s32[2]{0:T(128)}, u32[]{:S(2)}) copy-start(s32[2]{0:T(128)} %get-tuple-element.82) | copy-start | bytes 28
  199.7 27.2 %copy-start.43 = (s32[2]{0:T(128)S(1)}, s32[2]{0:T(128)}, u32[]{:S(2)}) copy-start(s32[2]{0:T(128)} %get-tuple-element.81) | copy-start | bytes 28
  220.6 34.2 %all-to-all-start.2 = ((bf16[32,64,512]{2,1,0:T(8,128)(2,1)}), bf16[32,64,512]{2,1,0:T(8,128)(2,1)}, u32[]{:S(2)}, u32[]{:S(2)}) async-start(bf16[32,64,512]{2,1,0:T(8,128)(2,1)} %bitcast.176), calls=%async_computation.2 | async-start | bytes 4194304 | tf_op jit(solution)/shard_map/all_to_all | solution.py:550
  254.8 5.0 %slice-start.4 = ((s8[4718592]{0:T(1024)(128)(4,1)}), s8[4194304]{0:T(1024)(128)(4,1)S(1)}, s32[]{:S(2)}) async-start(s8[4718592]{0:T(1024)(128)(4,1)} %bitcast.188), calls=%async_computation.7 | async-start | bytes 8388608
  256.8 3.0 slice-start.5
  256.8 3.7 copy-start.47
  256.8 4.9 %copy-start.48 = (f32[336,3072]{1,0:T(8,128)S(1)}, f32[336,3072]{1,0:T(8,128)}, u32[]{:S(2)}) copy-start(f32[336,3072]{1,0:T(8,128)} %get-tuple-element.69) | copy-start | bytes 12386308
  257.7 7.1 %slice-start.8 = ((s8[4718592]{0:T(1024)(128)(4,1)}), s8[4194304]{0:T(1024)(128)(4,1)S(1)}, s32[]{:S(2)}) async-start(s8[4718592]{0:T(1024)(128)(4,1)} %bitcast.194), calls=%async_computation.11 | async-start | bytes 8388608
  261.6 3.2 slice-start.9
  270.7 4.8 %copy-start.46 = (bf16[336,3072]{1,0:T(8,128)(2,1)S(1)}, bf16[336,3072]{1,0:T(8,128)(2,1)}, u32[]{:S(2)}) copy-start(bf16[336,3072]{1,0:T(8,128)(2,1)} %copy-done.45) | copy-start | bytes 6193156
  275.5 4.6 %copy-start.17 = (bf16[336,768]{1,0:T(8,128)(2,1)S(1)}, bf16[336,768]{1,0:T(8,128)(2,1)}, u32[]{:S(2)}) copy-start(bf16[336,768]{1,0:T(8,128)(2,1)} %convolution_convert_fusion.8) | copy-start | bytes 1548292
  280.4 4.8 %copy-start.19 = (bf16[336,768]{0,1:T(8,128)(2,1)S(1)}, bf16[336,768]{0,1:T(8,128)(2,1)}, u32[]{:S(2)}) copy-start(bf16[336,768]{0,1:T(8,128)(2,1)} %copy-done.18) | copy-start | bytes 1548292
  280.4 8.8 %slice-start = ((s8[6193152]{0:T(1024)(128)(4,1)}), s8[4194304]{0:T(1024)(128)(4,1)S(1)}, s32[]{:S(2)}) async-start(s8[6193152]{0:T(1024)(128)(4,1)} %bitcast.183), calls=%async_computation.3 | async-start | bytes 8388608
  285.2 4.0 slice-start.1
  290.2 2.3 copy-start.9
  290.3 2.4 copy-start.44
  292.6 2.4 copy-start.26
  292.7 2.4 copy-start.32
  303.5 10.1 %copy-start.5 = (bf16[768,768]{0,1:T(8,128)(2,1)S(1)}, bf16[768,768]{0,1:T(8,128)(2,1)}, u32[]{:S(2)}) copy-start(bf16[768,768]{0,1:T(8,128)(2,1)} %convolution_convert_fusion.6) | copy-start | bytes 3538948
  329.8 6.7 %copy-start.28 = (f32[336]{0:T(512)S(1)}, f32[336]{0:T(512)}, u32[]{:S(2)}) copy-start(f32[336]{0:T(512)} %copy-done.27) | copy-start | bytes 4036
  329.8 6.8 %copy-start.7 = (f32[336,768]{1,0:T(8,128)S(1)}, f32[336,768]{1,0:T(8,128)}, u32[]{:S(2)}) copy-start(f32[336,768]{1,0:T(8,128)} %get-tuple-element.73) | copy-start | bytes 3096580
  343.3 7.4 %copy-start.6 = (bf16[768,2,1,384]{3,0,1,2:T(8,128)(2,1)S(1)}, bf16[768,2,1,384]{3,0,1,2:T(8,128)(2,1)}, u32[]{:S(2)}) copy-start(bf16[768,2,1,384]{3,0,1,2:T(8,128)(2,1)} %copy.228) | copy-start | bytes 3538948
  359.7 79.2 %copy-start.8 = (f32[336,768]{1,0:T(8,128)S(1)}, f32[336,768]{1,0:T(8,128)}, u32[]{:S(2)}) copy-start(f32[336,768]{1,0:T(8,128)} %get-tuple-element.73) | copy-start | bytes 3096580
  433.0 7.9 %slice-start.10 = ((f32[2,80,384]{2,1,0:T(8,128)}), f32[2,18,384]{2,1,0:T(8,128)S(1)}, s32[]{:S(2)}) async-start(f32[2,80,384]{2,1,0:T(8,128)} %scatter_grads.1), calls=%async_computation.13 | async-start | bytes 147456 | tf_op jit(solution)/shard_map/slice | solution.py:480
  (15 other events, 19.0 us)

commit v2 on v1

v2 whole, which is shorter than its diff:
```python
import functools
import numpy as np
import jax, jax.numpy as jnp
from jax import lax
from jax.experimental import pallas as pl
from jax.experimental.pallas import tpu as pltpu
from jax.sharding import PartitionSpec as P

MESH = pl.DeviceIdType.MESH
LW = 384
SROWS = 80

def coords():
    dp = lax.axis_index("dp"); fs = lax.axis_index("fsdp")
    z = dp // 2
    x = (dp % 2) * 2 + fs // 8
    y = (fs % 8) // 2
    c = fs % 2
    return z, x, y, c

def dev(z, x, y, c):
    return (z * 2 + x // 2, (x % 2) * 8 + y * 2 + c)

def perm_matrix():
    m = np.zeros((624, 640), np.float32)
    for d in range(8):
        for u in range(8):
            for j in range(6):
                m[48 * u + 6 * d + j, d * 80 + 6 * u + j] = 1
        for j in range(6):
            m[48 * 8 + 6 * d + j, d * 80 + 72 + j] = 1
        for i in range(24):
            m[432 + 24 * d + i, d * 80 + 48 + i] = 1
    return m

ALL = slice(None)

def ag_chunks():
    return [
        [("g", "zx", (0, 2), (0, 1), (1, 2)), ("g", "xz", (2, 4), (2, 3), (3, 4))],
        [("g", "zx", (4, 6), (4, 5), (5, 6)), ("g", "xz", (6, 8), (6, 7), (7, 8))],
        [("g2", "zx", (0, 96), (0, 48), (48, 96)), ("g2", "xz", (96, 192), (96, 144), (144, 192))],
        [("g", "zx", (8, 9), (8, 9), None)],
    ]


def pack_vec(ln1_g, ln1_b, ln2_g, ln2_b, fc2_b, fc1_b, dec_b, mask):
    cols = [ln1_g[:, None], ln1_b[:, None], ln2_g[:, None], ln2_b[:, None], fc2_b[:, None], fc1_b.reshape(6, 4),
            jnp.pad(dec_b, (0, 2))[:, None], jnp.pad(mask, (0, 2))[:, None]]
    v = jnp.concatenate(cols, axis=1)
    return jnp.pad(v, ((0, 0), (0, 128 - v.shape[1])))


ROWS = 336
HEADS_PAIRS = 6
D = 768
NT = (((1,), (1,)), ((), ()))
TN = (((0,), (0,)), ((), ()))
f32, bf16 = jnp.float32, jnp.bfloat16


def cell_spread():
    m = np.zeros((768, 512), np.float32)
    for d in range(128):
        for j in range(4):
            m[6 * d + j, 4 * d + j] = 1
    return m


def quad_spread():
    m = np.zeros((192, 768), np.float32)
    m[np.arange(768) // 4, np.arange(768)] = 1
    return m


def stats(v):
    mean = jnp.mean(v, axis=-1, keepdims=True)
    center = v - mean
    rstd = lax.rsqrt(jnp.mean(center * center, axis=-1, keepdims=True) + 1e-6)
    return center * rstd, rstd


def gelu_pair(f):
    cdf = 0.5 * (1.0 + lax.erf(f * 0.7071067811865476))
    pdf = 0.3989422804014327 * jnp.exp(-0.5 * f * f)
    return f * cdf, cdf + f * pdf


def k1_kernel(tok, lens, pos, vec6, qkv_s, out_s, fc1_s, fc2_s, dec_s, p_ref, m2_ref, m4_ref,
              g_hbm, g2_hbm, rows_ref, a_ref, qkv_ref, p_out, o_ref, x2_ref, h2_ref, act_ref, dact_ref, e_ref, cells_ref,
              g_ref, g2_ref, sp, s_ref, s1, z_ref, ss1, rs1, loc, ssem, rsem, wsem):
    z, x, y, c = coords()
    zp, zm, zo = (z + 1) % 4, (z + 3) % 4, (z + 2) % 4
    xp, xm, xo = (x + 1) % 4, (x + 3) % 4, (x + 2) % 4
    o = 1 - c
    bar = pltpu.get_barrier_semaphore()
    targets = [dev(zp, x, y, c), dev(zm, x, y, c), dev(z, xp, y, c), dev(z, xm, y, c)]
    group = []
    for dy in range(4):
        for dc in range(2):
            if dy or dc:
                group.append((dy, dc, dev(z, x, (y + dy) % 4, (c + dc) % 2)))
    for t in targets + [g[2] for g in group]:
        pl.semaphore_signal(bar, inc=1, device_id=t, device_id_type=MESH)

    sp[...] = jnp.zeros_like(sp)
    for h in range(2):
        for u in range(3):
            sp[h, 6 * u:6 * u + 6, :] = qkv_s[:, h * 1152 + u * LW:h * 1152 + (u + 1) * LW].astype(f32)
        sp[h, 18:24, :] = out_s[:, h * LW:(h + 1) * LW].astype(f32)
        for u in range(4):
            sp[h, 24 + 6 * u:30 + 6 * u, :] = fc1_s[:, h * 1536 + u * LW:h * 1536 + (u + 1) * LW].astype(f32)
        sp[h, 48:72, :] = fc2_s[:, h * LW:(h + 1) * LW].astype(f32)
        sp[h, 72:78, 0:256] = dec_s[:, h * 256:(h + 1) * 256].astype(f32)
    sp[0, 72:78, 256:384] = vec6[...].astype(f32)
    s_ref[...] = sp[...].astype(bf16)
    pl.semaphore_wait(bar, len(targets) + len(group))

    me = 2 * y + c
    own = pltpu.make_async_copy(s_ref.at[c], s1.at[me], loc)
    own.start()
    firsts = []
    for i, (dy, dc, t) in enumerate(group):
        cp = pltpu.make_async_remote_copy(s_ref.at[(c + dc) % 2], s1.at[me], ss1.at[i], rs1.at[i], device_id=t, device_id_type=MESH)
        cp.start()
        src = 2 * ((y + 4 - dy) % 4) + (c + dc) % 2
        rc = pltpu.make_async_remote_copy(s_ref.at[c], s1.at[src], ss1.at[i], rs1.at[i], device_id=t, device_id_type=MESH)
        firsts.append((cp, rc))

    own.wait()
    for cp, rc in firsts:
        rc.wait_recv()

    def relay(lo, hi):
        flat = s1[...].reshape(640, LW)
        r = jnp.dot(p_ref[lo:hi, :], flat, preferred_element_type=f32)
        return r.astype(bf16)

    def place(p):
        if p == 0: g_ref[c, 0:4, z, x] = relay(0, 192).reshape(4, 48, LW)
        if p == 1: g_ref[c, 4:8, z, x] = relay(192, 384).reshape(4, 48, LW)
        if p == 2: g2_ref[c, z, x] = relay(432, 624)
        if p == 3: g_ref[c, 8, z, x] = relay(384, 432)

    def view(arr, h, part, zs, xs):
        if arr == "g":
            return g_ref.at[h, part[0]:part[1], zs, xs]
        return g2_ref.at[h, zs, xs, part[0]:part[1]]

    sends = []
    def mk(k, i, src, dst, to):
        return pltpu.make_async_remote_copy(src, dst, ssem.at[k, i], rsem.at[k, i], device_id=to, device_id_type=MESH)
    def send(k, i, v, to):
        cp = mk(k, i, v, v, to); cp.start(); sends.append(cp)
    def recv(k, i, v):
        mk(k, i, v, v, dev(z, x, y, o)).wait_recv()

    def steps(k, chunk):
        arr, order, full, fa, fb = chunk
        if order == "zx":
            d1p, d1m, d2p, d2m = targets
            p1, m1, o1, p2, m2, o2, s1_, s2_ = zp, zm, zo, xp, xm, xo, z, x
            V = lambda part, a, b, h=c: view(arr, h, part, a, b)
        else:
            d2p, d2m, d1p, d1m = targets
            p1, m1, o1, p2, m2, o2, s1_, s2_ = xp, xm, xo, zp, zm, zo, x, z
            V = lambda part, a, b, h=c: view(arr, h, part, b, a)
        sib = dev(z, x, y, o)
        def st0():
            send(k, 0, V(full, s1_, s2_), d1p)
            send(k, 1, V(full, s1_, s2_), d1m)
        def st1():
            recv(k, 0, V(full, m1, s2_))
            send(k, 2, V(fa, m1, s2_), d1p)
            recv(k, 1, V(full, p1, s2_))
            if fb is not None: send(k, 3, V(fb, p1, s2_), d1m)
        def st2():
            recv(k, 2, V(fa, o1, s2_))
            if fb is not None: recv(k, 3, V(fb, o1, s2_))
            send(k, 4, V(full, ALL, s2_), d2p)
            send(k, 5, V(full, ALL, s2_), d2m)
            send(k, 8, V(full, ALL, s2_), sib)
        def st3():
            recv(k, 4, V(full, ALL, m2))
            send(k, 6, V(fa, ALL, m2), d2p)
            send(k, 9, V(full, ALL, m2), sib)
            recv(k, 5, V(full, ALL, p2))
            if fb is not None: send(k, 7, V(fb, ALL, p2), d2m)
            send(k, 10, V(full, ALL, p2), sib)
        def st4():
            recv(k, 6, V(fa, ALL, o2))
            if fb is not None: recv(k, 7, V(fb, ALL, o2))
            send(k, 11, V(full, ALL, o2), sib)
        def st5():
            recv(k, 8, V(full, ALL, s2_, o))
            recv(k, 9, V(full, ALL, m2, o))
            recv(k, 10, V(full, ALL, p2, o))
            recv(k, 11, V(full, ALL, o2, o))
        return [st0, st1, st2, st3, st4, st5]

    outs = []
    def to_hbm(p):
        if p == 2: cp = pltpu.make_async_copy(g2_ref, g2_hbm, wsem.at[p])
        else:
            u0, u1 = ((0, 4), (4, 8), None, (8, 9))[p]
            cp = pltpu.make_async_copy(g_ref.at[:, u0:u1], g_hbm.at[:, u0:u1], wsem.at[p])
        cp.start(); outs.append(cp)

    def blocks(body, n=7):
        def step(i, _):
            body(pl.ds(pl.multiple_of(i * 48, 48), 48)); return 0
        lax.fori_loop(0, n, step, 0)

    def w(h, u):
        return g_ref[h, u].reshape(768, LW)

    def rows_of():
        v = jnp.concatenate([g_ref[0, 8, zz, xx, :, 256:384] for zz in range(4) for xx in range(4)], axis=0)
        vt = v.astype(f32).T
        rows_ref[0:5, 0:768] = vt[0:5]
        md = lax.dot_general(v, m2_ref[...], TN, preferred_element_type=f32)
        rows_ref[6:8, 0:512] = md[9:11]
        lane = lax.broadcasted_iota(jnp.int32, (8, 768), 1) % 4
        row = lax.broadcasted_iota(jnp.int32, (8, 768), 0)
        for s in range(4):
            q = lax.dot_general(v[192 * s:192 * s + 192], m4_ref[...], TN, preferred_element_type=f32)
            q = jnp.where(row == lane, q[5:13], 0.0)
            rows_ref[5:6, 768 * s:768 * s + 768] = jnp.sum(q, axis=0, keepdims=True)

    def ln1():
        def body(r):
            n, _ = stats(tok[r, :].astype(f32))
            a_ref[r, :] = (n * rows_ref[0:1, 0:768] + rows_ref[1:2, 0:768]).astype(bf16)
        blocks(body)

    def qkv():
        for h in range(2):
            wt = jnp.concatenate([w(h, u) for u in range(3)], axis=1)
            qkv_ref[:, h * 1152:(h + 1) * 1152] = jnp.dot(a_ref[...], wt, preferred_element_type=f32).astype(bf16)

    ends0 = lens[0] + 2
    ends1 = ends0 + lens[1] + 2
    def seg(shape, axis):
        r = lax.broadcasted_iota(jnp.int32, shape, axis)
        return (r >= ends0).astype(jnp.int32) + (r >= ends1).astype(jnp.int32)

    def attention():
        low = lax.broadcasted_iota(jnp.int32, (1, 128), 1) < 64
        same = seg((ROWS, 1), 0) == seg((1, ROWS), 1)
        bias = jnp.where(same, 0.0, -1e30)
        def pair(i, _):
            def cols(base):
                return qkv_ref[:, pl.ds(pl.multiple_of(base + i * 128, 128), 128)]
            q, k, v = cols(0), cols(768), cols(1536)
            outs_ = []
            for t in range(2):
                keep = low if t == 0 else jnp.logical_not(low)
                s = lax.dot_general(jnp.where(keep, q, jnp.zeros_like(q)), k, NT, preferred_element_type=f32)
                s = jnp.where(same, s * 0.125, -1e30)
                m = jnp.max(s, axis=-1, keepdims=True)
                ex = jnp.exp(s - m)
                pr = (ex / jnp.sum(ex, axis=-1, keepdims=True)).astype(bf16)
                p_out[2 * i + t] = pr
                outs_.append(jnp.dot(pr, v, preferred_element_type=f32))
            o_ref[:, pl.ds(pl.multiple_of(i * 128, 128), 128)] = jnp.where(low, outs_[0], outs_[1]).astype(bf16)
            return 0
        lax.fori_loop(0, HEADS_PAIRS, pair, 0)

    def out_proj():
        for h in range(2):
            cs = slice(h * LW, (h + 1) * LW)
            x2_ref[:, cs] = tok[0:ROWS, cs].astype(f32) + jnp.dot(o_ref[...], w(h, 3), preferred_element_type=f32)
        def body(r):
            n, _ = stats(x2_ref[r, :])
            h2_ref[r, :] = (n * rows_ref[2:3, 0:768] + rows_ref[3:4, 0:768]).astype(bf16)
        blocks(body)

    def fc1():
        for h in range(2):
            def unit(u, _):
                cs = pl.ds(pl.multiple_of(h * 1536 + u * LW, LW), LW)
                f = jnp.dot(h2_ref[...], w(h, 4 + u), preferred_element_type=f32) + rows_ref[5:6, cs]
                g, dg = gelu_pair(f)
                act_ref[:, cs] = g.astype(bf16)
                dact_ref[:, cs] = dg.astype(bf16)
                return 0
            lax.fori_loop(0, 4, unit, 0)

    def fc2():
        for h in range(2):
            cs = slice(h * LW, (h + 1) * LW)
            t = jnp.dot(act_ref[...], g2_ref[h].reshape(3072, LW), preferred_element_type=f32)
            e_ref[:, cs] = (x2_ref[:, cs] + t + rows_ref[4:5, cs]).astype(bf16)

    def dec():
        for h in range(2):
            cs = slice(h * 256, (h + 1) * 256)
            t = jnp.dot(e_ref[...], g_ref[h, 8, :, :, :, 0:256].reshape(768, 256), preferred_element_type=f32)
            z_ref[:, cs] = (t + rows_ref[6:7, cs]).astype(bf16)
        z_ref[:, 512:640] = jnp.ones((ROWS, 128), bf16)
        p_ = pos[0:1, 0:ROWS]
        target = jnp.where(p_ >= 0, seg((1, ROWS), 1) * 1024 + p_, -1)
        def block(i, _):
            slot = i // 4
            first = i * 256
            cell = first + lax.broadcasted_iota(jnp.int32, (256, 1), 0)
            fill = (cell == target).astype(f32).astype(bf16)
            r = jnp.dot(fill, z_ref[...], preferred_element_type=f32)
            limit = 4 * jnp.where(slot == 0, lens[0], lens[1])
            valid = (cell - slot * 1024 < limit).astype(f32)
            empty = jnp.where(valid > 0.0, 1.0 - r[:, 512:640], 0.0)
            for t in range(4):
                cs = slice(128 * t, 128 * t + 128)
                val = r[:, cs] + empty * rows_ref[7:8, cs]
                cells_ref[pl.ds(4 * (i % 4), 4), slot, :, cs] = val.astype(bf16).reshape(4, 64, 128)
            return 0
        lax.fori_loop(0, 8, block, 0)

    after = AFTER(dict(rows_of=rows_of, ln1=ln1, qkv=qkv, attention=attention, out_proj=out_proj, fc1=fc1, fc2=fc2, dec=dec))
    order = PIECE_ORDER
    pieces = [None] * 4
    k = 0
    for p, cl in enumerate(ag_chunks()):
        lst = []
        for ch in cl:
            lst.append(steps(k, ch)); k += 1
        pieces[p] = lst
    for t in range(len(pieces) + 5):
        for pos_, p in enumerate(order):
            s = t - pos_
            if s == 0: place(p)
            if 0 <= s < 6:
                for ch in pieces[p]: ch[s]()
            if s == 5: to_hbm(p)
        for fn in after.get(t, []): fn()
    for fn in after.get("end", []): fn()
    for cp, rc in firsts: cp.wait_send()
    for cp in sends: cp.wait_send()
    for cp in outs: cp.wait()

PIECE_ORDER = [3, 0, 1, 2]

def AFTER(f):
    return {"end": [f[n] for n in ("rows_of", "ln1", "qkv", "attention", "out_proj", "fc1", "fc2", "dec")]}

def k1_call(tok, lens, pos, vec6, qkv_s, out_s, fc1_s, fc2_s, dec_s):
    nk = sum(len(c) for c in ag_chunks())
    S = jax.ShapeDtypeStruct
    vm = pl.BlockSpec(memory_space=pltpu.VMEM)
    anyspec = pl.BlockSpec(memory_space=pl.ANY)
    V = pltpu.VMEM
    outs = (
        S((2, 9, 4, 4, 48, LW), bf16), S((2, 4, 4, 192, LW), bf16), S((8, 3072), f32), S((ROWS, 768), bf16),
        S((ROWS, 2304), bf16), S((12, ROWS, ROWS), bf16), S((ROWS, 768), bf16), S((ROWS, 768), f32),
        S((ROWS, 768), bf16), S((ROWS, 3072), bf16), S((ROWS, 3072), bf16), S((ROWS, 768), bf16), S((16, 2, 64, 512), bf16),
    )
    return pl.pallas_call(
        k1_kernel,
        out_shape=outs,
        in_specs=[vm, pl.BlockSpec(memory_space=pltpu.SMEM)] + [vm] * 10,
        out_specs=[anyspec, anyspec] + [vm] * 11,
        scratch_shapes=[
            V((2, 9, 4, 4, 48, LW), bf16), V((2, 4, 4, 192, LW), bf16),
            V((2, SROWS, LW), f32), V((2, SROWS, LW), bf16), V((8, SROWS, LW), bf16), V((ROWS, 640), bf16),
            pltpu.SemaphoreType.DMA((7,)), pltpu.SemaphoreType.DMA((7,)), pltpu.SemaphoreType.DMA(()),
            pltpu.SemaphoreType.DMA((nk, 12)), pltpu.SemaphoreType.DMA((nk, 12)), pltpu.SemaphoreType.DMA((4,)),
        ],
        compiler_params=pltpu.CompilerParams(collective_id=0, has_side_effects=True, vmem_limit_bytes=60 * 2**20),
        cost_estimate=pl.CostEstimate(flops=6 * 10**9, bytes_accessed=5 * 10**7, transcendentals=0),
        name="forward",
    )(tok, lens, pos, vec6, qkv_s, out_s, fc1_s, fc2_s, dec_s,
      jnp.asarray(perm_matrix(), bf16), jnp.asarray(cell_spread(), bf16), jnp.asarray(quad_spread(), bf16))


def k2_kernel(lens, g_hbm, g2_hbm, rows_ref, tok, a_ref, qkv_ref, p_hbm, o_ref, x2_ref, h2_ref, act_ref, dact_ref, e_ref,
              pos, dc_ref, pt_ref, m2_ref, m4_ref,
              tg_ref, oq_ref, oo_ref, of1_ref, of2_ref, od_ref, ov_ref,
              wd, wa, wb, sta, sta2, stc, sg, sg2, acc, acc2, xa, xa2, xb, xb2,
              dz, dx, dh, dm, df, dqkv, vsum, pb, db, fs, f1, fo, ssem, rsem, ss1, rs1, loc, wsem, psem, tsem, dsem):
    z, x, y, c = coords()
    zp, zm, zo = (z + 1) % 4, (z + 3) % 4, (z + 2) % 4
    xp, xm, xo = (x + 1) % 4, (x + 3) % 4, (x + 2) % 4
    o = 1 - c
    bar = pltpu.get_barrier_semaphore()
    targets = [dev(zp, x, y, c), dev(zm, x, y, c), dev(z, xp, y, c), dev(z, xm, y, c)]
    sib = dev(z, x, y, o)
    group = []
    for dy in range(4):
        for dc in range(2):
            if dy or dc:
                group.append((dy, dc, dev(z, x, (y + dy) % 4, (c + dc) % 2)))
    for t in targets + [g[2] for g in group]:
        pl.semaphore_signal(bar, inc=1, device_id=t, device_id_type=MESH)
    ld_d = pltpu.make_async_copy(g_hbm.at[:, 8], wd, wsem.at[0])
    ld_a = pltpu.make_async_copy(g2_hbm, wa, wsem.at[1])
    ld_b = pltpu.make_async_copy(g_hbm.at[:, 4:8], wb, wsem.at[2])
    ld_c = pltpu.make_async_copy(g_hbm.at[:, 0:4], wb, wsem.at[3])
    for l in (ld_d, ld_a, ld_b): l.start()
    pl.semaphore_wait(bar, len(targets) + len(group))

    sends = {}
    def send(k, i, src, dst, to):
        cp = pltpu.make_async_remote_copy(src, dst, ssem.at[k, i], rsem.at[k, i], device_id=to, device_id_type=MESH)
        cp.start(); sends[k, i] = cp
    def recv(k, i, v):
        pltpu.make_async_remote_copy(v, v, ssem.at[k, i], rsem.at[k, i], device_id=sib, device_id_type=MESH).wait_recv()

    def steps(k, piece, chunk):
        arr, order, full, fa, fb = chunk
        zx = order == "zx"
        if zx:
            d1p, d1m, d2p, d2m = targets
            p1, m1, o1, p2, m2, o2, s1_, s2_ = zp, zm, zo, xp, xm, xo, z, x
        else:
            d2p, d2m, d1p, d1m = targets
            p1, m1, o1, p2, m2, o2, s1_, s2_ = xp, xm, xo, zp, zm, zo, x, z
        def idx(part, a, b):
            zs, xs = (a, b) if zx else (b, a)
            r = pl.ds(part[0], part[1] - part[0])
            return (r, zs, xs) if arr == "g" else (zs, xs, r)
        A = acc if arr == "g" else acc2
        SG = sg if arr == "g" else sg2
        def stage(part):
            if piece == 2: return sta2.at[:, :, pl.ds(part[0], part[1] - part[0])]
            if piece == 3: return stc
            u = 4 * piece
            return sta.at[pl.ds(part[0] - u, part[1] - part[0])]
        def xav(way, part):
            r = slice(part[0], part[1])
            return xa.at[way, r] if arr == "g" else xa2.at[way, :, r]
        def xbv(way, part):
            r = slice(part[0], part[1])
            return xb.at[way, r] if arr == "g" else xb2.at[way, r]
        def add(part, a, b, *recvd):
            i = idx(part, a, b)
            t = A[i].astype(f32)
            for r in recvd: t = t + r[...].astype(f32)
            A[i] = t.astype(bf16)
        def st0():
            send(k, 8, stage(full), SG.at[idx(full, ALL, ALL)], sib)
        def st1():
            recv(k, 8, SG.at[idx(full, ALL, ALL)])
            def one(j, _):
                i = idx(full, j, ALL)
                A[i] = (A[i].astype(f32) + SG[i].astype(f32)).astype(bf16)
                return 0
            lax.fori_loop(0, 4, one, 0)
            send(k, 0, A.at[idx(fa, ALL, o2)], xav(0, fa), d2p)
            if fb is not None: send(k, 1, A.at[idx(fb, ALL, o2)], xav(0, fb), d2m)
        def st2():
            recv(k, 0, xav(0, fa)); add(fa, ALL, p2, xav(0, fa))
            send(k, 2, A.at[idx(full, ALL, p2)], xav(1, full), d2p)
            if fb is not None:
                recv(k, 1, xav(0, fb)); add(fb, ALL, m2, xav(0, fb))
            send(k, 3, A.at[idx(full, ALL, m2)], xav(2, full), d2m)
        def st3():
            recv(k, 2, xav(1, full)); recv(k, 3, xav(2, full))
            add(full, ALL, s2_, xav(1, full), xav(2, full))
            send(k, 4, A.at[idx(fa, o1, s2_)], xbv(0, fa), d1p)
            if fb is not None: send(k, 5, A.at[idx(fb, o1, s2_)], xbv(0, fb), d1m)
        def st4():
            recv(k, 4, xbv(0, fa)); add(fa, p1, s2_, xbv(0, fa))
            send(k, 6, A.at[idx(full, p1, s2_)], xbv(1, full), d1p)
            if fb is not None:
                recv(k, 5, xbv(0, fb)); add(fb, m1, s2_, xbv(0, fb))
            send(k, 7, A.at[idx(full, m1, s2_)], xbv(2, full), d1m)
        def st5():
            recv(k, 6, xbv(1, full)); recv(k, 7, xbv(2, full))
            add(full, s1_, s2_, xbv(1, full), xbv(2, full))
        return [st0, st1, st2, st3, st4, st5]

    table = {}
    keys = {}
    k = 0
    for p, cl in enumerate(ag_chunks()):
        lst = []
        for ch in cl:
            lst.append(steps(k, p, ch)); keys.setdefault(p, []).append(k); k += 1
        table[p] = lst
    def st(p, s):
        for ch in table[p]: ch[s]()

    def blocks(body, n=7):
        def step(i, _):
            body(pl.ds(pl.multiple_of(i * 48, 48), 48)); return 0
        lax.fori_loop(0, n, step, 0)
    ends0 = lens[0] + 2
    ends1 = ends0 + lens[1] + 2
    def col(base, width, unit):
        return pl.ds(pl.multiple_of(base, unit), width)

    def start_grads():
        p_ = jnp.broadcast_to(pos[0:1, 0:384], (8, 384)).astype(f32)
        r_ = lax.broadcasted_iota(jnp.int32, (8, 384), 1)
        seg = ((r_ >= ends0).astype(jnp.int32) + (r_ >= ends1).astype(jnp.int32)).astype(f32)
        target = jnp.where(p_ >= 0.0, seg * 1024.0 + p_, -1.0).T[0:ROWS, 0:1].astype(jnp.int32)
        dx[:, 0:512] = jnp.zeros((ROWS, 512), f32)
        vsum[...] = jnp.zeros_like(vsum)
        def load(i):
            return pltpu.make_async_copy(dc_ref.at[pl.ds(4 * (i % 4), 4), i // 4], db.at[i % 2], dsem.at[i % 2])
        load(0).start()
        def block(i, _):
            load(i).wait()
            pl.when(i < 7)(lambda: load(i + 1).start())
            slot = i // 4
            cell = i * 256 + lax.broadcasted_iota(jnp.int32, (1, 256), 1)
            hit = (target == cell).astype(f32)
            dcb = db[i % 2].reshape(256, 512)
            dx[:, 0:512] += jnp.dot(hit.astype(bf16), dcb, preferred_element_type=f32)
            limit = 4 * jnp.where(slot == 0, lens[0], lens[1])
            empty = jnp.where(cell - slot * 1024 < limit, 1.0 - jnp.sum(hit, axis=0, keepdims=True), 0.0)
            em = jnp.dot(jnp.broadcast_to(empty, (16, 256)).astype(bf16), dcb, preferred_element_type=f32)
            vsum[10:11, 0:512] += em[0:1]
            return 0
        lax.fori_loop(0, 8, block, 0)
        dz[...] = dx[:, 0:512].astype(bf16)
        vsum[9:10, 0:512] = jnp.sum(dz[...].astype(f32), axis=0, keepdims=True)

    def wdec(h):
        return wd[h, :, :, :, 0:256].reshape(768, 256)
    def dec_back():
        for n in range(2):
            rs = slice(n * 384, (n + 1) * 384)
            t = lax.dot_general(dz[:, 0:256], wdec(0)[rs], NT, preferred_element_type=f32)
            t = t + lax.dot_general(dz[:, 256:512], wdec(1)[rs], NT, preferred_element_type=f32)
            dx[:, rs] = t
            dm[:, rs] = t.astype(bf16)
        vsum[4:5, 0:768] = jnp.sum(dm[...].astype(f32), axis=0, keepdims=True)

    def grad_fc2(h, dst):
        def part(i, _):
            t = lax.dot_general(act_ref[:, col(i * 768, 768, 768)], dm[:, col(h * LW, LW, LW)], TN, preferred_element_type=f32)
            dst[i] = t.astype(bf16).reshape(4, 192, LW)
            return 0
        lax.fori_loop(0, 4, part, 0)

    def fc2_back():
        def part(i, _):
            cs = col(i * 768, 768, 768)
            t = lax.dot_general(dm[:, 0:LW], wa[0, i].reshape(768, LW), NT, preferred_element_type=f32)
            t = t + lax.dot_general(dm[:, LW:768], wa[1, i].reshape(768, LW), NT, preferred_element_type=f32)
            t = (t * dact_ref[:, cs].astype(f32)).astype(bf16)
            df[:, cs] = t
            vsum[5:6, cs] = jnp.sum(t.astype(f32), axis=0, keepdims=True)
            return 0
        lax.fori_loop(0, 4, part, 0)

    def wunit(h, u):
        return wb[h, u].reshape(768, LW)
    def fc1_back():
        for h in range(2):
            wt = lambda r: jnp.concatenate([wunit(h, u)[r] for u in range(4)], axis=1)
            for n in range(2):
                rs = slice(n * 384, (n + 1) * 384)
                t = lax.dot_general(df[:, h * 1536:(h + 1) * 1536], wt(rs), NT, preferred_element_type=f32)
                dh[:, rs] = t if h == 0 else dh[:, rs] + t

    def grad_fc1(h, dst, base):
        def part(u, _):
            t = lax.dot_general(h2_ref[...], df[:, col(h * 1536 + u * LW, LW, LW)], TN, preferred_element_type=f32)
            dst[base + u] = t.astype(bf16).reshape(4, 4, 48, LW)
            return 0
        lax.fori_loop(0, 4, part, 0)

    def norm_back(src, gain_row, into, out_lo, base):
        gain = rows_ref[gain_row:gain_row + 1, 0:768]
        def body(r):
            n, rstd = stats(src[r, :].astype(f32))
            d = dh[r, :]
            vsum[base:base + 1, 0:768] += jnp.sum(d * n, axis=0, keepdims=True)
            vsum[base + 1:base + 2, 0:768] += jnp.sum(d, axis=0, keepdims=True)
            dn = d * gain
            t = rstd * (dn - jnp.mean(dn, axis=-1, keepdims=True) - n * jnp.mean(dn * n, axis=-1, keepdims=True))
            t = dx[r, :] + t
            into[r, :] = t
            if out_lo is not None: out_lo[r, :] = t.astype(bf16)
        blocks(body)

    def out_back():
        t = lax.dot_general(dm[:, 0:LW], wunit(0, 3), NT, preferred_element_type=f32)
        t = t + lax.dot_general(dm[:, LW:768], wunit(1, 3), NT, preferred_element_type=f32)
        df[:, 0:768] = t.astype(bf16)

    def load_p(i):
        return pltpu.make_async_copy(p_hbm.at[pl.ds(2 * i, 2)], pb.at[i % 2], psem.at[i % 2])

    def attn_back(lo, hi):
        low = lax.broadcasted_iota(jnp.int32, (1, 128), 1) < 64
        def pair(i, _):
            load_p(i).wait()
            pl.when(i + 1 < HEADS_PAIRS)(lambda: load_p(i + 1).start())
            def cols(ref, base):
                return ref[:, col(base + i * 128, 128, 128)]
            q, kk, v, do = cols(qkv_ref, 0), cols(qkv_ref, 768), cols(qkv_ref, 1536), cols(df, 0)
            r = []
            for t in range(2):
                keep = low if t == 0 else jnp.logical_not(low)
                pr = pb[i % 2, t]
                dp = lax.dot_general(jnp.where(keep, do, jnp.zeros_like(do)), v, NT, preferred_element_type=f32)
                p32 = pr.astype(f32)
                ds = (p32 * (dp - jnp.sum(dp * p32, axis=-1, keepdims=True))).astype(bf16)
                dv = lax.dot_general(pr, do, TN, preferred_element_type=f32)
                dq = jnp.dot(ds, kk, preferred_element_type=f32)
                dk = lax.dot_general(ds, q, TN, preferred_element_type=f32)
                r.append((dq, dk, dv))
            dqkv[:, col(i * 128, 128, 128)] = (0.125 * jnp.where(low, r[0][0], r[1][0])).astype(bf16)
            dqkv[:, col(768 + i * 128, 128, 128)] = (0.125 * jnp.where(low, r[0][1], r[1][1])).astype(bf16)
            dqkv[:, col(1536 + i * 128, 128, 128)] = jnp.where(low, r[0][2], r[1][2]).astype(bf16)
            return 0
        lax.fori_loop(lo, hi, pair, 0)

    def qkv_back():
        for h in range(2):
            wt = lambda r: jnp.concatenate([wunit(h, u)[r] for u in range(3)], axis=1)
            for n in range(2):
                rs = slice(n * 384, (n + 1) * 384)
                t = lax.dot_general(dqkv[:, h * 1152:(h + 1) * 1152], wt(rs), NT, preferred_element_type=f32)
                dh[:, rs] = t if h == 0 else dh[:, rs] + t

    def grad_qkv(h, dst):
        def part(u, _):
            t = lax.dot_general(a_ref[...], dqkv[:, col(h * 1152 + u * LW, LW, LW)], TN, preferred_element_type=f32)
            dst[u] = t.astype(bf16).reshape(4, 4, 48, LW)
            return 0
        lax.fori_loop(0, 3, part, 0)
    def grad_out(h, dst):
        t = lax.dot_general(o_ref[...], dm[:, col(h * LW, LW, LW)], TN, preferred_element_type=f32)
        dst[3] = t.astype(bf16).reshape(4, 4, 48, LW)

    def vec_cols():
        rt = jnp.concatenate([vsum[0:8, 0:768], jnp.zeros((120, 768), f32)], axis=0)
        srow = lax.broadcasted_iota(jnp.int32, (128, 768), 0)
        rt = jnp.where(srow < 5, rt, 0.0)
        v = rt.T
        r2 = jnp.concatenate([vsum[0:16, 0:512], jnp.zeros((112, 512), f32)], axis=0)
        srow2 = lax.broadcasted_iota(jnp.int32, (128, 512), 0)
        r2 = jnp.where((srow2 == 9) | (srow2 == 10), r2, 0.0).astype(bf16)
        v = v + lax.dot_general(m2_ref[...], r2, NT, preferred_element_type=f32)
        lane = lax.broadcasted_iota(jnp.int32, (128, 768), 1) % 4
        parts = []
        for s in range(4):
            wrow = jnp.broadcast_to(vsum[5:6, 768 * s:768 * s + 768], (128, 768))
            wt = jnp.where(srow - 5 == lane, wrow, 0.0).astype(bf16)
            parts.append(lax.dot_general(m4_ref[...], wt, NT, preferred_element_type=f32))
        return (v + jnp.concatenate(parts, axis=0)).astype(bf16)

    def grad_dec(h, dst_store):
        t = lax.dot_general(e_ref[...], dz[:, col(h * 256, 256, 256)], TN, preferred_element_type=f32)
        dst_store(t.astype(bf16).reshape(4, 4, 48, 256), slice(0, 256))

    def acc8(v, cs): acc[8, :, :, :, cs] = v
    def stc8(v, cs): stc[0, :, :, :, cs] = v

    start_grads()
    ld_d.wait()
    dec_back()
    grad_fc2(o, sta2); st(2, 0)
    grad_fc2(c, acc2)
    ld_a.wait()
    fc2_back()
    st(2, 1)
    ld_b.wait()
    fc1_back()
    ld_c.start()
    load_p(0).start()
    grad_fc1(o, sta, 0); st(1, 0)
    st(2, 2)
    grad_fc1(c, acc, 4)
    norm_back(x2_ref, 2, dx, dm, 2)
    st(2, 3); st(1, 1)
    ld_c.wait()
    for kk in keys[1]: sends[kk, 8].wait_send(); del sends[kk, 8]
    grad_out(o, sta); grad_out(c, acc)
    out_back()
    st(2, 4); st(1, 2)
    attn_back(0, 3)
    st(2, 5); st(1, 3)
    attn_back(3, 6)
    st(1, 4)
    grad_qkv(o, sta)
    st(0, 0)
    grad_qkv(c, acc)
    st(1, 5)
    qkv_back()
    norm_back(tok, 0, dx, None, 0)
    dh[0:512 - ROWS, :] = jnp.zeros((512 - ROWS, 768), f32)
    tgs = [pltpu.make_async_copy(dx, tg_ref.at[0:ROWS], tsem.at[0]), pltpu.make_async_copy(dh.at[0:512 - ROWS], tg_ref.at[ROWS:512], tsem.at[1])]
    for t in tgs: t.start()
    st(0, 1)
    v = vec_cols().reshape(4, 4, 48, 128)
    zero = jnp.zeros_like(v)
    acc8(jnp.where(c == 0, v, zero), slice(256, 384)); stc8(jnp.where(c == 0, zero, v), slice(256, 384))
    grad_dec(o, stc8)
    st(3, 0)
    grad_dec(c, acc8)
    st(0, 2); st(3, 1); st(0, 3); st(3, 2); st(0, 4); st(3, 3); st(0, 5); st(3, 4); st(3, 5)

    blk = jnp.concatenate([acc[:, z, x].reshape(432, LW), acc2[z, x]], axis=0)
    fs[...] = jnp.dot(pt_ref[...], blk, preferred_element_type=f32).astype(bf16).reshape(8, SROWS, LW)
    me = 2 * y + c
    own = pltpu.make_async_copy(fs.at[me], f1.at[me], loc)
    own.start()
    lasts = []
    for i, (dy, dc, t) in enumerate(group):
        dst = 2 * ((y + dy) % 4) + (c + dc) % 2
        cp = pltpu.make_async_remote_copy(fs.at[dst], f1.at[me], ss1.at[i], rs1.at[i], device_id=t, device_id_type=MESH)
        cp.start()
        src = 2 * ((y + 4 - dy) % 4) + (c + dc) % 2
        rc = pltpu.make_async_remote_copy(fs.at[me], f1.at[src], ss1.at[i], rs1.at[i], device_id=t, device_id_type=MESH)
        lasts.append((cp, rc))
    own.wait()
    for cp, rc in lasts: rc.wait_recv()
    for h in range(2):
        t = f1[h].astype(f32)
        for yy in range(1, 4): t = t + f1[2 * yy + h].astype(f32)
        fo[h] = t
    for h in range(2):
        for u in range(3):
            oq_ref[:, h * 1152 + u * LW:h * 1152 + (u + 1) * LW] = fo[h, 6 * u:6 * u + 6, :]
        oo_ref[:, h * LW:(h + 1) * LW] = fo[h, 18:24, :]
        for u in range(4):
            of1_ref[:, h * 1536 + u * LW:h * 1536 + (u + 1) * LW] = fo[h, 24 + 6 * u:30 + 6 * u, :]
        of2_ref[:, h * LW:(h + 1) * LW] = fo[h, 48:72, :]
        od_ref[:, h * 256:(h + 1) * 256] = fo[h, 72:78, 0:256]
    ov_ref[...] = fo[0, 72:78, 256:384]
    for t in tgs: t.wait()
    for cp, rc in lasts: cp.wait_send()
    for cp in sends.values(): cp.wait_send()


def k2_call(lens, g, g2, rows, tok, a, qkv, pr, o, x2, h2, act, dact, e, pos, dc):
    nk = sum(len(c) for c in ag_chunks())
    S = jax.ShapeDtypeStruct
    vm = pl.BlockSpec(memory_space=pltpu.VMEM)
    anyspec = pl.BlockSpec(memory_space=pl.ANY)
    V, DMA = pltpu.VMEM, pltpu.SemaphoreType.DMA
    outs = (S((512, 768), f32), S((6, 2304), f32), S((6, 768), f32), S((6, 3072), f32), S((24, 768), f32), S((6, 512), f32), S((6, 128), f32))
    return pl.pallas_call(
        k2_kernel,
        out_shape=outs,
        in_specs=[pl.BlockSpec(memory_space=pltpu.SMEM), anyspec, anyspec] + [vm] * 4 + [anyspec] + [vm] * 7 + [anyspec] + [vm] * 3,
        out_specs=[anyspec] + [vm] * 6,
        scratch_shapes=[
            V((2, 4, 4, 48, LW), bf16), V((2, 4, 4, 192, LW), bf16), V((2, 4, 4, 4, 48, LW), bf16),
            V((4, 4, 4, 48, LW), bf16), V((4, 4, 192, LW), bf16), V((1, 4, 4, 48, LW), bf16),
            V((9, 4, 4, 48, LW), bf16), V((4, 4, 192, LW), bf16),
            V((9, 4, 4, 48, LW), bf16), V((4, 4, 192, LW), bf16),
            V((3, 9, 4, 48, LW), bf16), V((3, 4, 192, LW), bf16),
            V((3, 9, 48, LW), bf16), V((3, 192, LW), bf16),
            V((ROWS, 512), bf16), V((ROWS, 768), f32), V((ROWS, 768), f32), V((ROWS, 768), bf16), V((ROWS, 3072), bf16),
            V((ROWS, 2304), bf16), V((16, 3072), f32), V((2, 2, ROWS, ROWS), bf16), V((2, 4, 64, 512), bf16),
            V((8, SROWS, LW), bf16), V((8, SROWS, LW), bf16), V((2, SROWS, LW), f32),
            DMA((nk, 9)), DMA((nk, 9)), DMA((7,)), DMA((7,)), DMA(()), DMA((4,)), DMA((2,)), DMA((2,)), DMA((2,)),
        ],
        compiler_params=pltpu.CompilerParams(collective_id=1, has_side_effects=True, vmem_limit_bytes=60 * 2**20),
        cost_estimate=pl.CostEstimate(flops=12 * 10**9, bytes_accessed=5 * 10**7, transcendentals=0),
        name="backward",
    )(lens, g, g2, rows, tok, a, qkv, pr, o, x2, h2, act, dact, e, pos, dc,
      jnp.asarray(perm_matrix().T, bf16), jnp.asarray(cell_spread(), bf16), jnp.asarray(quad_spread(), bf16))


def body(tokens, chip_lengths, chip_ids, positions, ln1_gain, ln1_bias, qkv_weight, out_weight, ln2_gain, ln2_bias, fc1_weight,
         fc1_bias, fc2_weight, fc2_bias, dec_weight, dec_bias, mask_token, grid_cotangent):
    n = lax.axis_size("fsdp")
    tags = jnp.broadcast_to(chip_ids.astype(bf16)[None], (n, 2))
    owner = lax.all_to_all(tags, "fsdp", split_axis=0, concat_axis=0).reshape(32).astype(jnp.int32)
    placement = (jnp.arange(32, dtype=jnp.int32)[:, None] == owner[None, :]).astype(bf16)
    back = lax.dot_general(placement, grid_cotangent.reshape(32, -1), TN, preferred_element_type=f32).astype(bf16)
    cots = lax.all_to_all(back.reshape(16, 2, 64, 512), "fsdp", split_axis=0, concat_axis=0)
    vec = pack_vec(ln1_gain, ln1_bias, ln2_gain, ln2_bias, fc2_bias, fc1_bias, dec_bias, mask_token)
    pos = positions.reshape(1, 512)
    *saved, cells = k1_call(tokens, chip_lengths, pos, vec, qkv_weight, out_weight, fc1_weight, fc2_weight, dec_weight)
    g, g2, rows, *acts = saved
    arrived = lax.all_to_all(cells, "fsdp", split_axis=0, concat_axis=0)
    tg, dq, do, df1, df2, dd, dv = k2_call(chip_lengths, g, g2, rows, tokens, *acts, pos, cots)
    grid = jnp.dot(placement, arrived.reshape(32, -1), preferred_element_type=f32).astype(bf16).reshape(32, 64, 512)
    return (grid, tg, dv[:, 0], dv[:, 1], dq, do, dv[:, 2], dv[:, 3], df1, dv[:, 5:9].reshape(24), df2, dv[:, 4], dd,
            dv[:4, 9], dv[:4, 10])


def solution(mesh):
    both = ("dp", "fsdp")
    r1, r2, grid = P(both), P(both, None), P("dp", "fsdp", None)
    weights = (r1, r1, r2, r2, r1, r1, r2, r1, r2, r1, r2, r1, r1)
    return jax.shard_map(body, mesh=mesh, in_specs=(r2, r1, r1, r1) + weights + (grid,), out_specs=(grid, r2) + weights,
                         check_vma=False)
```

time: 454 us -> 293 us (0.65); the launches traced: 446 us -> 292 us
  local copies, waits for them, and re-layouts: 135 us -> 27 us
  matrix products: 74.3 us -> 3.04 us
  Pallas kernels: 147 us -> 199 us
  other arithmetic: 27.4 us -> 0.69 us
    dot_general x23 -> x2, matrix products: 69.6 us -> 3.04 us  [the longest x1 2.35 us: body(): lax.dot_general(placement, grid_cotangent.reshape(32, -1), TN, preferred_...]
    reshape x23 -> x1, local copies, waits for them, and re-layouts: 53.7 us -> 0.59 us  [body(): dv[:, 5:9].reshape(24)]
    pallas_call x2, Pallas kernels: 147 us -> 199 us  [the longest x1 103 us: k2_call(): pl.pallas_call(k2_kernel, out_shape=outs, in_specs=[pl.BlockSpec(memory_s...]
    slice x24 -> x3, local copies, waits for them, and re-layouts: 21.4 us -> 3.85 us  [the longest x1 1.62 us: body(): dv[:, 4]]
    convert_element_type x7 -> x1, local copies, waits for them, and re-layouts: 12 us -> 0.08 us  [body(): lax.all_to_all(tags, 'fsdp', split_axis=0, concat_axis=0).reshape(32)]
    concatenate x2 -> x0, other arithmetic: 10.2 us -> none  [the longest x1 9 us: pack_grads(): jnp.concatenate([u(qkv), u(out), u(fc1), dv], axis=1)]
    dot_general x2 -> x0, local copies, waits for them, and re-layouts: 8.18 us -> none  [body(): jnp.dot(empty_cells, flat_grad, preferred_element_type=jnp.float32)]
    transpose x3 -> x0, local copies, waits for them, and re-layouts: 6.17 us -> none  [the longest x1 6.13 us: u(): return w.reshape(768, 2, n, LW).transpose(1, 2, 0, 3)]
  transfers between devices with their start and end apart: 3 -> 3, of which waited for: 2 -> 2; matrix products, arithmetic and copies ran while one was open for 27% -> 7% of each run, Pallas kernels for 17% -> 33%
where the time goes in v2:
time: 293 us; the launch traced here: 292 us
  Pallas kernels  199 us (68%)
  waiting for transfers between devices  43.6 us (15%)
  local copies, waits for them, and re-layouts  27 us (9%)
  starting transfers between devices  18.1 us (6%)
  matrix products  3.04 us (1%)
    pallas_call x1, Pallas kernels, k2_call(): pl.pallas_call(k2_kernel, out_shape=outs, in_specs=[pl.BlockSpec(memory_s...  103 us
    pallas_call x1, Pallas kernels, k1_call(): pl.pallas_call(k1_kernel, out_shape=outs, in_specs=[vm, pl.BlockSpec(memo...  95.6 us
    all_to_all x1, waiting for transfers between devices, body(): lax.all_to_all(back.reshape(16, 2, 64, 512), 'fsdp', split_axis=0, concat...  24.2 us
    all_to_all x1, waiting for transfers between devices, body(): arrived = lax.all_to_all(cells, 'fsdp', split_axis=0, concat_axis=0)  19.4 us
    unnamed x20, local copies, waits for them, and re-layouts  15.1 us
    all_to_all x1, starting transfers between devices, body(): lax.all_to_all(tags, 'fsdp', split_axis=0, concat_axis=0).reshape(32)  6.91 us
    all_to_all x1, starting transfers between devices, body(): lax.all_to_all(back.reshape(16, 2, 64, 512), 'fsdp', split_axis=0, concat...  6.29 us
  transfers between devices with their start and end apart: 3, of which 2 were waited for; matrix products, arithmetic and copies ran while one was open for 7% of the time, Pallas kernels for 33%

profile of v2, /device:TPU:1, one launch (start us, length us, event | category | flops | bytes accessed | tf_op | source)
XLA Modules:
  0.0 291.8 jit_solution(6966031004655407895)
XLA Ops:
  0.6 0.7 convert_element_type.25
  1.3 0.6 broadcast_in_dim.29
  1.9 6.9 %all-to-all-start = ((bf16[16,1,2]{2,1,0:T(2,128)(2,1)}), bf16[16,1,2]{2,1,0:T(2,128)(2,1)S(1)}, u32[]{:S(2)}, u32[]{:S(2)}) async-start(bf16[16,1,2]{2,1,0:T(2,128)(2,1)} %broadcast_in_dim.29), calls=%async_computation | async-start | bytes 16384 | tf_op jit(solution)/shard_map/all_to_all | solution.py:766
  8.8 0.7 pad_bitcast_fusion.1
  9.5 0.7 pad_bitcast_fusion
  10.1 0.1 copy.59
  10.3 0.1 copy.58
  10.4 0.8 copy.53
  11.1 0.8 copy.54
  11.9 0.8 copy.55
  12.6 0.8 copy.56
  13.4 0.7 reshape.67
  14.1 0.8 copy.57
  14.9 0.1 concatenate.3
  15.0 0.6 pad.13.vec6
  15.6 95.6 %forward.1 = (bf16[2,9,4,4,48,384]{5,4,3,2,1,0:T(8,128)(2,1)}, bf16[2,4,4,192,384]{4,3,2,1,0:T(8,128)(2,1)}, f32[8,3072]{1,0:T(8,128)}, bf16[336,768]{1,0:T(8,12...) custom-call(bf16[512,768]{1,0:T(8,128)(2,1)} %tok.3, ...), custom_call_target="tpu_custom_call" | custom-call | flops 6000000000 | bytes 50000000 | tf_op jit(solution)/shard_map/forward/pallas_call | solution.py:357
  111.1 0.0 all-to-all-done
  111.1 4.9 %all-to-all-start.1 = ((bf16[16,2,64,512]{3,2,1,0:T(8,128)(2,1)}), bf16[16,2,64,512]{3,2,1,0:T(8,128)(2,1)S(1)}, u32[]{:S(2)}, u32[]{:S(2)}) async-start(bf16[16,2,64,512]{3,2,1,0:T(8,128)(2,1)} %get-tuple-element.35), calls=%async_computation.1 | async-start | bytes 4194304 | tf_op jit(solution)/shard_map/all_to_all | solution.py:774
  116.0 4.1 %copy.62 = bf16[4,8,64,512]{3,1,2,0:T(8,128)(2,1)} copy(bf16[4,8,64,512]{3,2,1,0:T(8,128)(2,1)} %bitcast.28) | data formatting | bytes 4194304
  120.1 0.1 reshape.73
  120.2 2.4 convolution_convert_fusion
  122.6 2.1 copy.63
  124.6 19.4 %all-to-all-done.1 = bf16[16,2,64,512]{3,2,1,0:T(8,128)(2,1)S(1)} async-done(((bf16[16,2,64,512]{3,2,1,0:T(8,128)(2,1)}), bf16[16,2,64,512]{3,2,1,0:T(8,128)(2,1)S(1)}, u32[]{:S(2)}, u32[]{:S(2)}) %all-to-all-start.1) | async-done | bytes 2097184 | tf_op jit(solution)/shard_map/all_to_all | solution.py:774
  144.0 6.3 %all-to-all-start.2 = ((bf16[16,2,64,512]{3,2,1,0:T(8,128)(2,1)}), bf16[16,2,64,512]{3,2,1,0:T(8,128)(2,1)}, u32[]{:S(2)}, u32[]{:S(2)}) async-start(bf16[16,2,64,512]{3,2,1,0:T(8,128)(2,1)} %bitcast.23), calls=%async_computation.2 | async-start | bytes 4194304 | tf_op jit(solution)/shard_map/all_to_all | solution.py:769
  150.3 1.2 copy.60
  151.5 0.7 convolution_convert_fusion.1
  152.2 2.0 copy.61
  154.2 24.2 %all-to-all-done.2.dc_ref = bf16[16,2,64,512]{3,2,1,0:T(8,128)(2,1)} async-done(((bf16[16,2,64,512]{3,2,1,0:T(8,128)(2,1)}), bf16[16,2,64,512]{3,2,1,0:T(8,128)(2,1)}, u32[]{:S(2)}, u32[]{:S(2)}) %all-to-all-start.2) | async-done | bytes 2097184 | tf_op jit(solution)/shard_map/all_to_all | solution.py:769
  178.4 103.1 %backward.1 = (f32[512,768]{1,0:T(8,128)}, f32[6,2304]{1,0:T(8,128)}, f32[6,768]{1,0:T(8,128)}, f32[6,3072]{1,0:T(8,128)}, f32[24,768]{1,0:T(8,128)}, /*index=5*/f32[6,512]{1,0:T(8,128)}, f32[6,128]{1,0:T(8,128)}) custom-call(s32[2]{0:T(128)} %lens.3, bf16[2,9,4,4,48,384]{5,4,3,2,1,0:T(8,128)(2,1)} %get-tuple-element.36.g_hbm, ...), custom_call_target="tpu_custom_call" | custom-call | flops 12000000000 | bytes 50000000 | tf_op jit(solution)/shard_map/backward/pallas_call | solution.py:738
  281.5 0.0 copy-start.2
  281.5 0.0 copy-start.3
  281.5 0.0 copy-start
  281.5 0.0 copy-start.1
  281.5 0.0 copy-start.4
  281.5 1.5 slice_reduce_fusion.5
  283.0 1.6 slice_reduce_fusion
  284.7 0.7 slice.28
  285.4 0.6 reshape.72
  286.0 2.7 copy.70
  288.6 0.0 copy-done.2
  288.6 0.6 copy.71
  289.3 0.0 copy-done.3
  289.3 0.6 copy.72
  289.9 0.0 copy-done
  289.9 0.6 copy.73
  290.5 0.6 copy.74
  291.2 0.0 copy-done.4
  291.2 0.6 copy.75
  (2 shorter events, 0.0 us)
Async XLA Ops:
  1.9 109.2 %all-to-all-start = ((bf16[16,1,2]{2,1,0:T(2,128)(2,1)}), bf16[16,1,2]{2,1,0:T(2,128)(2,1)S(1)}, u32[]{:S(2)}, u32[]{:S(2)}) async-start(bf16[16,1,2]{2,1,0:T(2,128)(2,1)} %broadcast_in_dim.29), calls=%async_computation | async-start | bytes 16384 | tf_op jit(solution)/shard_map/all_to_all | solution.py:766
  111.1 32.9 %all-to-all-start.1 = ((bf16[16,2,64,512]{3,2,1,0:T(8,128)(2,1)}), bf16[16,2,64,512]{3,2,1,0:T(8,128)(2,1)S(1)}, u32[]{:S(2)}, u32[]{:S(2)}) async-start(bf16[16,2,64,512]{3,2,1,0:T(8,128)(2,1)} %get-tuple-element.35), calls=%async_computation.1 | async-start | bytes 4194304 | tf_op jit(solution)/shard_map/all_to_all | solution.py:774
  144.0 34.4 %all-to-all-start.2 = ((bf16[16,2,64,512]{3,2,1,0:T(8,128)(2,1)}), bf16[16,2,64,512]{3,2,1,0:T(8,128)(2,1)}, u32[]{:S(2)}, u32[]{:S(2)}) async-start(bf16[16,2,64,512]{3,2,1,0:T(8,128)(2,1)} %bitcast.23), calls=%async_computation.2 | async-start | bytes 4194304 | tf_op jit(solution)/shard_map/all_to_all | solution.py:769
  281.5 7.1 %copy-start.2 = (f32[6,2304]{1,0:T(8,128)S(1)}, f32[6,2304]{1,0:T(8,128)}, u32[]{:S(2)}) copy-start(f32[6,2304]{1,0:T(8,128)} %get-tuple-element.81) | copy-start | bytes 165892
  281.5 7.8 %copy-start.3 = (f32[6,768]{1,0:T(8,128)S(1)}, f32[6,768]{1,0:T(8,128)}, u32[]{:S(2)}) copy-start(f32[6,768]{1,0:T(8,128)} %get-tuple-element.82) | copy-start | bytes 55300
  281.5 8.4 %copy-start = (f32[6,3072]{1,0:T(8,128)S(1)}, f32[6,3072]{1,0:T(8,128)}, u32[]{:S(2)}) copy-start(f32[6,3072]{1,0:T(8,128)} %get-tuple-element.85) | copy-start | bytes 221188
  281.5 9.0 %copy-start.1 = (f32[24,768]{1,0:T(8,128)S(1)}, f32[24,768]{1,0:T(8,128)}, u32[]{:S(2)}) copy-start(f32[24,768]{1,0:T(8,128)} %get-tuple-element.87) | copy-start | bytes 221188
  281.5 9.6 %copy-start.4 = (f32[6,512]{1,0:T(8,128)S(1)}, f32[6,512]{1,0:T(8,128)}, u32[]{:S(2)}) copy-start(f32[6,512]{1,0:T(8,128)} %get-tuple-element.89) | copy-start | bytes 36868

commit v3 on v2

--- a/solution.py
+++ b/solution.py
@@ -44,13 +44,6 @@
     ]
 
 
-def pack_vec(ln1_g, ln1_b, ln2_g, ln2_b, fc2_b, fc1_b, dec_b, mask):
-    cols = [ln1_g[:, None], ln1_b[:, None], ln2_g[:, None], ln2_b[:, None], fc2_b[:, None], fc1_b.reshape(6, 4),
-            jnp.pad(dec_b, (0, 2))[:, None], jnp.pad(mask, (0, 2))[:, None]]
-    v = jnp.concatenate(cols, axis=1)
-    return jnp.pad(v, ((0, 0), (0, 128 - v.shape[1])))
-
-
 ROWS = 336
 HEADS_PAIRS = 6
 D = 768
@@ -67,10 +60,20 @@
     return m
 
 
-def quad_spread():
+def fc1_bias_spread():
     m = np.zeros((192, 768), np.float32)
-    m[np.arange(768) // 4, np.arange(768)] = 1
+    n = np.arange(768)
+    m[6 * (n // 24) + n % 6, n] = 1
     return m
+
+
+def peers(f):
+    return [(r, (f + r) % 16) for r in range(1, 16)]
+
+
+def greet(bar, devices):
+    for t in devices:
+        pl.semaphore_signal(bar, inc=1, device_id=t, device_id_type=MESH)
 
 
 def stats(v):
@@ -86,10 +89,16 @@
     return f * cdf, cdf + f * pdf
 
 
-def k1_kernel(tok, lens, pos, vec6, qkv_s, out_s, fc1_s, fc2_s, dec_s, p_ref, m2_ref, m4_ref,
-              g_hbm, g2_hbm, rows_ref, a_ref, qkv_ref, p_out, o_ref, x2_ref, h2_ref, act_ref, dact_ref, e_ref, cells_ref,
-              g_ref, g2_ref, sp, s_ref, s1, z_ref, ss1, rs1, loc, ssem, rsem, wsem):
+def k1_kernel(ids, lens, pos, tok, l1g, l1b, qkv_s, out_s, l2g, l2b, fc1_s, fc1b, fc2_s, fc2b, dec_s, decb, maskt, cot_hbm,
+              p_ref, m2_ref, m4_ref,
+              g_hbm, g2_hbm, rows_hbm, a_hbm, qkv_hbm, p_hbm, o_hbm, x2_hbm, h2_hbm, act_hbm, dact_hbm, e_hbm, cells_hbm,
+              dz_hbm, dx_hbm, dm_hbm, vs_hbm, inv_hbm,
+              g_ref, g2_ref, rows_ref, a_ref, qkv_ref, p_out, o_ref, x2_ref, h2_ref, act_ref, dact_ref, e_ref, cells_ref,
+              dz, dx, dm, vs, inv,
+              sp, s_ref, s1, z_ref, vrow, tag, tags, idv, idm, cot, cotsend, dc, hits,
+              ss1, rs1, loc, ssem, rsem, wsem, osem, tss, tsr, bss, bsr, mss, msr, lsem):
     z, x, y, c = coords()
+    dp, f = lax.axis_index("dp"), lax.axis_index("fsdp")
     zp, zm, zo = (z + 1) % 4, (z + 3) % 4, (z + 2) % 4
     xp, xm, xo = (x + 1) % 4, (x + 3) % 4, (x + 2) % 4
     o = 1 - c
@@ -97,11 +106,13 @@
     targets = [dev(zp, x, y, c), dev(zm, x, y, c), dev(z, xp, y, c), dev(z, xm, y, c)]
     group = []
     for dy in range(4):
-        for dc in range(2):
-            if dy or dc:
-                group.append((dy, dc, dev(z, x, (y + dy) % 4, (c + dc) % 2)))
-    for t in targets + [g[2] for g in group]:
-        pl.semaphore_signal(bar, inc=1, device_id=t, device_id_type=MESH)
+        for dc_ in range(2):
+            if dy or dc_:
+                group.append((dy, dc_, dev(z, x, (y + dy) % 4, (c + dc_) % 2)))
+    greeted = targets + [(dp, g) for _, g in peers(f)]
+    greet(bar, greeted)
+    ld_cot = pltpu.make_async_copy(cot_hbm, cot, lsem.at[0])
+    ld_cot.start()
 
     sp[...] = jnp.zeros_like(sp)
     for h in range(2):
@@ -112,24 +123,93 @@
             sp[h, 24 + 6 * u:30 + 6 * u, :] = fc1_s[:, h * 1536 + u * LW:h * 1536 + (u + 1) * LW].astype(f32)
         sp[h, 48:72, :] = fc2_s[:, h * LW:(h + 1) * LW].astype(f32)
         sp[h, 72:78, 0:256] = dec_s[:, h * 256:(h + 1) * 256].astype(f32)
-    sp[0, 72:78, 256:384] = vec6[...].astype(f32)
+    vrow[...] = jnp.zeros_like(vrow)
+    for i, r in enumerate((l1g, l1b, l2g, l2b, fc2b)):
+        vrow[i:i + 1, 0:6] = r[...].astype(f32)
+    for q in range(4):
+        vrow[5 + q:6 + q, 0:6] = fc1b[:, 6 * q:6 * q + 6].astype(f32)
+    vrow[9:10, 0:4] = decb[...].astype(f32)
+    vrow[10:11, 0:4] = maskt[...].astype(f32)
+    sp[0, 72:78, 256:384] = vrow[...].T[0:6]
     s_ref[...] = sp[...].astype(bf16)
-    pl.semaphore_wait(bar, len(targets) + len(group))
+    first_small = lens[0] < lens[1]
+    trow = lax.broadcasted_iota(jnp.int32, (8, 128), 0)
+    tag[...] = jnp.where(trow == 0, jnp.where(first_small, ids[1], ids[0]), jnp.where(first_small, ids[0], ids[1]))
+    pl.semaphore_wait(bar, len(greeted))
 
     me = 2 * y + c
     own = pltpu.make_async_copy(s_ref.at[c], s1.at[me], loc)
     own.start()
     firsts = []
-    for i, (dy, dc, t) in enumerate(group):
-        cp = pltpu.make_async_remote_copy(s_ref.at[(c + dc) % 2], s1.at[me], ss1.at[i], rs1.at[i], device_id=t, device_id_type=MESH)
+    for i, (dy, dc_, t) in enumerate(group):
+        cp = pltpu.make_async_remote_copy(s_ref.at[(c + dc_) % 2], s1.at[me], ss1.at[i], rs1.at[i], device_id=t, device_id_type=MESH)
         cp.start()
-        src = 2 * ((y + 4 - dy) % 4) + (c + dc) % 2
+        src = 2 * ((y + 4 - dy) % 4) + (c + dc_) % 2
         rc = pltpu.make_async_remote_copy(s_ref.at[c], s1.at[src], ss1.at[i], rs1.at[i], device_id=t, device_id_type=MESH)
         firsts.append((cp, rc))
+
+    tagged = []
+    tags[f] = tag[...]
+    for r, g in peers(f):
+        cp = pltpu.make_async_remote_copy(tag, tags.at[f], tss.at[r], tsr.at[r], device_id=(dp, g), device_id_type=MESH)
+        cp.start(); tagged.append(cp)
+    for r, g in peers(f):
+        src = (f + 16 - r) % 16
+        pltpu.make_async_remote_copy(tag, tags.at[src], tss.at[r], tsr.at[r], device_id=(dp, g), device_id_type=MESH).wait_recv()
+    for s in range(16):
+        idv[s:s + 1, :] = tags[s, 0:1, :]
+        idv[16 + s:17 + s, :] = tags[s, 1:2, :]
+    ld_ids = pltpu.make_async_copy(idv, idm, lsem.at[1])
+    ld_ids.start()
+    srow = lax.broadcasted_iota(jnp.int32, (32, 128), 0)
+    hit = idv[...] == lax.broadcasted_iota(jnp.int32, (32, 128), 1)
+    place_of = jnp.where((srow >= 16) & (f >= 4), 32, srow)
+    inv[...] = jnp.broadcast_to(jnp.sum(jnp.where(hit, place_of, 0), axis=0, keepdims=True), (8, 128))
+    ld_ids.wait()
+    ld_cot.wait()
+    for s in range(32):
+        cotsend[s] = cot[idm[s, 0]]
 
     own.wait()
     for cp, rc in firsts:
         rc.wait_recv()
+
+    few = f < 4
+    def to_peer(i, g):
+        big = pltpu.make_async_remote_copy(cotsend.at[g], dc.at[f], bss.at[i], bsr.at[i], device_id=(dp, g), device_id_type=MESH)
+        return big
+    def small_to_peer(i, g):
+        return pltpu.make_async_remote_copy(cotsend.at[16 + g], dc.at[16 + f % 4], mss.at[i], msr.at[f % 4], device_id=(dp, g), device_id_type=MESH)
+    own_dc = pltpu.make_async_copy(cotsend.at[f], dc.at[f], lsem.at[2])
+    own_small = pltpu.make_async_copy(cotsend.at[16 + f], dc.at[16 + f % 4], lsem.at[3])
+    def send_cotangents():
+        own_dc.start()
+        for r, g in peers(f):
+            to_peer(r, g).start()
+        @pl.when(few)
+        def _():
+            own_small.start()
+            for r, g in peers(f):
+                small_to_peer(r, g).start()
+    def get_cotangents():
+        own_dc.wait()
+        for r, g in peers(f):
+            src = (f + 16 - r) % 16
+            pltpu.make_async_remote_copy(cotsend.at[g], dc.at[src], bss.at[r], bsr.at[r], device_id=(dp, g), device_id_type=MESH).wait_recv()
+        for s in range(4):
+            @pl.when(f != s)
+            def _():
+                pltpu.make_async_remote_copy(cotsend.at[16], dc.at[16 + s], mss.at[0], msr.at[s], device_id=(dp, s), device_id_type=MESH).wait_recv()
+        @pl.when(few)
+        def _():
+            own_small.wait()
+    def finish_cotangents():
+        for r, g in peers(f):
+            to_peer(r, g).wait_send()
+        @pl.when(few)
+        def _():
+            for r, g in peers(f):
+                small_to_peer(r, g).wait_send()
 
     def relay(lo, hi):
         flat = s1[...].reshape(640, LW)
@@ -220,7 +300,7 @@
         rows_ref[0:5, 0:768] = vt[0:5]
         md = lax.dot_general(v, m2_ref[...], TN, preferred_element_type=f32)
         rows_ref[6:8, 0:512] = md[9:11]
-        lane = lax.broadcasted_iota(jnp.int32, (8, 768), 1) % 4
+        lane = (lax.broadcasted_iota(jnp.int32, (8, 768), 1) % 24) // 6
         row = lax.broadcasted_iota(jnp.int32, (8, 768), 0)
         for s in range(4):
             q = lax.dot_general(v[192 * s:192 * s + 192], m4_ref[...], TN, preferred_element_type=f32)
@@ -244,7 +324,7 @@
         r = lax.broadcasted_iota(jnp.int32, shape, axis)
         return (r >= ends0).astype(jnp.int32) + (r >= ends1).astype(jnp.int32)
 
-    def attention():
+    def attention(lo, hi):
         low = lax.broadcasted_iota(jnp.int32, (1, 128), 1) < 64
         same = seg((ROWS, 1), 0) == seg((1, ROWS), 1)
         bias = jnp.where(same, 0.0, -1e30)
@@ -264,7 +344,7 @@
                 outs_.append(jnp.dot(pr, v, preferred_element_type=f32))
             o_ref[:, pl.ds(pl.multiple_of(i * 128, 128), 128)] = jnp.where(low, outs_[0], outs_[1]).astype(bf16)
             return 0
-        lax.fori_loop(0, HEADS_PAIRS, pair, 0)
+        lax.fori_loop(lo, hi, pair, 0)
 
     def out_proj():
         for h in range(2):
@@ -298,25 +378,60 @@
             t = jnp.dot(e_ref[...], g_ref[h, 8, :, :, :, 0:256].reshape(768, 256), preferred_element_type=f32)
             z_ref[:, cs] = (t + rows_ref[6:7, cs]).astype(bf16)
         z_ref[:, 512:640] = jnp.ones((ROWS, 128), bf16)
-        p_ = pos[0:1, 0:ROWS]
-        target = jnp.where(p_ >= 0, seg((1, ROWS), 1) * 1024 + p_, -1)
         def block(i, _):
-            slot = i // 4
-            first = i * 256
-            cell = first + lax.broadcasted_iota(jnp.int32, (256, 1), 0)
-            fill = (cell == target).astype(f32).astype(bf16)
+            fill = hits[pl.ds(pl.multiple_of(i * 256, 256), 256), :]
             r = jnp.dot(fill, z_ref[...], preferred_element_type=f32)
-            limit = 4 * jnp.where(slot == 0, lens[0], lens[1])
-            valid = (cell - slot * 1024 < limit).astype(f32)
-            empty = jnp.where(valid > 0.0, 1.0 - r[:, 512:640], 0.0)
+            empty = 1.0 - r[:, 512:640]
             for t in range(4):
                 cs = slice(128 * t, 128 * t + 128)
                 val = r[:, cs] + empty * rows_ref[7:8, cs]
-                cells_ref[pl.ds(4 * (i % 4), 4), slot, :, cs] = val.astype(bf16).reshape(4, 64, 128)
+                cells_ref[pl.ds(4 * i, 4), :, cs] = val.astype(bf16).reshape(4, 64, 128)
             return 0
-        lax.fori_loop(0, 8, block, 0)
-
-    after = AFTER(dict(rows_of=rows_of, ln1=ln1, qkv=qkv, attention=attention, out_proj=out_proj, fc1=fc1, fc2=fc2, dec=dec))
+        lax.fori_loop(0, 5, block, 0)
+
+    def fills():
+        p_ = pos[0:1, 0:ROWS]
+        large = seg((1, ROWS), 1) == jnp.where(first_small, 1, 0)
+        target = jnp.where(p_ >= 0, jnp.where(large, p_, 1024 + p_), -1)
+        def block(i, _):
+            cell = i * 256 + lax.broadcasted_iota(jnp.int32, (256, 1), 0)
+            hits[pl.ds(pl.multiple_of(i * 256, 256), 256), :] = (cell == target).astype(f32).astype(bf16)
+            return 0
+        lax.fori_loop(0, 5, block, 0)
+
+    def cell_grads():
+        get_cotangents()
+        d = dc[...].reshape(1280, 512)
+        dz[...] = lax.dot_general(hits[...], d, TN, preferred_element_type=f32).astype(bf16)
+        covered = lax.dot_general(jnp.ones((16, ROWS), bf16), hits[...], NT, preferred_element_type=f32)
+        vs[10:11, :] = jnp.dot((1.0 - covered).astype(bf16), d, preferred_element_type=f32)[0:1]
+        vs[9:10, :] = jnp.sum(dz[...].astype(f32), axis=0, keepdims=True)
+        for n in range(2):
+            rs = slice(n * 384, (n + 1) * 384)
+            wt = [g_ref[h, 8, :, :, :, 0:256].reshape(768, 256)[rs] for h in range(2)]
+            t = lax.dot_general(dz[:, 0:256], wt[0], NT, preferred_element_type=f32)
+            t = t + lax.dot_general(dz[:, 256:512], wt[1], NT, preferred_element_type=f32)
+            dx[:, rs] = t
+            dm[:, rs] = t.astype(bf16)
+
+    kept = dict(rows=(rows_ref, rows_hbm), a=(a_ref, a_hbm), qkv=(qkv_ref, qkv_hbm), p=(p_out, p_hbm), o=(o_ref, o_hbm),
+                x2=(x2_ref, x2_hbm), h2=(h2_ref, h2_hbm), act=(act_ref, act_hbm), dact=(dact_ref, dact_hbm), e=(e_ref, e_hbm),
+                cells=(cells_ref, cells_hbm), dz=(dz, dz_hbm), dx=(dx, dx_hbm), dm=(dm, dm_hbm), vs=(vs, vs_hbm), inv=(inv, inv_hbm))
+    def keep(*names):
+        for n in names:
+            cp = pltpu.make_async_copy(*kept[n], osem.at[list(kept).index(n)])
+            cp.start(); outs.append(cp)
+
+    vs[...] = jnp.zeros_like(vs)
+    rows_ref[...] = jnp.zeros_like(rows_ref)
+    after = {
+        0: [send_cotangents, lambda: keep("inv"), fills],
+        5: [rows_of, ln1, lambda: keep("rows", "a")],
+        6: [qkv, lambda: attention(0, 3), lambda: keep("qkv")],
+        7: [lambda: attention(3, 6), out_proj, lambda: keep("p", "o", "x2", "h2"), fc1, lambda: keep("act", "dact"), cell_grads,
+            lambda: keep("dz", "dx", "dm", "vs")],
+        8: [fc2, lambda: keep("e"), dec, lambda: keep("cells")],
+    }
     order = PIECE_ORDER
     pieces = [None] * 4
     k = 0
@@ -333,51 +448,53 @@
                 for ch in pieces[p]: ch[s]()
             if s == 5: to_hbm(p)
         for fn in after.get(t, []): fn()
-    for fn in after.get("end", []): fn()
     for cp, rc in firsts: cp.wait_send()
     for cp in sends: cp.wait_send()
+    for cp in tagged: cp.wait_send()
+    finish_cotangents()
     for cp in outs: cp.wait()
 
 PIECE_ORDER = [3, 0, 1, 2]
 
-def AFTER(f):
-    return {"end": [f[n] for n in ("rows_of", "ln1", "qkv", "attention", "out_proj", "fc1", "fc2", "dec")]}
-
-def k1_call(tok, lens, pos, vec6, qkv_s, out_s, fc1_s, fc2_s, dec_s):
+def k1_call(*args):
     nk = sum(len(c) for c in ag_chunks())
     S = jax.ShapeDtypeStruct
-    vm = pl.BlockSpec(memory_space=pltpu.VMEM)
+    vm, smem = pl.BlockSpec(memory_space=pltpu.VMEM), pl.BlockSpec(memory_space=pltpu.SMEM)
     anyspec = pl.BlockSpec(memory_space=pl.ANY)
-    V = pltpu.VMEM
+    V, DMA = pltpu.VMEM, pltpu.SemaphoreType.DMA
     outs = (
         S((2, 9, 4, 4, 48, LW), bf16), S((2, 4, 4, 192, LW), bf16), S((8, 3072), f32), S((ROWS, 768), bf16),
         S((ROWS, 2304), bf16), S((12, ROWS, ROWS), bf16), S((ROWS, 768), bf16), S((ROWS, 768), f32),
-        S((ROWS, 768), bf16), S((ROWS, 3072), bf16), S((ROWS, 3072), bf16), S((ROWS, 768), bf16), S((16, 2, 64, 512), bf16),
+        S((ROWS, 768), bf16), S((ROWS, 3072), bf16), S((ROWS, 3072), bf16), S((ROWS, 768), bf16), S((20, 64, 512), bf16),
+        S((ROWS, 512), bf16), S((ROWS, 768), f32), S((ROWS, 768), bf16), S((16, 512), f32), S((8, 128), jnp.int32),
     )
     return pl.pallas_call(
         k1_kernel,
         out_shape=outs,
-        in_specs=[vm, pl.BlockSpec(memory_space=pltpu.SMEM)] + [vm] * 10,
-        out_specs=[anyspec, anyspec] + [vm] * 11,
-        scratch_shapes=[
-            V((2, 9, 4, 4, 48, LW), bf16), V((2, 4, 4, 192, LW), bf16),
-            V((2, SROWS, LW), f32), V((2, SROWS, LW), bf16), V((8, SROWS, LW), bf16), V((ROWS, 640), bf16),
-            pltpu.SemaphoreType.DMA((7,)), pltpu.SemaphoreType.DMA((7,)), pltpu.SemaphoreType.DMA(()),
-            pltpu.SemaphoreType.DMA((nk, 12)), pltpu.SemaphoreType.DMA((nk, 12)), pltpu.SemaphoreType.DMA((4,)),
+        in_specs=[smem, smem] + [vm] * 15 + [anyspec] + [vm] * 3,
+        out_specs=[anyspec] * 18,
+        scratch_shapes=[V(t.shape, t.dtype) for t in outs] + [
+            V((2, SROWS, LW), f32), V((2, SROWS, LW), bf16), V((8, SROWS, LW), bf16), V((ROWS, 640), bf16), V((128, 128), f32),
+            V((8, 128), jnp.int32), V((16, 8, 128), jnp.int32), V((32, 128), jnp.int32), pltpu.SMEM((32, 128), jnp.int32),
+            V((32, 64, 512), bf16), V((32, 64, 512), bf16), V((20, 64, 512), bf16), V((1280, ROWS), bf16),
+            DMA((7,)), DMA((7,)), DMA(()), DMA((nk, 12)), DMA((nk, 12)), DMA((4,)), DMA((16,)), DMA((16,)), DMA((16,)),
+            DMA((16,)), DMA((16,)), DMA((16,)), DMA((4,)), DMA((4,)),
         ],
         compiler_params=pltpu.CompilerParams(collective_id=0, has_side_effects=True, vmem_limit_bytes=60 * 2**20),
         cost_estimate=pl.CostEstimate(flops=6 * 10**9, bytes_accessed=5 * 10**7, transcendentals=0),
         name="forward",
-    )(tok, lens, pos, vec6, qkv_s, out_s, fc1_s, fc2_s, dec_s,
-      jnp.asarray(perm_matrix(), bf16), jnp.asarray(cell_spread(), bf16), jnp.asarray(quad_spread(), bf16))
-
-
-def k2_kernel(lens, g_hbm, g2_hbm, rows_ref, tok, a_ref, qkv_ref, p_hbm, o_ref, x2_ref, h2_ref, act_ref, dact_ref, e_ref,
-              pos, dc_ref, pt_ref, m2_ref, m4_ref,
-              tg_ref, oq_ref, oo_ref, of1_ref, of2_ref, od_ref, ov_ref,
-              wd, wa, wb, sta, sta2, stc, sg, sg2, acc, acc2, xa, xa2, xb, xb2,
-              dz, dx, dh, dm, df, dqkv, vsum, pb, db, fs, f1, fo, ssem, rsem, ss1, rs1, loc, wsem, psem, tsem, dsem):
+    )(*args, jnp.asarray(perm_matrix(), bf16), jnp.asarray(cell_spread(), bf16), jnp.asarray(fc1_bias_spread(), bf16))
+
+
+def k2_kernel(g_hbm, g2_hbm, rows_hbm, a_hbm, qkv_hbm, p_hbm, o_hbm, x2_hbm, h2_hbm, act_hbm, dact_hbm, e_hbm, cells_hbm,
+              dz_hbm, dx_hbm, dm_hbm, vs_hbm, tok_hbm, pt_ref, m2_ref, m4_ref,
+              tg_ref, arr, oq_ref, oo_ref, of1_ref, of2_ref, od_ref, v0_ref, v1_ref, v2_ref, v3_ref, v4_ref, vf_ref, vd_ref, vm_ref,
+              rows_ref, a_ref, qkv_ref, o_ref, x2_ref, h2_ref, act_ref, dact_ref, e_ref, dz, dx, dm, vs, tok,
+              wa, wb, sta, sta2, stc, sg, sg2, acc, acc2, xa, xa2, xb, xb2,
+              dh, df, dqkv, vsum, pb, fs, f1, fo, zb, vt,
+              ssem, rsem, ss1, rs1, loc, wsem, psem, tsem, isem, css, csr, csl):
     z, x, y, c = coords()
+    dp, f = lax.axis_index("dp"), lax.axis_index("fsdp")
     zp, zm, zo = (z + 1) % 4, (z + 3) % 4, (z + 2) % 4
     xp, xm, xo = (x + 1) % 4, (x + 3) % 4, (x + 2) % 4
     o = 1 - c
@@ -389,14 +506,58 @@
         for dc in range(2):
             if dy or dc:
                 group.append((dy, dc, dev(z, x, (y + dy) % 4, (c + dc) % 2)))
-    for t in targets + [g[2] for g in group]:
-        pl.semaphore_signal(bar, inc=1, device_id=t, device_id_type=MESH)
-    ld_d = pltpu.make_async_copy(g_hbm.at[:, 8], wd, wsem.at[0])
-    ld_a = pltpu.make_async_copy(g2_hbm, wa, wsem.at[1])
-    ld_b = pltpu.make_async_copy(g_hbm.at[:, 4:8], wb, wsem.at[2])
-    ld_c = pltpu.make_async_copy(g_hbm.at[:, 0:4], wb, wsem.at[3])
-    for l in (ld_d, ld_a, ld_b): l.start()
-    pl.semaphore_wait(bar, len(targets) + len(group))
+    greeted = targets + [(dp, g) for _, g in peers(f)]
+    greet(bar, greeted)
+    loads = {}
+    def load(name, src, dst):
+        loads[name] = pltpu.make_async_copy(src, dst, isem.at[len(loads)])
+        return loads[name]
+    for name, src, dst in (
+        ("dm", dm_hbm, dm), ("act", act_hbm, act_ref), ("fc2", g2_hbm, wa), ("dact", dact_hbm, dact_ref), ("fc1", g_hbm.at[:, 4:8], wb),
+        ("h2", h2_hbm, h2_ref), ("x2", x2_hbm, x2_ref), ("dx", dx_hbm, dx), ("rows", rows_hbm, rows_ref), ("o", o_hbm, o_ref),
+        ("qkv", qkv_hbm, qkv_ref), ("e", e_hbm, e_ref), ("dz", dz_hbm, dz), ("a", a_hbm, a_ref), ("tok", tok_hbm.at[0:ROWS], tok),
+        ("vs", vs_hbm, vs),
+    ):
+        load(name, src, dst).start()
+    def need(*names):
+        for n in names: loads[n].wait()
+    ld_c = pltpu.make_async_copy(g_hbm.at[:, 0:4], wb, wsem.at[0])
+    zb[...] = jnp.zeros_like(zb)
+    vt[...] = jnp.zeros_like(vt)
+    vsum[...] = jnp.zeros_like(vsum)
+    pl.semaphore_wait(bar, len(greeted))
+
+    few = f < 4
+    def cells_to(i, g):
+        return pltpu.make_async_remote_copy(cells_hbm.at[g], arr.at[f], css.at[i], csr.at[i], device_id=(dp, g), device_id_type=MESH)
+    def small_cells_to(i, g):
+        return pltpu.make_async_remote_copy(cells_hbm.at[16 + g % 4], arr.at[16 + f], css.at[16 + i], csr.at[16 + i], device_id=(dp, g), device_id_type=MESH)
+    locals_ = [pltpu.make_async_copy(cells_hbm.at[f], arr.at[f], csl.at[0]), pltpu.make_async_copy(zb, arr.at[32], csl.at[1])]
+    own_small = pltpu.make_async_copy(cells_hbm.at[16 + f % 4], arr.at[16 + f], csl.at[2])
+    for l in locals_: l.start()
+    for r, g in peers(f):
+        cells_to(r, g).start()
+        @pl.when(g < 4)
+        def _():
+            small_cells_to(r, g).start()
+    @pl.when(few)
+    def _():
+        own_small.start()
+    def finish_cells():
+        for l in locals_: l.wait()
+        for r, g in peers(f):
+            src = (f + 16 - r) % 16
+            pltpu.make_async_remote_copy(cells_hbm.at[g], arr.at[src], css.at[r], csr.at[r], device_id=(dp, g), device_id_type=MESH).wait_recv()
+            cells_to(r, g).wait_send()
+            @pl.when(g < 4)
+            def _():
+                small_cells_to(r, g).wait_send()
+        @pl.when(few)
+        def _():
+            own_small.wait()
+            for r, g in peers(f):
+                src = (f + 16 - r) % 16
+                pltpu.make_async_remote_copy(cells_hbm.at[16], arr.at[16 + src], css.at[16 + r], csr.at[16 + r], device_id=(dp, g), device_id_type=MESH).wait_recv()
 
     sends = {}
     def send(k, i, src, dst, to):
@@ -484,48 +645,8 @@
         def step(i, _):
             body(pl.ds(pl.multiple_of(i * 48, 48), 48)); return 0
         lax.fori_loop(0, n, step, 0)
-    ends0 = lens[0] + 2
-    ends1 = ends0 + lens[1] + 2
     def col(base, width, unit):
         return pl.ds(pl.multiple_of(base, unit), width)
-
-    def start_grads():
-        p_ = jnp.broadcast_to(pos[0:1, 0:384], (8, 384)).astype(f32)
-        r_ = lax.broadcasted_iota(jnp.int32, (8, 384), 1)
-        seg = ((r_ >= ends0).astype(jnp.int32) + (r_ >= ends1).astype(jnp.int32)).astype(f32)
-        target = jnp.where(p_ >= 0.0, seg * 1024.0 + p_, -1.0).T[0:ROWS, 0:1].astype(jnp.int32)
-        dx[:, 0:512] = jnp.zeros((ROWS, 512), f32)
-        vsum[...] = jnp.zeros_like(vsum)
-        def load(i):
-            return pltpu.make_async_copy(dc_ref.at[pl.ds(4 * (i % 4), 4), i // 4], db.at[i % 2], dsem.at[i % 2])
-        load(0).start()
-        def block(i, _):
-            load(i).wait()
-            pl.when(i < 7)(lambda: load(i + 1).start())
-            slot = i // 4
-            cell = i * 256 + lax.broadcasted_iota(jnp.int32, (1, 256), 1)
-            hit = (target == cell).astype(f32)
-            dcb = db[i % 2].reshape(256, 512)
-            dx[:, 0:512] += jnp.dot(hit.astype(bf16), dcb, preferred_element_type=f32)
-            limit = 4 * jnp.where(slot == 0, lens[0], lens[1])
-            empty = jnp.where(cell - slot * 1024 < limit, 1.0 - jnp.sum(hit, axis=0, keepdims=True), 0.0)
-            em = jnp.dot(jnp.broadcast_to(empty, (16, 256)).astype(bf16), dcb, preferred_element_type=f32)
-            vsum[10:11, 0:512] += em[0:1]
-            return 0
-        lax.fori_loop(0, 8, block, 0)
-        dz[...] = dx[:, 0:512].astype(bf16)
-        vsum[9:10, 0:512] = jnp.sum(dz[...].astype(f32), axis=0, keepdims=True)
-
-    def wdec(h):
-        return wd[h, :, :, :, 0:256].reshape(768, 256)
-    def dec_back():
-        for n in range(2):
-            rs = slice(n * 384, (n + 1) * 384)
-            t = lax.dot_general(dz[:, 0:256], wdec(0)[rs], NT, preferred_element_type=f32)
-            t = t + lax.dot_general(dz[:, 256:512], wdec(1)[rs], NT, preferred_element_type=f32)
-            dx[:, rs] = t
-            dm[:, rs] = t.astype(bf16)
-        vsum[4:5, 0:768] = jnp.sum(dm[...].astype(f32), axis=0, keepdims=True)
 
     def grad_fc2(h, dst):
         def part(i, _):
@@ -636,7 +757,7 @@
         srow2 = lax.broadcasted_iota(jnp.int32, (128, 512), 0)
         r2 = jnp.where((srow2 == 9) | (srow2 == 10), r2, 0.0).astype(bf16)
         v = v + lax.dot_general(m2_ref[...], r2, NT, preferred_element_type=f32)
-        lane = lax.broadcasted_iota(jnp.int32, (128, 768), 1) % 4
+        lane = (lax.broadcasted_iota(jnp.int32, (128, 768), 1) % 24) // 6
         parts = []
         for s in range(4):
             wrow = jnp.broadcast_to(vsum[5:6, 768 * s:768 * s + 768], (128, 768))
@@ -651,25 +772,27 @@
     def acc8(v, cs): acc[8, :, :, :, cs] = v
     def stc8(v, cs): stc[0, :, :, :, cs] = v
 
-    start_grads()
-    ld_d.wait()
-    dec_back()
+    need("dm", "act")
     grad_fc2(o, sta2); st(2, 0)
     grad_fc2(c, acc2)
-    ld_a.wait()
+    vsum[4:5, 0:768] = jnp.sum(dm[...].astype(f32), axis=0, keepdims=True)
+    need("fc2", "dact")
     fc2_back()
     st(2, 1)
-    ld_b.wait()
+    need("fc1")
     fc1_back()
     ld_c.start()
     load_p(0).start()
+    need("h2")
     grad_fc1(o, sta, 0); st(1, 0)
     st(2, 2)
     grad_fc1(c, acc, 4)
+    need("x2", "dx", "rows")
     norm_back(x2_ref, 2, dx, dm, 2)
     st(2, 3); st(1, 1)
     ld_c.wait()
     for kk in keys[1]: sends[kk, 8].wait_send(); del sends[kk, 8]
+    need("o", "qkv")
     grad_out(o, sta); grad_out(c, acc)
     out_back()
     st(2, 4); st(1, 2)
@@ -677,11 +800,14 @@
     st(2, 5); st(1, 3)
     attn_back(3, 6)
     st(1, 4)
+    need("a")
     grad_qkv(o, sta)
     st(0, 0)
     grad_qkv(c, acc)
     st(1, 5)
     qkv_back()
+    need("tok", "vs", "e", "dz")
+    vsum[9:11, 0:512] = vs[9:11, :]
     norm_back(tok, 0, dx, None, 0)
     dh[0:512 - ROWS, :] = jnp.zeros((512 - ROWS, 768), f32)
     tgs = [pltpu.make_async_copy(dx, tg_ref.at[0:ROWS], tsem.at[0]), pltpu.make_async_copy(dh.at[0:512 - ROWS], tg_ref.at[ROWS:512], tsem.at[1])]
@@ -722,60 +848,95 @@
             of1_ref[:, h * 1536 + u * LW:h * 1536 + (u + 1) * LW] = fo[h, 24 + 6 * u:30 + 6 * u, :]
         of2_ref[:, h * LW:(h + 1) * LW] = fo[h, 48:72, :]
         od_ref[:, h * 256:(h + 1) * 256] = fo[h, 72:78, 0:256]
-    ov_ref[...] = fo[0, 72:78, 256:384]
+    vt[0:6, :] = fo[0, 72:78, 256:384]
+    vrows = vt[...].T
+    for i, r in enumerate((v0_ref, v1_ref, v2_ref, v3_ref, v4_ref)):
+        r[...] = vrows[i:i + 1, 0:6]
+    for q in range(4):
+        vf_ref[:, 6 * q:6 * q + 6] = vrows[5 + q:6 + q, 0:6]
+    vd_ref[...] = vrows[9:10, 0:4]
+    vm_ref[...] = vrows[10:11, 0:4]
+    finish_cells()
     for t in tgs: t.wait()
     for cp, rc in lasts: cp.wait_send()
     for cp in sends.values(): cp.wait_send()
 
 
-def k2_call(lens, g, g2, rows, tok, a, qkv, pr, o, x2, h2, act, dact, e, pos, dc):
+def k2_call(*args):
     nk = sum(len(c) for c in ag_chunks())
     S = jax.ShapeDtypeStruct
     vm = pl.BlockSpec(memory_space=pltpu.VMEM)
     anyspec = pl.BlockSpec(memory_space=pl.ANY)
     V, DMA = pltpu.VMEM, pltpu.SemaphoreType.DMA
-    outs = (S((512, 768), f32), S((6, 2304), f32), S((6, 768), f32), S((6, 3072), f32), S((24, 768), f32), S((6, 512), f32), S((6, 128), f32))
+    outs = (S((512, 768), f32), S((33, 64, 512), bf16), S((6, 2304), f32), S((6, 768), f32), S((6, 3072), f32), S((24, 768), f32),
+            S((6, 512), f32)) + (S((1, 6), f32),) * 5 + (S((1, 24), f32), S((1, 4), f32), S((1, 4), f32))
     return pl.pallas_call(
         k2_kernel,
         out_shape=outs,
-        in_specs=[pl.BlockSpec(memory_space=pltpu.SMEM), anyspec, anyspec] + [vm] * 4 + [anyspec] + [vm] * 7 + [anyspec] + [vm] * 3,
-        out_specs=[anyspec] + [vm] * 6,
+        in_specs=[anyspec] * 18 + [vm] * 3,
+        out_specs=[anyspec] * 2 + [vm] * 13,
         scratch_shapes=[
-            V((2, 4, 4, 48, LW), bf16), V((2, 4, 4, 192, LW), bf16), V((2, 4, 4, 4, 48, LW), bf16),
+            V((8, 3072), f32), V((ROWS, 768), bf16), V((ROWS, 2304), bf16), V((ROWS, 768), bf16), V((ROWS, 768), f32),
+            V((ROWS, 768), bf16), V((ROWS, 3072), bf16), V((ROWS, 3072), bf16), V((ROWS, 768), bf16), V((ROWS, 512), bf16),
+            V((ROWS, 768), f32), V((ROWS, 768), bf16), V((16, 512), f32), V((ROWS, 768), bf16),
+            V((2, 4, 4, 192, LW), bf16), V((2, 4, 4, 4, 48, LW), bf16),
             V((4, 4, 4, 48, LW), bf16), V((4, 4, 192, LW), bf16), V((1, 4, 4, 48, LW), bf16),
             V((9, 4, 4, 48, LW), bf16), V((4, 4, 192, LW), bf16),
             V((9, 4, 4, 48, LW), bf16), V((4, 4, 192, LW), bf16),
             V((3, 9, 4, 48, LW), bf16), V((3, 4, 192, LW), bf16),
             V((3, 9, 48, LW), bf16), V((3, 192, LW), bf16),
-            V((ROWS, 512), bf16), V((ROWS, 768), f32), V((ROWS, 768), f32), V((ROWS, 768), bf16), V((ROWS, 3072), bf16),
-            V((ROWS, 2304), bf16), V((16, 3072), f32), V((2, 2, ROWS, ROWS), bf16), V((2, 4, 64, 512), bf16),
-            V((8, SROWS, LW), bf16), V((8, SROWS, LW), bf16), V((2, SROWS, LW), f32),
-            DMA((nk, 9)), DMA((nk, 9)), DMA((7,)), DMA((7,)), DMA(()), DMA((4,)), DMA((2,)), DMA((2,)), DMA((2,)),
+            V((ROWS, 768), f32), V((ROWS, 3072), bf16), V((ROWS, 2304), bf16), V((16, 3072), f32), V((2, 2, ROWS, ROWS), bf16),
+            V((8, SROWS, LW), bf16), V((8, SROWS, LW), bf16), V((2, SROWS, LW), f32), V((64, 512), bf16), V((128, 128), f32),
+            DMA((nk, 9)), DMA((nk, 9)), DMA((7,)), DMA((7,)), DMA(()), DMA((1,)), DMA((2,)), DMA((2,)), DMA((16,)),
+            DMA((32,)), DMA((32,)), DMA((3,)),
         ],
         compiler_params=pltpu.CompilerParams(collective_id=1, has_side_effects=True, vmem_limit_bytes=60 * 2**20),
         cost_estimate=pl.CostEstimate(flops=12 * 10**9, bytes_accessed=5 * 10**7, transcendentals=0),
         name="backward",
-    )(lens, g, g2, rows, tok, a, qkv, pr, o, x2, h2, act, dact, e, pos, dc,
-      jnp.asarray(perm_matrix().T, bf16), jnp.asarray(cell_spread(), bf16), jnp.asarray(quad_spread(), bf16))
+    )(*args, jnp.asarray(perm_matrix().T, bf16), jnp.asarray(cell_spread(), bf16), jnp.asarray(fc1_bias_spread(), bf16))
+
+
+def k3_kernel(inv, arr, tg, *refs):
+    n = len(refs) - 3
+    small, (grid, tg_out, *outs), (gv, tv, sem) = refs[:13], refs[13:n], refs[n:]
+    ins = [pltpu.make_async_copy(tg, tv, sem.at[0])]
+    ins += [pltpu.make_async_copy(arr.at[inv[0, r]], gv.at[r], sem.at[1 + r]) for r in range(32)]
+    for cp in ins: cp.start()
+    for a, b in zip(small, outs): b[...] = a[...]
+    back = [pltpu.make_async_copy(tv, tg_out, sem.at[33])]
+    back += [pltpu.make_async_copy(gv.at[pl.ds(8 * i, 8)], grid.at[pl.ds(8 * i, 8)], sem.at[34 + i]) for i in range(4)]
+    ins[0].wait()
+    back[0].start()
+    for i in range(4):
+        for r in range(8): ins[1 + 8 * i + r].wait()
+        back[1 + i].start()
+    for cp in back: cp.wait()
+
+
+def k3_call(inv, arr, tg, *small):
+    S = jax.ShapeDtypeStruct
+    vm = pl.BlockSpec(memory_space=pltpu.VMEM)
+    anyspec = pl.BlockSpec(memory_space=pl.ANY)
+    return pl.pallas_call(
+        k3_kernel,
+        out_shape=(S((32, 64, 512), bf16), S((512, 768), f32)) + tuple(S(t.shape, t.dtype) for t in small),
+        in_specs=[pl.BlockSpec(memory_space=pltpu.SMEM), anyspec, anyspec] + [vm] * 13,
+        out_specs=[anyspec, anyspec] + [vm] * 13,
+        scratch_shapes=[pltpu.VMEM((32, 64, 512), bf16), pltpu.VMEM((512, 768), f32), pltpu.SemaphoreType.DMA((38,))],
+        name="results",
+    )(inv, arr, tg, *small)
 
 
 def body(tokens, chip_lengths, chip_ids, positions, ln1_gain, ln1_bias, qkv_weight, out_weight, ln2_gain, ln2_bias, fc1_weight,
          fc1_bias, fc2_weight, fc2_bias, dec_weight, dec_bias, mask_token, grid_cotangent):
-    n = lax.axis_size("fsdp")
-    tags = jnp.broadcast_to(chip_ids.astype(bf16)[None], (n, 2))
-    owner = lax.all_to_all(tags, "fsdp", split_axis=0, concat_axis=0).reshape(32).astype(jnp.int32)
-    placement = (jnp.arange(32, dtype=jnp.int32)[:, None] == owner[None, :]).astype(bf16)
-    back = lax.dot_general(placement, grid_cotangent.reshape(32, -1), TN, preferred_element_type=f32).astype(bf16)
-    cots = lax.all_to_all(back.reshape(16, 2, 64, 512), "fsdp", split_axis=0, concat_axis=0)
-    vec = pack_vec(ln1_gain, ln1_bias, ln2_gain, ln2_bias, fc2_bias, fc1_bias, dec_bias, mask_token)
-    pos = positions.reshape(1, 512)
-    *saved, cells = k1_call(tokens, chip_lengths, pos, vec, qkv_weight, out_weight, fc1_weight, fc2_weight, dec_weight)
-    g, g2, rows, *acts = saved
-    arrived = lax.all_to_all(cells, "fsdp", split_axis=0, concat_axis=0)
-    tg, dq, do, df1, df2, dd, dv = k2_call(chip_lengths, g, g2, rows, tokens, *acts, pos, cots)
-    grid = jnp.dot(placement, arrived.reshape(32, -1), preferred_element_type=f32).astype(bf16).reshape(32, 64, 512)
-    return (grid, tg, dv[:, 0], dv[:, 1], dq, do, dv[:, 2], dv[:, 3], df1, dv[:, 5:9].reshape(24), df2, dv[:, 4], dd,
-            dv[:4, 9], dv[:4, 10])
+    row = lambda v: v.reshape(1, -1)
+    *saved, inv = k1_call(chip_ids, chip_lengths, row(positions), tokens, row(ln1_gain), row(ln1_bias), qkv_weight, out_weight,
+                          row(ln2_gain), row(ln2_bias), fc1_weight, row(fc1_bias), fc2_weight, row(fc2_bias), dec_weight,
+                          row(dec_bias), row(mask_token), grid_cotangent)
+    tg, arrived, *small = k2_call(*saved, tokens)
+    grid, tg, dq, do, df1, df2, dd, *v = k3_call(inv, arrived, tg, *small)
+    v = [t.reshape(-1) for t in v]
+    return (grid, tg, v[0], v[1], dq, do, v[2], v[3], df1, v[5], df2, v[4], dd, v[6], v[7])
 
 
 def solution(mesh):

time: 293 us -> 219 us (0.75)
  waiting for transfers between devices: 43.6 us -> 0 us
  local copies, waits for them, and re-layouts: 27 us -> 0 us
  Pallas kernels: 199 us -> 218 us
  starting transfers between devices: 18.1 us -> 0 us
  matrix products: 3.04 us -> 0 us
    all_to_all x3 -> x0, waiting for transfers between devices: 43.6 us -> none  [the longest x1 24.2 us: body(): lax.all_to_all(back.reshape(16, 2, 64, 512), 'fsdp', split_axis=0, concat...]
    pallas_call x2 -> x3, Pallas kernels: 199 us -> 218 us  [the longest x1 107 us: k1_call(): pl.pallas_call(k1_kernel, out_shape=outs, in_specs=[smem, smem] + [vm] *...]
    all_to_all x3 -> x0, starting transfers between devices: 18.1 us -> none  [the longest x1 6.91 us: body(): lax.all_to_all(tags, 'fsdp', split_axis=0, concat_axis=0).reshape(32)]
    unnamed x20 -> x0, local copies, waits for them, and re-layouts: 15.1 us -> none
    broadcast_in_dim x10 -> x0, local copies, waits for them, and re-layouts: 5.91 us -> none  [the longest x2 0.77 us: pack_vec(): jnp.pad(mask, (0, 2))[:, None]]
    slice x3 -> x0, local copies, waits for them, and re-layouts: 3.85 us -> none  [the longest x1 1.62 us: body(): dv[:, 4]]
    dot_general x2 -> x0, matrix products: 3.04 us -> none  [the longest x1 2.35 us: body(): lax.dot_general(placement, grid_cotangent.reshape(32, -1), TN, preferred_...]
  transfers between devices with their start and end apart: 3 -> 0, of which waited for: 2 -> 0; matrix products, arithmetic and copies ran while one was open for 7% -> 0% of each run, Pallas kernels for 33% -> 0%
where the time goes in v3:
time: 219 us; the launch traced here: 218 us
  Pallas kernels  218 us (100%)
    pallas_call x1, Pallas kernels, k1_call(): pl.pallas_call(k1_kernel, out_shape=outs, in_specs=[smem, smem] + [vm] *...  107 us
    pallas_call x1, Pallas kernels, k2_call(): pl.pallas_call(k2_kernel, out_shape=outs, in_specs=[anyspec] * 18 + [vm]...  105 us
    pallas_call x1, Pallas kernels, k3_call(): pl.pallas_call(k3_kernel, out_shape=(S((32, 64, 512), bf16), S((512, 768)...  5.37 us

profile of v3, /device:TPU:1, one launch (start us, length us, event | category | flops | bytes accessed | tf_op | source)
XLA Modules:
  0.0 218.4 jit_solution(6247338341698189114)
XLA Ops:
  0.7 107.1 %forward.1 = (bf16[2,9,4,4,48,384]{5,4,3,2,1,0:T(8,128)(2,1)}, bf16[2,4,4,192,384]{4,3,2,1,0:T(8,128)(2,1)}, f32[8,3072]{1,0:T(8,128)}, bf16[336,768]{1,0:T(8,12...) custom-call(s32[2]{0:T(128)} %ids.1, s32[2]{0:T(128)} %lens.1, ...), custom_call_target="tpu_custom_call" | custom-call | flops 6000000000 | bytes 50000000 | tf_op jit(solution)/shard_map/forward/pallas_call | solution.py:471
  107.8 105.1 %backward.1 = (f32[512,768]{1,0:T(8,128)}, bf16[33,64,512]{2,1,0:T(8,128)(2,1)}, f32[6,2304]{1,0:T(8,128)}, f32[6,768]{1,0:T(8,128)}, f32[6,3072]{1,0:T(8,128)},...) custom-call(bf16[2,9,4,4,48,384]{5,4,3,2,1,0:T(8,128)(2,1)} %get-tup, ...), custom_call_target="tpu_custom_call" | custom-call | flops 12000000000 | bytes 50000000 | tf_op jit(solution)/shard_map/backward/pallas_call | solution.py:873
  212.9 5.4 %results.1 = (bf16[32,64,512]{2,1,0:T(8,128)(2,1)}, f32[512,768]{1,0:T(8,128)}, f32[6,2304]{1,0:T(8,128)}, f32[6,768]{1,0:T(8,128)}, f32[6,3072]{1,0:T(8,128)}, ...) custom-call(s32[8,128]{1,0:T(8,128)} %get-tuple-element.63.inv, ...), custom_call_target="tpu_custom_call" | custom-call | tf_op jit(solution)/shard_map/results/pallas_call | solution.py:920

commit v4 on v3

--- a/solution.py
+++ b/solution.py
@@ -8,7 +8,8 @@
 
 MESH = pl.DeviceIdType.MESH
 LW = 384
-SROWS = 80
+SROWS = 96
+YROWS = 64
 
 def coords():
     dp = lax.axis_index("dp"); fs = lax.axis_index("fsdp")
@@ -21,27 +22,34 @@
 def dev(z, x, y, c):
     return (z * 2 + x // 2, (x % 2) * 8 + y * 2 + c)
 
+UNIT_ROWS = (32, 38, 44, 50, 0, 6, 12, 18, 56)
+FC2_ROWS = 64
+
+
 def perm_matrix():
-    m = np.zeros((624, 640), np.float32)
-    for d in range(8):
-        for u in range(8):
+    m = np.zeros((432, 512), np.float32)
+    for u, base in enumerate(UNIT_ROWS):
+        for d in range(8):
             for j in range(6):
-                m[48 * u + 6 * d + j, d * 80 + 6 * u + j] = 1
-        for j in range(6):
-            m[48 * 8 + 6 * d + j, d * 80 + 72 + j] = 1
-        for i in range(24):
-            m[432 + 24 * d + i, d * 80 + 48 + i] = 1
+                m[48 * u + 6 * d + j, d * 64 + base + j] = 1
     return m
 
+
+def spread_matrix(units, first):
+    m = perm_matrix().reshape(9, 48, 8, 64)[list(units), :, :, first:first + 32]
+    return m.reshape(48 * len(units), 256).T
+
+
 ALL = slice(None)
 
-def ag_chunks():
-    return [
-        [("g", "zx", (0, 2), (0, 1), (1, 2)), ("g", "xz", (2, 4), (2, 3), (3, 4))],
-        [("g", "zx", (4, 6), (4, 5), (5, 6)), ("g", "xz", (6, 8), (6, 7), (7, 8))],
-        [("g2", "zx", (0, 96), (0, 48), (48, 96)), ("g2", "xz", (96, 192), (96, 144), (144, 192))],
-        [("g", "zx", (8, 9), (8, 9), None)],
-    ]
+
+def ring_places(z, x, y, c):
+    out = {}
+    for name, v in (("z", z), ("x", x), ("y", y)):
+        at = {0: v, 1: (v + 1) % 4, -1: (v + 3) % 4, 2: (v + 2) % 4}
+        to = {k: dev(*(at[k] if n == name else w for n, w in (("z", z), ("x", x), ("y", y))), c) for k in (1, -1)}
+        out[name] = (at, to)
+    return out
 
 
 ROWS = 336
@@ -90,20 +98,19 @@
 
 
 def k1_kernel(ids, lens, pos, tok, l1g, l1b, qkv_s, out_s, l2g, l2b, fc1_s, fc1b, fc2_s, fc2b, dec_s, decb, maskt, cot_hbm,
-              p_ref, m2_ref, m4_ref,
+              p1_ref, p2_ref, m2_ref, m4_ref,
               g_hbm, g2_hbm, rows_hbm, a_hbm, qkv_hbm, p_hbm, o_hbm, x2_hbm, h2_hbm, act_hbm, dact_hbm, e_hbm, cells_hbm,
               dz_hbm, dx_hbm, dm_hbm, vs_hbm, inv_hbm,
               g_ref, g2_ref, rows_ref, a_ref, qkv_ref, p_out, o_ref, x2_ref, h2_ref, act_ref, dact_ref, e_ref, cells_ref,
               dz, dx, dm, vs, inv,
-              sp, s_ref, s1, z_ref, vrow, tag, tags, idv, idm, cot, cotsend, dc, hits,
+              sp, s_ref, s1, s2, z_ref, vrow, tag, tags, idv, idm, cot, cotsend, dc, hits,
               ss1, rs1, loc, ssem, rsem, wsem, osem, tss, tsr, bss, bsr, mss, msr, lsem):
     z, x, y, c = coords()
     dp, f = lax.axis_index("dp"), lax.axis_index("fsdp")
-    zp, zm, zo = (z + 1) % 4, (z + 3) % 4, (z + 2) % 4
-    xp, xm, xo = (x + 1) % 4, (x + 3) % 4, (x + 2) % 4
     o = 1 - c
     bar = pltpu.get_barrier_semaphore()
-    targets = [dev(zp, x, y, c), dev(zm, x, y, c), dev(z, xp, y, c), dev(z, xm, y, c)]
+    rings = ring_places(z, x, y, c)
+    targets = [rings[a][1][d] for a in "zx" for d in (1, -1)]
     group = []
     for dy in range(4):
         for dc_ in range(2):
@@ -117,12 +124,14 @@
     sp[...] = jnp.zeros_like(sp)
     for h in range(2):
         for u in range(3):
-            sp[h, 6 * u:6 * u + 6, :] = qkv_s[:, h * 1152 + u * LW:h * 1152 + (u + 1) * LW].astype(f32)
-        sp[h, 18:24, :] = out_s[:, h * LW:(h + 1) * LW].astype(f32)
+            for b in range(3):
+                first = 768 * b + 128 * (3 * h + u)
+                sp[h, 32 + 6 * u:38 + 6 * u, 128 * b:128 * b + 128] = qkv_s[:, first:first + 128].astype(f32)
+        sp[h, 50:56, :] = out_s[:, h * LW:(h + 1) * LW].astype(f32)
         for u in range(4):
-            sp[h, 24 + 6 * u:30 + 6 * u, :] = fc1_s[:, h * 1536 + u * LW:h * 1536 + (u + 1) * LW].astype(f32)
-        sp[h, 48:72, :] = fc2_s[:, h * LW:(h + 1) * LW].astype(f32)
-        sp[h, 72:78, 0:256] = dec_s[:, h * 256:(h + 1) * 256].astype(f32)
+            sp[h, 6 * u:6 * u + 6, :] = fc1_s[:, h * 1536 + u * LW:h * 1536 + (u + 1) * LW].astype(f32)
+        sp[h, 64:88, :] = fc2_s[:, h * LW:(h + 1) * LW].astype(f32)
+        sp[h, 56:62, 0:256] = dec_s[:, h * 256:(h + 1) * 256].astype(f32)
     vrow[...] = jnp.zeros_like(vrow)
     for i, r in enumerate((l1g, l1b, l2g, l2b, fc2b)):
         vrow[i:i + 1, 0:6] = r[...].astype(f32)
@@ -130,7 +139,7 @@
         vrow[5 + q:6 + q, 0:6] = fc1b[:, 6 * q:6 * q + 6].astype(f32)
     vrow[9:10, 0:4] = decb[...].astype(f32)
     vrow[10:11, 0:4] = maskt[...].astype(f32)
-    sp[0, 72:78, 256:384] = vrow[...].T[0:6]
+    sp[0, 56:62, 256:384] = vrow[...].T[0:6]
     s_ref[...] = sp[...].astype(bf16)
     first_small = lens[0] < lens[1]
     trow = lax.broadcasted_iota(jnp.int32, (8, 128), 0)
@@ -138,41 +147,47 @@
     pl.semaphore_wait(bar, len(greeted))
 
     me = 2 * y + c
-    own = pltpu.make_async_copy(s_ref.at[c], s1.at[me], loc)
-    own.start()
+    sib = dev(z, x, y, o)
+    mate = pltpu.make_async_remote_copy(s_ref.at[o, YROWS:SROWS], s2, ss1.at[2, 0], rs1.at[2, 0], device_id=sib, device_id_type=MESH)
+    mate.start()
     firsts = []
-    for i, (dy, dc_, t) in enumerate(group):
-        cp = pltpu.make_async_remote_copy(s_ref.at[(c + dc_) % 2], s1.at[me], ss1.at[i], rs1.at[i], device_id=t, device_id_type=MESH)
-        cp.start()
-        src = 2 * ((y + 4 - dy) % 4) + (c + dc_) % 2
-        rc = pltpu.make_async_remote_copy(s_ref.at[c], s1.at[src], ss1.at[i], rs1.at[i], device_id=t, device_id_type=MESH)
-        firsts.append((cp, rc))
-
+    for j, rows in enumerate((slice(32, 64), slice(0, 32))):
+        own = pltpu.make_async_copy(s_ref.at[c, rows], s1.at[me, rows], loc.at[j])
+        own.start()
+        got = []
+        for i, (dy, dc_, t) in enumerate(group):
+            cp = pltpu.make_async_remote_copy(s_ref.at[(c + dc_) % 2, rows], s1.at[me, rows], ss1.at[j, i], rs1.at[j, i], device_id=t, device_id_type=MESH)
+            cp.start()
+            src = 2 * ((y + 4 - dy) % 4) + (c + dc_) % 2
+            rc = pltpu.make_async_remote_copy(s_ref.at[c, rows], s1.at[src, rows], ss1.at[j, i], rs1.at[j, i], device_id=t, device_id_type=MESH)
+            got.append((cp, rc))
+        firsts.append((own, got))
+    def shards(j):
+        own, got = firsts[j]
+        own.wait()
+        for _, rc in got: rc.wait_recv()
     tagged = []
     tags[f] = tag[...]
     for r, g in peers(f):
         cp = pltpu.make_async_remote_copy(tag, tags.at[f], tss.at[r], tsr.at[r], device_id=(dp, g), device_id_type=MESH)
         cp.start(); tagged.append(cp)
-    for r, g in peers(f):
-        src = (f + 16 - r) % 16
-        pltpu.make_async_remote_copy(tag, tags.at[src], tss.at[r], tsr.at[r], device_id=(dp, g), device_id_type=MESH).wait_recv()
-    for s in range(16):
-        idv[s:s + 1, :] = tags[s, 0:1, :]
-        idv[16 + s:17 + s, :] = tags[s, 1:2, :]
-    ld_ids = pltpu.make_async_copy(idv, idm, lsem.at[1])
-    ld_ids.start()
-    srow = lax.broadcasted_iota(jnp.int32, (32, 128), 0)
-    hit = idv[...] == lax.broadcasted_iota(jnp.int32, (32, 128), 1)
-    place_of = jnp.where((srow >= 16) & (f >= 4), 32, srow)
-    inv[...] = jnp.broadcast_to(jnp.sum(jnp.where(hit, place_of, 0), axis=0, keepdims=True), (8, 128))
-    ld_ids.wait()
-    ld_cot.wait()
-    for s in range(32):
-        cotsend[s] = cot[idm[s, 0]]
-
-    own.wait()
-    for cp, rc in firsts:
-        rc.wait_recv()
+    def sort_cotangents():
+        for r, g in peers(f):
+            src = (f + 16 - r) % 16
+            pltpu.make_async_remote_copy(tag, tags.at[src], tss.at[r], tsr.at[r], device_id=(dp, g), device_id_type=MESH).wait_recv()
+        for s in range(16):
+            idv[s:s + 1, :] = tags[s, 0:1, :]
+            idv[16 + s:17 + s, :] = tags[s, 1:2, :]
+        ld_ids = pltpu.make_async_copy(idv, idm, lsem.at[1])
+        ld_ids.start()
+        srow = lax.broadcasted_iota(jnp.int32, (32, 128), 0)
+        hit = idv[...] == lax.broadcasted_iota(jnp.int32, (32, 128), 1)
+        place_of = jnp.where((srow >= 16) & (f >= 4), 32, srow)
+        inv[...] = jnp.broadcast_to(jnp.sum(jnp.where(hit, place_of, 0), axis=0, keepdims=True), (8, 128))
+        ld_ids.wait()
+        ld_cot.wait()
+        for s in range(32):
+            cotsend[s] = cot[idm[s, 0]]
 
     few = f < 4
     def to_peer(i, g):
@@ -211,72 +226,77 @@
             for r, g in peers(f):
                 small_to_peer(r, g).wait_send()
 
-    def relay(lo, hi):
-        flat = s1[...].reshape(640, LW)
-        r = jnp.dot(p_ref[lo:hi, :], flat, preferred_element_type=f32)
+    def relay(perm, rows, lo, hi):
+        flat = s1[:, rows].reshape(256, LW)
+        r = jnp.dot(perm[lo:hi, :], flat, preferred_element_type=f32)
         return r.astype(bf16)
 
     def place(p):
-        if p == 0: g_ref[c, 0:4, z, x] = relay(0, 192).reshape(4, 48, LW)
-        if p == 1: g_ref[c, 4:8, z, x] = relay(192, 384).reshape(4, 48, LW)
-        if p == 2: g2_ref[c, z, x] = relay(432, 624)
-        if p == 3: g_ref[c, 8, z, x] = relay(384, 432)
-
-    def view(arr, h, part, zs, xs):
-        if arr == "g":
-            return g_ref.at[h, part[0]:part[1], zs, xs]
-        return g2_ref.at[h, zs, xs, part[0]:part[1]]
+        if p == 0: g_ref[c, 0:4, z, x] = relay(p2_ref, slice(32, 64), 0, 192).reshape(4, 48, LW)
+        if p == 1: g_ref[c, 4:8, z, x] = relay(p1_ref, slice(0, 32), 0, 192).reshape(4, 48, LW)
+        if p == 2:
+            mate.wait_recv()
+            both = [s_ref[c, YROWS:SROWS].astype(f32)[0:24], s2[...].astype(f32)[0:24]]
+            both = [jnp.where(c == k, both[0], both[1]) for k in range(2)]
+            g2_ref[c, z, x, y] = jnp.concatenate(both, axis=0).astype(bf16)
+        if p == 3: g_ref[c, 8, z, x] = relay(p2_ref, slice(32, 64), 192, 240)
 
     sends = []
-    def mk(k, i, src, dst, to):
-        return pltpu.make_async_remote_copy(src, dst, ssem.at[k, i], rsem.at[k, i], device_id=to, device_id_type=MESH)
+    def mk(k, i, v, to):
+        return pltpu.make_async_remote_copy(v, v, ssem.at[k, i], rsem.at[k, i], device_id=to, device_id_type=MESH)
     def send(k, i, v, to):
-        cp = mk(k, i, v, v, to); cp.start(); sends.append(cp)
+        cp = mk(k, i, v, to); cp.start(); sends.append(cp)
     def recv(k, i, v):
-        mk(k, i, v, v, dev(z, x, y, o)).wait_recv()
-
-    def steps(k, chunk):
-        arr, order, full, fa, fb = chunk
-        if order == "zx":
-            d1p, d1m, d2p, d2m = targets
-            p1, m1, o1, p2, m2, o2, s1_, s2_ = zp, zm, zo, xp, xm, xo, z, x
-            V = lambda part, a, b, h=c: view(arr, h, part, a, b)
-        else:
-            d2p, d2m, d1p, d1m = targets
-            p1, m1, o1, p2, m2, o2, s1_, s2_ = xp, xm, xo, zp, zm, zo, x, z
-            V = lambda part, a, b, h=c: view(arr, h, part, b, a)
-        sib = dev(z, x, y, o)
-        def st0():
-            send(k, 0, V(full, s1_, s2_), d1p)
-            send(k, 1, V(full, s1_, s2_), d1m)
-        def st1():
-            recv(k, 0, V(full, m1, s2_))
-            send(k, 2, V(fa, m1, s2_), d1p)
-            recv(k, 1, V(full, p1, s2_))
-            if fb is not None: send(k, 3, V(fb, p1, s2_), d1m)
-        def st2():
-            recv(k, 2, V(fa, o1, s2_))
-            if fb is not None: recv(k, 3, V(fb, o1, s2_))
-            send(k, 4, V(full, ALL, s2_), d2p)
-            send(k, 5, V(full, ALL, s2_), d2m)
-            send(k, 8, V(full, ALL, s2_), sib)
-        def st3():
-            recv(k, 4, V(full, ALL, m2))
-            send(k, 6, V(fa, ALL, m2), d2p)
-            send(k, 9, V(full, ALL, m2), sib)
-            recv(k, 5, V(full, ALL, p2))
-            if fb is not None: send(k, 7, V(fb, ALL, p2), d2m)
-            send(k, 10, V(full, ALL, p2), sib)
-        def st4():
-            recv(k, 6, V(fa, ALL, o2))
-            if fb is not None: recv(k, 7, V(fb, ALL, o2))
-            send(k, 11, V(full, ALL, o2), sib)
-        def st5():
-            recv(k, 8, V(full, ALL, s2_, o))
-            recv(k, 9, V(full, ALL, m2, o))
-            recv(k, 10, V(full, ALL, p2, o))
-            recv(k, 11, V(full, ALL, o2, o))
-        return [st0, st1, st2, st3, st4, st5]
+        mk(k, i, v, sib).wait_recv()
+
+    def steps(k, axes, view, parts):
+        last = len(axes) - 1
+        def opposite(l):
+            at, _ = rings[axes[l]]
+            _, fa, fb = parts[l]
+            recv(k, 4 * l + 2, view(l, at[2], fa, c))
+            if fb is not None: recv(k, 4 * l + 3, view(l, at[2], fb, c))
+        def first(l):
+            at, to = rings[axes[l]]
+            full = parts[l][0]
+            if l: opposite(l - 1)
+            for i, d in enumerate((1, -1)): send(k, 4 * l + i, view(l, at[0], full, c), to[d])
+            if l == last: send(k, 12, view(l, at[0], full, c), sib)
+        def second(l):
+            at, to = rings[axes[l]]
+            full, fa, fb = parts[l]
+            recv(k, 4 * l, view(l, at[-1], full, c))
+            send(k, 4 * l + 2, view(l, at[-1], fa, c), to[1])
+            if l == last: send(k, 13, view(l, at[-1], full, c), sib)
+            recv(k, 4 * l + 1, view(l, at[1], full, c))
+            if fb is not None: send(k, 4 * l + 3, view(l, at[1], fb, c), to[-1])
+            if l == last: send(k, 14, view(l, at[1], full, c), sib)
+        def third():
+            at, _ = rings[axes[last]]
+            opposite(last)
+            send(k, 15, view(last, at[2], parts[last][0], c), sib)
+        def fourth():
+            at, _ = rings[axes[last]]
+            for i, d in enumerate((0, -1, 1, 2)): recv(k, 12 + i, view(last, at[d], parts[last][0], o))
+        out = []
+        for l in range(last + 1):
+            out += [functools.partial(first, l), functools.partial(second, l)]
+        return out + [third, fourth]
+
+    def unit_chunk(k, axes, *parts):
+        def view(l, at, part, h):
+            u0, u1, l0, l1 = part
+            zs, xs = [(z, at), (at, ALL)][l] if axes == "xz" else [(at, x), (ALL, at)][l]
+            return g_ref.at[h, u0:u1, zs, xs, :, l0:l1]
+        return steps(k, axes, view, [parts, parts])
+    def fc2_chunk(k):
+        def view(l, at, part, h):
+            a, b = part
+            if l == 0: return g2_ref.at[h, z, at, y, a:b]
+            if l == 1: return g2_ref.at[h, at, a:b, y]
+            return g2_ref.at[h, a:b, :, at]
+        ring = ((0, 4), (0, 2), (2, 4))
+        return steps(k, "xzy", view, [((0, 48), (0, 32), (32, 48)), ring, ring])
 
     outs = []
     def to_hbm(p):
@@ -329,9 +349,7 @@
         same = seg((ROWS, 1), 0) == seg((1, ROWS), 1)
         bias = jnp.where(same, 0.0, -1e30)
         def pair(i, _):
-            def cols(base):
-                return qkv_ref[:, pl.ds(pl.multiple_of(base + i * 128, 128), 128)]
-            q, k, v = cols(0), cols(768), cols(1536)
+            q, k, v = (qkv_ref[:, pl.ds(pl.multiple_of(LW * i + 128 * b, 128), 128)] for b in range(3))
             outs_ = []
             for t in range(2):
                 keep = low if t == 0 else jnp.logical_not(low)
@@ -355,7 +373,7 @@
             h2_ref[r, :] = (n * rows_ref[2:3, 0:768] + rows_ref[3:4, 0:768]).astype(bf16)
         blocks(body)
 
-    def fc1():
+    def fc1(first):
         for h in range(2):
             def unit(u, _):
                 cs = pl.ds(pl.multiple_of(h * 1536 + u * LW, LW), LW)
@@ -364,7 +382,7 @@
                 act_ref[:, cs] = g.astype(bf16)
                 dact_ref[:, cs] = dg.astype(bf16)
                 return 0
-            lax.fori_loop(0, 4, unit, 0)
+            lax.fori_loop(first, first + 2, unit, 0)
 
     def fc2():
         for h in range(2):
@@ -424,46 +442,67 @@
 
     vs[...] = jnp.zeros_like(vs)
     rows_ref[...] = jnp.zeros_like(rows_ref)
-    after = {
-        0: [send_cotangents, lambda: keep("inv"), fills],
-        5: [rows_of, ln1, lambda: keep("rows", "a")],
-        6: [qkv, lambda: attention(0, 3), lambda: keep("qkv")],
-        7: [lambda: attention(3, 6), out_proj, lambda: keep("p", "o", "x2", "h2"), fc1, lambda: keep("act", "dact"), cell_grads,
-            lambda: keep("dz", "dx", "dm", "vs")],
-        8: [fc2, lambda: keep("e"), dec, lambda: keep("cells")],
+    half = lambda u: ((u, u + 2, 0, LW), (u, u + 1, 0, LW), (u + 1, u + 2, 0, LW))
+    pieces = {
+        3: [unit_chunk(0, "xz", (8, 9, 0, LW), (8, 9, 0, 256), (8, 9, 256, LW))],
+        2: [fc2_chunk(1)],
+        0: [unit_chunk(2, "xz", *half(0)), unit_chunk(3, "zx", *half(2))],
+        "1a": [unit_chunk(4, "xz", *half(4))],
+        "1b": [unit_chunk(5, "zx", *half(6))],
     }
-    order = PIECE_ORDER
-    pieces = [None] * 4
-    k = 0
-    for p, cl in enumerate(ag_chunks()):
-        lst = []
-        for ch in cl:
-            lst.append(steps(k, ch)); k += 1
-        pieces[p] = lst
-    for t in range(len(pieces) + 5):
-        for pos_, p in enumerate(order):
-            s = t - pos_
-            if s == 0: place(p)
-            if 0 <= s < 6:
-                for ch in pieces[p]: ch[s]()
-            if s == 5: to_hbm(p)
-        for fn in after.get(t, []): fn()
-    for cp, rc in firsts: cp.wait_send()
+    def go(step, *names):
+        for p in names:
+            for ch in pieces[p]: ch[step]()
+    place(2); go(0, 2)
+    shards(0)
+    place(3); place(0); go(0, 0, 3)
+    go(1, 2, 0, 3)
+    shards(1)
+    place(1); go(0, "1a", "1b")
+    go(2, 0, 3, 2)
+    sort_cotangents(); keep("inv")
+    go(1, "1a", "1b")
+    go(3, 2, 0, 3)
+    go(2, "1a", "1b")
+    go(4, 2)
+    send_cotangents()
+    fills()
+    go(4, 0, 3)
+    go(5, 3); to_hbm(3)
+    rows_of(); ln1(); keep("rows", "a")
+    go(5, 0); to_hbm(0)
+    qkv(); keep("qkv")
+    go(3, "1a", "1b")
+    go(5, 2)
+    attention(0, 3)
+    go(4, "1a", "1b")
+    attention(3, 6)
+    keep("p")
+    go(6, 2)
+    out_proj(); keep("o", "x2", "h2")
+    cell_grads(); keep("dz", "dx", "dm", "vs")
+    go(5, "1a"); fc1(0)
+    go(5, "1b"); to_hbm(1)
+    fc1(2); keep("act", "dact")
+    go(7, 2); to_hbm(2)
+    fc2(); keep("e")
+    dec(); keep("cells")
+    for _, got in firsts:
+        for cp, _ in got: cp.wait_send()
     for cp in sends: cp.wait_send()
+    mate.wait_send()
     for cp in tagged: cp.wait_send()
     finish_cotangents()
     for cp in outs: cp.wait()
 
-PIECE_ORDER = [3, 0, 1, 2]
 
 def k1_call(*args):
-    nk = sum(len(c) for c in ag_chunks())
     S = jax.ShapeDtypeStruct
     vm, smem = pl.BlockSpec(memory_space=pltpu.VMEM), pl.BlockSpec(memory_space=pltpu.SMEM)
     anyspec = pl.BlockSpec(memory_space=pl.ANY)
     V, DMA = pltpu.VMEM, pltpu.SemaphoreType.DMA
     outs = (
-        S((2, 9, 4, 4, 48, LW), bf16), S((2, 4, 4, 192, LW), bf16), S((8, 3072), f32), S((ROWS, 768), bf16),
+        S((2, 9, 4, 4, 48, LW), bf16), S((2, 4, 4, 4, 48, LW), bf16), S((8, 3072), f32), S((ROWS, 768), bf16),
         S((ROWS, 2304), bf16), S((12, ROWS, ROWS), bf16), S((ROWS, 768), bf16), S((ROWS, 768), f32),
         S((ROWS, 768), bf16), S((ROWS, 3072), bf16), S((ROWS, 3072), bf16), S((ROWS, 768), bf16), S((20, 64, 512), bf16),
         S((ROWS, 512), bf16), S((ROWS, 768), f32), S((ROWS, 768), bf16), S((16, 512), f32), S((8, 128), jnp.int32),
@@ -471,51 +510,53 @@
     return pl.pallas_call(
         k1_kernel,
         out_shape=outs,
-        in_specs=[smem, smem] + [vm] * 15 + [anyspec] + [vm] * 3,
+        in_specs=[smem, smem] + [vm] * 15 + [anyspec] + [vm] * 4,
         out_specs=[anyspec] * 18,
         scratch_shapes=[V(t.shape, t.dtype) for t in outs] + [
-            V((2, SROWS, LW), f32), V((2, SROWS, LW), bf16), V((8, SROWS, LW), bf16), V((ROWS, 640), bf16), V((128, 128), f32),
+            V((2, SROWS, LW), f32), V((2, SROWS, LW), bf16), V((8, YROWS, LW), bf16), V((SROWS - YROWS, LW), bf16), V((ROWS, 640), bf16), V((128, 128), f32),
             V((8, 128), jnp.int32), V((16, 8, 128), jnp.int32), V((32, 128), jnp.int32), pltpu.SMEM((32, 128), jnp.int32),
             V((32, 64, 512), bf16), V((32, 64, 512), bf16), V((20, 64, 512), bf16), V((1280, ROWS), bf16),
-            DMA((7,)), DMA((7,)), DMA(()), DMA((nk, 12)), DMA((nk, 12)), DMA((4,)), DMA((16,)), DMA((16,)), DMA((16,)),
+            DMA((3, 7)), DMA((3, 7)), DMA((2,)), DMA((6, 16)), DMA((6, 16)), DMA((4,)), DMA((16,)), DMA((16,)), DMA((16,)),
             DMA((16,)), DMA((16,)), DMA((16,)), DMA((4,)), DMA((4,)),
         ],
         compiler_params=pltpu.CompilerParams(collective_id=0, has_side_effects=True, vmem_limit_bytes=60 * 2**20),
         cost_estimate=pl.CostEstimate(flops=6 * 10**9, bytes_accessed=5 * 10**7, transcendentals=0),
         name="forward",
-    )(*args, jnp.asarray(perm_matrix(), bf16), jnp.asarray(cell_spread(), bf16), jnp.asarray(fc1_bias_spread(), bf16))
+    )(*args, jnp.asarray(spread_matrix((4, 5, 6, 7), 0).T, bf16), jnp.asarray(spread_matrix((0, 1, 2, 3, 8), 32).T, bf16),
+      jnp.asarray(cell_spread(), bf16), jnp.asarray(fc1_bias_spread(), bf16))
 
 
 def k2_kernel(g_hbm, g2_hbm, rows_hbm, a_hbm, qkv_hbm, p_hbm, o_hbm, x2_hbm, h2_hbm, act_hbm, dact_hbm, e_hbm, cells_hbm,
-              dz_hbm, dx_hbm, dm_hbm, vs_hbm, tok_hbm, pt_ref, m2_ref, m4_ref,
+              dz_hbm, dx_hbm, dm_hbm, vs_hbm, tok_hbm, pt1_ref, pt2_ref, m2_ref, m4_ref,
               tg_ref, arr, oq_ref, oo_ref, of1_ref, of2_ref, od_ref, v0_ref, v1_ref, v2_ref, v3_ref, v4_ref, vf_ref, vd_ref, vm_ref,
               rows_ref, a_ref, qkv_ref, o_ref, x2_ref, h2_ref, act_ref, dact_ref, e_ref, dz, dx, dm, vs, tok,
-              wa, wb, sta, sta2, stc, sg, sg2, acc, acc2, xa, xa2, xb, xb2,
-              dh, df, dqkv, vsum, pb, fs, f1, fo, zb, vt,
-              ssem, rsem, ss1, rs1, loc, wsem, psem, tsem, isem, css, csr, csl):
+              wa, wb, sta, sta2, stc, sg, sg2, acc, acc2, xa, xa2, xb, xc, xd,
+              dh, df, dqkv, vsum, pb, fs, f1, fo, fs2, f2, zb, vt, vout, vin,
+              ssem, rsem, ss1, rs1, loc, wsem, psem, tsem, isem, css, csr, csl, vss, vrs):
     z, x, y, c = coords()
     dp, f = lax.axis_index("dp"), lax.axis_index("fsdp")
-    zp, zm, zo = (z + 1) % 4, (z + 3) % 4, (z + 2) % 4
-    xp, xm, xo = (x + 1) % 4, (x + 3) % 4, (x + 2) % 4
     o = 1 - c
     bar = pltpu.get_barrier_semaphore()
-    targets = [dev(zp, x, y, c), dev(zm, x, y, c), dev(z, xp, y, c), dev(z, xm, y, c)]
+    rings = ring_places(z, x, y, c)
+    targets = [rings[a][1][d] for a in "zx" for d in (1, -1)]
     sib = dev(z, x, y, o)
     group = []
     for dy in range(4):
         for dc in range(2):
             if dy or dc:
                 group.append((dy, dc, dev(z, x, (y + dy) % 4, (c + dc) % 2)))
-    greeted = targets + [(dp, g) for _, g in peers(f)]
+    plane = [(4 * dz_ + dx_, (z + dz_) % 4, (x + dx_) % 4, (z + 4 - dz_) % 4, (x + 4 - dx_) % 4)
+             for dz_ in range(4) for dx_ in range(4) if dz_ or dx_]
+    greeted = targets + [(dp, g) for _, g in peers(f)] + [dev(zz, xx, y, c) for _, zz, xx, _, _ in plane]
     greet(bar, greeted)
     loads = {}
     def load(name, src, dst):
         loads[name] = pltpu.make_async_copy(src, dst, isem.at[len(loads)])
         return loads[name]
     for name, src, dst in (
-        ("dm", dm_hbm, dm), ("act", act_hbm, act_ref), ("fc2", g2_hbm, wa), ("dact", dact_hbm, dact_ref), ("fc1", g_hbm.at[:, 4:8], wb),
+        ("dm", dm_hbm, dm), ("act", act_hbm, act_ref), ("e", e_hbm, e_ref), ("dz", dz_hbm, dz), ("fc2", g2_hbm, wa), ("dact", dact_hbm, dact_ref), ("fc1", g_hbm.at[:, 4:8], wb),
         ("h2", h2_hbm, h2_ref), ("x2", x2_hbm, x2_ref), ("dx", dx_hbm, dx), ("rows", rows_hbm, rows_ref), ("o", o_hbm, o_ref),
-        ("qkv", qkv_hbm, qkv_ref), ("e", e_hbm, e_ref), ("dz", dz_hbm, dz), ("a", a_hbm, a_ref), ("tok", tok_hbm.at[0:ROWS], tok),
+        ("qkv", qkv_hbm, qkv_ref), ("a", a_hbm, a_ref), ("tok", tok_hbm.at[0:ROWS], tok),
         ("vs", vs_hbm, vs),
     ):
         load(name, src, dst).start()
@@ -566,80 +607,136 @@
     def recv(k, i, v):
         pltpu.make_async_remote_copy(v, v, ssem.at[k, i], rsem.at[k, i], device_id=sib, device_id_type=MESH).wait_recv()
 
-    def steps(k, piece, chunk):
-        arr, order, full, fa, fb = chunk
-        zx = order == "zx"
-        if zx:
-            d1p, d1m, d2p, d2m = targets
-            p1, m1, o1, p2, m2, o2, s1_, s2_ = zp, zm, zo, xp, xm, xo, z, x
-        else:
-            d2p, d2m, d1p, d1m = targets
-            p1, m1, o1, p2, m2, o2, s1_, s2_ = xp, xm, xo, zp, zm, zo, x, z
-        def idx(part, a, b):
-            zs, xs = (a, b) if zx else (b, a)
-            r = pl.ds(part[0], part[1] - part[0])
-            return (r, zs, xs) if arr == "g" else (zs, xs, r)
-        A = acc if arr == "g" else acc2
-        SG = sg if arr == "g" else sg2
-        def stage(part):
-            if piece == 2: return sta2.at[:, :, pl.ds(part[0], part[1] - part[0])]
-            if piece == 3: return stc
-            u = 4 * piece
-            return sta.at[pl.ds(part[0] - u, part[1] - part[0])]
-        def xav(way, part):
-            r = slice(part[0], part[1])
-            return xa.at[way, r] if arr == "g" else xa2.at[way, :, r]
-        def xbv(way, part):
-            r = slice(part[0], part[1])
-            return xb.at[way, r] if arr == "g" else xb2.at[way, r]
-        def add(part, a, b, *recvd):
-            i = idx(part, a, b)
-            t = A[i].astype(f32)
-            for r in recvd: t = t + r[...].astype(f32)
-            A[i] = t.astype(bf16)
-        def st0():
-            send(k, 8, stage(full), SG.at[idx(full, ALL, ALL)], sib)
-        def st1():
-            recv(k, 8, SG.at[idx(full, ALL, ALL)])
-            def one(j, _):
-                i = idx(full, j, ALL)
-                A[i] = (A[i].astype(f32) + SG[i].astype(f32)).astype(bf16)
-                return 0
-            lax.fori_loop(0, 4, one, 0)
-            send(k, 0, A.at[idx(fa, ALL, o2)], xav(0, fa), d2p)
-            if fb is not None: send(k, 1, A.at[idx(fb, ALL, o2)], xav(0, fb), d2m)
-        def st2():
-            recv(k, 0, xav(0, fa)); add(fa, ALL, p2, xav(0, fa))
-            send(k, 2, A.at[idx(full, ALL, p2)], xav(1, full), d2p)
+    def steps(k, axes, ours, theirs, from_sib, inbox, parts):
+        last = len(axes) - 1
+        def add(v, *more):
+            t = v[...].astype(f32)
+            for m in more: t = t + m[...].astype(f32)
+            v[...] = t.astype(bf16)
+        def opposite(l):
+            at, to = rings[axes[l]]
+            _, fa, fb = parts[l]
+            send(k, 4 * l, ours(l, at[2], fa), inbox(l, 0, fa), to[1])
+            if fb is not None: send(k, 4 * l + 1, ours(l, at[2], fb), inbox(l, 0, fb), to[-1])
+        def start():
+            send(k, 12, theirs, from_sib, sib)
+        def join():
+            recv(k, 12, from_sib)
+            at, _ = rings[axes[last]]
+            for d in (2, 1, -1, 0):
+                add(ours(last, at[d], parts[last][0]), share(last, at[d]))
+                if d == 2: opposite(last)
+        def share(l, place):
+            return from_sib_view[k](place)
+        def near(l):
+            at, to = rings[axes[l]]
+            full, fa, fb = parts[l]
+            recv(k, 4 * l, inbox(l, 0, fa)); add(ours(l, at[1], fa), inbox(l, 0, fa))
+            send(k, 4 * l + 2, ours(l, at[1], full), inbox(l, 1, full), to[1])
             if fb is not None:
-                recv(k, 1, xav(0, fb)); add(fb, ALL, m2, xav(0, fb))
-            send(k, 3, A.at[idx(full, ALL, m2)], xav(2, full), d2m)
-        def st3():
-            recv(k, 2, xav(1, full)); recv(k, 3, xav(2, full))
-            add(full, ALL, s2_, xav(1, full), xav(2, full))
-            send(k, 4, A.at[idx(fa, o1, s2_)], xbv(0, fa), d1p)
-            if fb is not None: send(k, 5, A.at[idx(fb, o1, s2_)], xbv(0, fb), d1m)
-        def st4():
-            recv(k, 4, xbv(0, fa)); add(fa, p1, s2_, xbv(0, fa))
-            send(k, 6, A.at[idx(full, p1, s2_)], xbv(1, full), d1p)
-            if fb is not None:
-                recv(k, 5, xbv(0, fb)); add(fb, m1, s2_, xbv(0, fb))
-            send(k, 7, A.at[idx(full, m1, s2_)], xbv(2, full), d1m)
-        def st5():
-            recv(k, 6, xbv(1, full)); recv(k, 7, xbv(2, full))
-            add(full, s1_, s2_, xbv(1, full), xbv(2, full))
-        return [st0, st1, st2, st3, st4, st5]
-
-    table = {}
-    keys = {}
-    k = 0
-    for p, cl in enumerate(ag_chunks()):
-        lst = []
-        for ch in cl:
-            lst.append(steps(k, p, ch)); keys.setdefault(p, []).append(k); k += 1
-        table[p] = lst
-    def st(p, s):
-        for ch in table[p]: ch[s]()
+                recv(k, 4 * l + 1, inbox(l, 0, fb)); add(ours(l, at[-1], fb), inbox(l, 0, fb))
+            send(k, 4 * l + 3, ours(l, at[-1], full), inbox(l, 2, full), to[-1])
+        def here(l):
+            at, to = rings[axes[l]]
+            full = parts[l][0]
+            recv(k, 4 * l + 2, inbox(l, 1, full)); recv(k, 4 * l + 3, inbox(l, 2, full))
+            add(ours(l, at[0], full), inbox(l, 1, full), inbox(l, 2, full))
+            if l: opposite(l - 1)
+        out = [start, join]
+        for l in range(last, -1, -1):
+            out += [functools.partial(near, l), functools.partial(here, l)]
+        return out
+
+    from_sib_view = {}
+    def unit_chunk(k, axes, staged, *parts):
+        def at_level(l, at):
+            return [(z, at), (at, ALL)][l] if axes == "xz" else [(at, x), (ALL, at)][l]
+        def cut(ref, part, l, at):
+            u0, u1, l0, l1 = part
+            zs, xs = at_level(l, at)
+            return ref.at[u0:u1, zs, xs, :, l0:l1]
+        def inbox(l, way, part):
+            u0, u1, l0, l1 = part
+            return xb.at[way, u0:u1, :, l0:l1] if l == 0 else xa.at[way, u0:u1, :, :, l0:l1]
+        u0, u1, l0, l1 = parts[0]
+        from_sib_view[k] = lambda place: cut(sg, parts[0], 1, place)
+        return steps(k, axes, lambda l, at, part: cut(acc, part, l, at), staged, sg.at[u0:u1, :, :, :, l0:l1], inbox, [parts, parts])
+    def fc2_chunk(k):
+        def ours(l, at, part):
+            a, b = part
+            if l == 0: return acc2.at[z, at, y, a:b]
+            if l == 1: return acc2.at[at, a:b, y]
+            return acc2.at[a:b, :, at]
+        def inbox(l, way, part):
+            a, b = part
+            return (xd, xc, xa2)[l].at[way, a:b]
+        ring = ((0, 4), (0, 2), (2, 4))
+        from_sib_view[k] = lambda place: sg2.at[:, :, place]
+        return steps(k, "xzy", ours, sta2, sg2, inbox, [((0, 48), (0, 32), (32, 48)), ring, ring])
+
+    lanes = lambda u, l0, lm, l1: ((u, u + 1, l0, l1), (u, u + 1, l0, lm), (u, u + 1, lm, l1))
+    pair = lambda u: ((u, u + 2, 0, LW), (u, u + 1, 0, LW), (u + 1, u + 2, 0, LW))
+    table = {
+        "fc2": fc2_chunk(0),
+        "dec": unit_chunk(1, "xz", stc.at[:, :, :, :, 0:256], *lanes(8, 0, 128, 256)),
+        "f1a": unit_chunk(2, "xz", sta.at[0:2], *pair(4)),
+        "f1b": unit_chunk(3, "xz", sta.at[2:4], *pair(6)),
+        "out": unit_chunk(4, "zx", sta.at[3:4], *lanes(3, 0, 256, LW)),
+        "q0": unit_chunk(5, "xz", sta.at[0:1], *lanes(0, 0, 256, LW)),
+        "q1": unit_chunk(6, "zx", sta.at[1:2], *lanes(1, 0, 256, LW)),
+        "q2": unit_chunk(8, "xz", sta.at[2:3, :, :, :, 0:256], *lanes(2, 0, 128, 256)),
+        "q3": unit_chunk(9, "zx", sta.at[2:3, :, :, :, 256:LW], (2, 3, 256, LW), (2, 3, 256, LW), None),
+    }
+    def st(s, *names):
+        for n in names: table[n][s]()
+
+    def send_small(v):
+        vout[...] = v.reshape(4, 4, 48, 128)
+        vin[4 * z + x] = vout[z, x]
+        for i, zz, xx, _, _ in plane:
+            cp = pltpu.make_async_remote_copy(vout.at[zz, xx], vin.at[4 * z + x], vss.at[i], vrs.at[i], device_id=dev(zz, xx, y, c), device_id_type=MESH)
+            cp.start(); lasts.append(cp)
+    def sum_small():
+        for i, zz, xx, sz, sx in plane:
+            pltpu.make_async_remote_copy(vout.at[zz, xx], vin.at[4 * sz + sx], vss.at[i], vrs.at[i], device_id=dev(zz, xx, y, c), device_id_type=MESH).wait_recv()
+        acc[8, z, x, :, 256:LW] = jnp.sum(vin[...].astype(f32), axis=0).astype(bf16)
+
+    lasts = []
+    me = 2 * y + c
+    def last_exchange(j, pt, units):
+        rs_ = slice(32 * j, 32 * j + 32)
+        blk = jnp.concatenate([acc[u, z, x] for u in units], axis=0)
+        fs[:, rs_] = jnp.dot(pt[...], blk, preferred_element_type=f32).astype(bf16).reshape(8, 32, LW)
+        own = pltpu.make_async_copy(fs.at[me, rs_], f1.at[me, rs_], loc.at[j])
+        own.start()
+        got = []
+        for i, (dy, dc, t) in enumerate(group):
+            dst = 2 * ((y + dy) % 4) + (c + dc) % 2
+            cp = pltpu.make_async_remote_copy(fs.at[dst, rs_], f1.at[me, rs_], ss1.at[j, i], rs1.at[j, i], device_id=t, device_id_type=MESH)
+            cp.start()
+            src = 2 * ((y + 4 - dy) % 4) + (c + dc) % 2
+            rc = pltpu.make_async_remote_copy(fs.at[me, rs_], f1.at[src, rs_], ss1.at[j, i], rs1.at[j, i], device_id=t, device_id_type=MESH)
+            lasts.append(cp); got.append(rc)
+        def finish():
+            own.wait()
+            for rc in got: rc.wait_recv()
+            for h in range(2):
+                t = f1[h, rs_].astype(f32)
+                for yy in range(1, 4): t = t + f1[2 * yy + h, rs_].astype(f32)
+                fo[h, rs_] = t
+        return finish
+    def fc2_exchange():
+        v = acc2[z, x, y].astype(f32)
+        pad = jnp.zeros((8, LW), f32)
+        for k in range(2):
+            fs2[k] = jnp.concatenate([v[24 * k:24 * k + 24], pad], axis=0).astype(bf16)
+        cp = pltpu.make_async_remote_copy(fs2.at[o], f2, ss1.at[0, 7], rs1.at[0, 7], device_id=sib, device_id_type=MESH)
+        cp.start(); lasts.append(cp)
+        of2_ref[:, pl.ds(pl.multiple_of(c * LW, LW), LW)] = jnp.where(c == 0, v[0:24], v[24:48])
+        def finish():
+            cp.wait_recv()
+            of2_ref[:, pl.ds(pl.multiple_of(o * LW, LW), LW)] = f2[...].astype(f32)[0:24]
+        return finish
 
     def blocks(body, n=7):
         def step(i, _):
@@ -651,7 +748,7 @@
     def grad_fc2(h, dst):
         def part(i, _):
             t = lax.dot_general(act_ref[:, col(i * 768, 768, 768)], dm[:, col(h * LW, LW, LW)], TN, preferred_element_type=f32)
-            dst[i] = t.astype(bf16).reshape(4, 192, LW)
+            dst[i] = t.astype(bf16).reshape(4, 4, 48, LW)
             return 0
         lax.fori_loop(0, 4, part, 0)
 
@@ -703,32 +800,32 @@
         df[:, 0:768] = t.astype(bf16)
 
     def load_p(i):
-        return pltpu.make_async_copy(p_hbm.at[pl.ds(2 * i, 2)], pb.at[i % 2], psem.at[i % 2])
-
-    def attn_back(lo, hi):
+        return pltpu.make_async_copy(p_hbm.at[pl.ds(2 * (i // 2 + 3 * (i % 2)), 2)], pb.at[i % 2], psem.at[i % 2])
+
+    def attn_back(u):
         low = lax.broadcasted_iota(jnp.int32, (1, 128), 1) < 64
-        def pair(i, _):
-            load_p(i).wait()
-            pl.when(i + 1 < HEADS_PAIRS)(lambda: load_p(i + 1).start())
-            def cols(ref, base):
-                return ref[:, col(base + i * 128, 128, 128)]
-            q, kk, v, do = cols(qkv_ref, 0), cols(qkv_ref, 768), cols(qkv_ref, 1536), cols(df, 0)
+        def pair(j, _):
+            load_p(2 * u + j).wait()
+            i = u + 3 * j
+            def cols(b):
+                return qkv_ref[:, col(LW * i + 128 * b, 128, 128)]
+            q, kk, v, do = cols(0), cols(1), cols(2), df[:, col(i * 128, 128, 128)]
             r = []
             for t in range(2):
                 keep = low if t == 0 else jnp.logical_not(low)
-                pr = pb[i % 2, t]
+                pr = pb[j, t]
                 dp = lax.dot_general(jnp.where(keep, do, jnp.zeros_like(do)), v, NT, preferred_element_type=f32)
                 p32 = pr.astype(f32)
                 ds = (p32 * (dp - jnp.sum(dp * p32, axis=-1, keepdims=True))).astype(bf16)
                 dv = lax.dot_general(pr, do, TN, preferred_element_type=f32)
                 dq = jnp.dot(ds, kk, preferred_element_type=f32)
                 dk = lax.dot_general(ds, q, TN, preferred_element_type=f32)
-                r.append((dq, dk, dv))
-            dqkv[:, col(i * 128, 128, 128)] = (0.125 * jnp.where(low, r[0][0], r[1][0])).astype(bf16)
-            dqkv[:, col(768 + i * 128, 128, 128)] = (0.125 * jnp.where(low, r[0][1], r[1][1])).astype(bf16)
-            dqkv[:, col(1536 + i * 128, 128, 128)] = jnp.where(low, r[0][2], r[1][2]).astype(bf16)
+                r.append((0.125 * dq, 0.125 * dk, dv))
+            for b in range(3):
+                dqkv[:, col(LW * i + 128 * b, 128, 128)] = jnp.where(low, r[0][b], r[1][b]).astype(bf16)
+            if u < 2: load_p(2 * u + j + 2).start()
             return 0
-        lax.fori_loop(lo, hi, pair, 0)
+        lax.fori_loop(0, 2, pair, 0)
 
     def qkv_back():
         for h in range(2):
@@ -738,12 +835,9 @@
                 t = lax.dot_general(dqkv[:, h * 1152:(h + 1) * 1152], wt(rs), NT, preferred_element_type=f32)
                 dh[:, rs] = t if h == 0 else dh[:, rs] + t
 
-    def grad_qkv(h, dst):
-        def part(u, _):
-            t = lax.dot_general(a_ref[...], dqkv[:, col(h * 1152 + u * LW, LW, LW)], TN, preferred_element_type=f32)
-            dst[u] = t.astype(bf16).reshape(4, 4, 48, LW)
-            return 0
-        lax.fori_loop(0, 3, part, 0)
+    def grad_qkv(u, h, dst):
+        t = lax.dot_general(a_ref[...], dqkv[:, col(h * 1152 + u * LW, LW, LW)], TN, preferred_element_type=f32)
+        dst[u] = t.astype(bf16).reshape(4, 4, 48, LW)
     def grad_out(h, dst):
         t = lax.dot_general(o_ref[...], dm[:, col(h * LW, LW, LW)], TN, preferred_element_type=f32)
         dst[3] = t.astype(bf16).reshape(4, 4, 48, LW)
@@ -773,82 +867,77 @@
     def stc8(v, cs): stc[0, :, :, :, cs] = v
 
     need("dm", "act")
-    grad_fc2(o, sta2); st(2, 0)
+    grad_fc2(o, sta2); st(0, "fc2")
     grad_fc2(c, acc2)
     vsum[4:5, 0:768] = jnp.sum(dm[...].astype(f32), axis=0, keepdims=True)
+    need("e", "dz")
+    grad_dec(o, stc8); st(0, "dec")
+    grad_dec(c, acc8)
     need("fc2", "dact")
     fc2_back()
-    st(2, 1)
+    st(1, "fc2", "dec")
+    need("h2")
+    grad_fc1(o, sta, 0); st(0, "f1a", "f1b")
+    grad_fc1(c, acc, 4)
+    st(2, "dec")
     need("fc1")
     fc1_back()
     ld_c.start()
-    load_p(0).start()
-    need("h2")
-    grad_fc1(o, sta, 0); st(1, 0)
-    st(2, 2)
-    grad_fc1(c, acc, 4)
+    load_p(0).start(); load_p(1).start()
+    st(1, "f1a", "f1b")
     need("x2", "dx", "rows")
     norm_back(x2_ref, 2, dx, dm, 2)
-    st(2, 3); st(1, 1)
     ld_c.wait()
-    for kk in keys[1]: sends[kk, 8].wait_send(); del sends[kk, 8]
+    for kk in (2, 3): sends[kk, 12].wait_send(); del sends[kk, 12]
     need("o", "qkv")
-    grad_out(o, sta); grad_out(c, acc)
+    grad_out(o, sta); st(0, "out")
+    grad_out(c, acc)
     out_back()
-    st(2, 4); st(1, 2)
-    attn_back(0, 3)
-    st(2, 5); st(1, 3)
-    attn_back(3, 6)
-    st(1, 4)
+    st(3, "dec"); st(1, "out")
     need("a")
-    grad_qkv(o, sta)
-    st(0, 0)
-    grad_qkv(c, acc)
-    st(1, 5)
+    attn_back(0)
+    st(2, "f1a", "f1b")
+    grad_qkv(0, o, sta); st(0, "q0"); grad_qkv(0, c, acc)
+    st(2, "fc2"); st(2, "out"); st(4, "dec")
+    attn_back(1)
+    st(3, "out"); st(5, "dec"); st(1, "q0")
+    grad_qkv(1, o, sta); st(0, "q1"); grad_qkv(1, c, acc)
+    st(3, "f1a", "f1b")
+    attn_back(2)
+    st(2, "q0"); st(1, "q1"); st(3, "fc2")
+    grad_qkv(2, o, sta); st(0, "q2", "q3"); grad_qkv(2, c, acc)
+    st(4, "out", "f1a", "f1b"); st(3, "q0"); st(4, "fc2")
     qkv_back()
-    need("tok", "vs", "e", "dz")
+    st(1, "q2", "q3"); st(2, "q1"); st(5, "out", "f1a", "f1b", "fc2")
+    finish_first = last_exchange(0, pt1_ref, (4, 5, 6, 7))
+    need("tok", "vs")
     vsum[9:11, 0:512] = vs[9:11, :]
     norm_back(tok, 0, dx, None, 0)
+    st(2, "q2", "q3")
+    send_small(vec_cols())
     dh[0:512 - ROWS, :] = jnp.zeros((512 - ROWS, 768), f32)
     tgs = [pltpu.make_async_copy(dx, tg_ref.at[0:ROWS], tsem.at[0]), pltpu.make_async_copy(dh.at[0:512 - ROWS], tg_ref.at[ROWS:512], tsem.at[1])]
     for t in tgs: t.start()
-    st(0, 1)
-    v = vec_cols().reshape(4, 4, 48, 128)
-    zero = jnp.zeros_like(v)
-    acc8(jnp.where(c == 0, v, zero), slice(256, 384)); stc8(jnp.where(c == 0, zero, v), slice(256, 384))
-    grad_dec(o, stc8)
-    st(3, 0)
-    grad_dec(c, acc8)
-    st(0, 2); st(3, 1); st(0, 3); st(3, 2); st(0, 4); st(3, 3); st(0, 5); st(3, 4); st(3, 5)
-
-    blk = jnp.concatenate([acc[:, z, x].reshape(432, LW), acc2[z, x]], axis=0)
-    fs[...] = jnp.dot(pt_ref[...], blk, preferred_element_type=f32).astype(bf16).reshape(8, SROWS, LW)
-    me = 2 * y + c
-    own = pltpu.make_async_copy(fs.at[me], f1.at[me], loc)
-    own.start()
-    lasts = []
-    for i, (dy, dc, t) in enumerate(group):
-        dst = 2 * ((y + dy) % 4) + (c + dc) % 2
-        cp = pltpu.make_async_remote_copy(fs.at[dst], f1.at[me], ss1.at[i], rs1.at[i], device_id=t, device_id_type=MESH)
-        cp.start()
-        src = 2 * ((y + 4 - dy) % 4) + (c + dc) % 2
-        rc = pltpu.make_async_remote_copy(fs.at[me], f1.at[src], ss1.at[i], rs1.at[i], device_id=t, device_id_type=MESH)
-        lasts.append((cp, rc))
-    own.wait()
-    for cp, rc in lasts: rc.wait_recv()
+    st(3, "q1"); st(4, "q0"); st(6, "fc2")
+    st(3, "q2", "q3"); st(5, "q0"); st(4, "q1"); st(7, "fc2")
+    finish_fc2 = fc2_exchange()
+    st(4, "q2", "q3"); st(5, "q1")
+    sum_small()
+    finish_fc2(); finish_first()
+    st(5, "q2", "q3")
+    finish_second = last_exchange(1, pt2_ref, (0, 1, 2, 3, 8))
     for h in range(2):
-        t = f1[h].astype(f32)
-        for yy in range(1, 4): t = t + f1[2 * yy + h].astype(f32)
-        fo[h] = t
+        for u in range(4):
+            of1_ref[:, h * 1536 + u * LW:h * 1536 + (u + 1) * LW] = fo[h, 6 * u:6 * u + 6, :]
+    finish_second()
     for h in range(2):
         for u in range(3):
-            oq_ref[:, h * 1152 + u * LW:h * 1152 + (u + 1) * LW] = fo[h, 6 * u:6 * u + 6, :]
-        oo_ref[:, h * LW:(h + 1) * LW] = fo[h, 18:24, :]
-        for u in range(4):
-            of1_ref[:, h * 1536 + u * LW:h * 1536 + (u + 1) * LW] = fo[h, 24 + 6 * u:30 + 6 * u, :]
-        of2_ref[:, h * LW:(h + 1) * LW] = fo[h, 48:72, :]
-        od_ref[:, h * 256:(h + 1) * 256] = fo[h, 72:78, 0:256]
-    vt[0:6, :] = fo[0, 72:78, 256:384]
+            for b in range(3):
+                first = 768 * b + 128 * (3 * h + u)
+                oq_ref[:, first:first + 128] = fo[h, 32 + 6 * u:38 + 6 * u, 128 * b:128 * b + 128]
+        oo_ref[:, h * LW:(h + 1) * LW] = fo[h, 50:56, :]
+        od_ref[:, h * 256:(h + 1) * 256] = fo[h, 56:62, 0:256]
+    vt[0:6, :] = fo[0, 56:62, 256:384] + fo[1, 56:62, 256:384]
     vrows = vt[...].T
     for i, r in enumerate((v0_ref, v1_ref, v2_ref, v3_ref, v4_ref)):
         r[...] = vrows[i:i + 1, 0:6]
@@ -858,12 +947,11 @@
     vm_ref[...] = vrows[10:11, 0:4]
     finish_cells()
     for t in tgs: t.wait()
-    for cp, rc in lasts: cp.wait_send()
+    for cp in lasts: cp.wait_send()
     for cp in sends.values(): cp.wait_send()
 
 
 def k2_call(*args):
-    nk = sum(len(c) for c in ag_chunks())
     S = jax.ShapeDtypeStruct
     vm = pl.BlockSpec(memory_space=pltpu.VMEM)
     anyspec = pl.BlockSpec(memory_space=pl.ANY)
@@ -873,27 +961,28 @@
     return pl.pallas_call(
         k2_kernel,
         out_shape=outs,
-        in_specs=[anyspec] * 18 + [vm] * 3,
+        in_specs=[anyspec] * 18 + [vm] * 4,
         out_specs=[anyspec] * 2 + [vm] * 13,
         scratch_shapes=[
             V((8, 3072), f32), V((ROWS, 768), bf16), V((ROWS, 2304), bf16), V((ROWS, 768), bf16), V((ROWS, 768), f32),
             V((ROWS, 768), bf16), V((ROWS, 3072), bf16), V((ROWS, 3072), bf16), V((ROWS, 768), bf16), V((ROWS, 512), bf16),
             V((ROWS, 768), f32), V((ROWS, 768), bf16), V((16, 512), f32), V((ROWS, 768), bf16),
-            V((2, 4, 4, 192, LW), bf16), V((2, 4, 4, 4, 48, LW), bf16),
-            V((4, 4, 4, 48, LW), bf16), V((4, 4, 192, LW), bf16), V((1, 4, 4, 48, LW), bf16),
-            V((9, 4, 4, 48, LW), bf16), V((4, 4, 192, LW), bf16),
-            V((9, 4, 4, 48, LW), bf16), V((4, 4, 192, LW), bf16),
-            V((3, 9, 4, 48, LW), bf16), V((3, 4, 192, LW), bf16),
-            V((3, 9, 48, LW), bf16), V((3, 192, LW), bf16),
+            V((2, 4, 4, 4, 48, LW), bf16), V((2, 4, 4, 4, 48, LW), bf16),
+            V((4, 4, 4, 48, LW), bf16), V((4, 4, 4, 48, LW), bf16), V((1, 4, 4, 48, LW), bf16),
+            V((9, 4, 4, 48, LW), bf16), V((4, 4, 4, 48, LW), bf16),
+            V((9, 4, 4, 48, LW), bf16), V((4, 4, 4, 48, LW), bf16),
+            V((3, 9, 4, 48, LW), bf16), V((3, 4, 4, 48, LW), bf16),
+            V((3, 9, 48, LW), bf16), V((3, 4, 48, LW), bf16), V((3, 48, LW), bf16),
             V((ROWS, 768), f32), V((ROWS, 3072), bf16), V((ROWS, 2304), bf16), V((16, 3072), f32), V((2, 2, ROWS, ROWS), bf16),
-            V((8, SROWS, LW), bf16), V((8, SROWS, LW), bf16), V((2, SROWS, LW), f32), V((64, 512), bf16), V((128, 128), f32),
-            DMA((nk, 9)), DMA((nk, 9)), DMA((7,)), DMA((7,)), DMA(()), DMA((1,)), DMA((2,)), DMA((2,)), DMA((16,)),
-            DMA((32,)), DMA((32,)), DMA((3,)),
+            V((8, YROWS, LW), bf16), V((8, YROWS, LW), bf16), V((2, YROWS, LW), f32), V((2, 32, LW), bf16), V((32, LW), bf16), V((64, 512), bf16), V((128, 128), f32), V((4, 4, 48, 128), bf16), V((16, 48, 128), bf16),
+            DMA((10, 13)), DMA((10, 13)), DMA((2, 8)), DMA((2, 8)), DMA((2,)), DMA((1,)), DMA((2,)), DMA((2,)), DMA((16,)),
+            DMA((32,)), DMA((32,)), DMA((3,)), DMA((16,)), DMA((16,)),
         ],
         compiler_params=pltpu.CompilerParams(collective_id=1, has_side_effects=True, vmem_limit_bytes=60 * 2**20),
         cost_estimate=pl.CostEstimate(flops=12 * 10**9, bytes_accessed=5 * 10**7, transcendentals=0),
         name="backward",
-    )(*args, jnp.asarray(perm_matrix().T, bf16), jnp.asarray(cell_spread(), bf16), jnp.asarray(fc1_bias_spread(), bf16))
+    )(*args, jnp.asarray(spread_matrix((4, 5, 6, 7), 0), bf16), jnp.asarray(spread_matrix((0, 1, 2, 3, 8), 32), bf16),
+      jnp.asarray(cell_spread(), bf16), jnp.asarray(fc1_bias_spread(), bf16))
 
 
 def k3_kernel(inv, arr, tg, *refs):

time: 219 us -> 185 us (0.84)
  Pallas kernels: 218 us -> 184 us
    pallas_call x1, Pallas kernels: 107 us -> 89.5 us  [k1_call(): pl.pallas_call(k1_kernel, out_shape=outs, in_specs=[smem, smem] + [vm] *...]
    pallas_call x1, Pallas kernels: 105 us -> 89 us  [k2_call(): pl.pallas_call(k2_kernel, out_shape=outs, in_specs=[anyspec] * 18 + [vm]...]
where the time goes in v4:
time: 185 us
  Pallas kernels  184 us (99%)
    pallas_call x1, Pallas kernels, k1_call(): pl.pallas_call(k1_kernel, out_shape=outs, in_specs=[smem, smem] + [vm] *...  89.5 us
    pallas_call x1, Pallas kernels, k2_call(): pl.pallas_call(k2_kernel, out_shape=outs, in_specs=[anyspec] * 18 + [vm]...  89 us
    pallas_call x1, Pallas kernels, k3_call(): pl.pallas_call(k3_kernel, out_shape=(S((32, 64, 512), bf16), S((512, 768)...  5.37 us

profile of v4, /device:TPU:1, one launch (start us, length us, event | category | flops | bytes accessed | tf_op | source)
XLA Modules:
  0.0 184.7 jit_solution(12704219938077057731)
XLA Ops:
  0.7 89.5 %forward.1 = (bf16[2,9,4,4,48,384]{5,4,3,2,1,0:T(8,128)(2,1)}, bf16[2,4,4,4,48,384]{5,4,3,2,1,0:T(8,128)(2,1)}, f32[8,3072]{1,0:T(8,128)}, bf16[336,768]{1,0:T(8...) custom-call(s32[2]{0:T(128)} %ids.1, s32[2]{0:T(128)} %lens.1, ...), custom_call_target="tpu_custom_call" | custom-call | flops 6000000000 | bytes 50000000 | tf_op jit(solution)/shard_map/forward/pallas_call | solution.py:510
  90.1 89.0 %backward.1 = (f32[512,768]{1,0:T(8,128)}, bf16[33,64,512]{2,1,0:T(8,128)(2,1)}, f32[6,2304]{1,0:T(8,128)}, f32[6,768]{1,0:T(8,128)}, f32[6,3072]{1,0:T(8,128)},...) custom-call(bf16[2,9,4,4,48,384]{5,4,3,2,1,0:T(8,128)(2,1)} %get-tup, ...), custom_call_target="tpu_custom_call" | custom-call | flops 12000000000 | bytes 50000000 | tf_op jit(solution)/shard_map/backward/pallas_call | solution.py:961
  179.1 5.4 %results.1 = (bf16[32,64,512]{2,1,0:T(8,128)(2,1)}, f32[512,768]{1,0:T(8,128)}, f32[6,2304]{1,0:T(8,128)}, f32[6,768]{1,0:T(8,128)}, f32[6,3072]{1,0:T(8,128)}, ...) custom-call(s32[8,128]{1,0:T(8,128)} %get-tuple-element.63.inv, ...), custom_call_target="tpu_custom_call" | custom-call | tf_op jit(solution)/shard_map/results/pallas_call | solution.py:1009

commit v5 on v4

--- a/solution.py
+++ b/solution.py
@@ -201,6 +201,7 @@
         own_dc.start()
         for r, g in peers(f):
             to_peer(r, g).start()
+    def send_small_cotangents():
         @pl.when(few)
         def _():
             own_small.start()
@@ -461,6 +462,7 @@
     place(1); go(0, "1a", "1b")
     go(2, 0, 3, 2)
     sort_cotangents(); keep("inv")
+    send_small_cotangents()
     go(1, "1a", "1b")
     go(3, 2, 0, 3)
     go(2, "1a", "1b")

time: 185 us -> 183 us (0.989)
  Pallas kernels: 184 us -> 181 us
    pallas_call x1, Pallas kernels: 89.5 us -> 86.8 us  [k1_call(): pl.pallas_call(k1_kernel, out_shape=outs, in_specs=[smem, smem] + [vm] *...]
where the time goes in v5:
time: 183 us; the launch traced here: 182 us
  Pallas kernels  181 us (99%)
    pallas_call x1, Pallas kernels, k2_call(): pl.pallas_call(k2_kernel, out_shape=outs, in_specs=[anyspec] * 18 + [vm]...  89.2 us
    pallas_call x1, Pallas kernels, k1_call(): pl.pallas_call(k1_kernel, out_shape=outs, in_specs=[smem, smem] + [vm] *...  86.8 us
    pallas_call x1, Pallas kernels, k3_call(): pl.pallas_call(k3_kernel, out_shape=(S((32, 64, 512), bf16), S((512, 768)...  5.37 us

profile of v5, /device:TPU:1, one launch (start us, length us, event | category | flops | bytes accessed | tf_op | source)
XLA Modules:
  0.0 182.3 jit_solution(1241528528725907122)
XLA Ops:
  0.7 86.8 %forward.1 = (bf16[2,9,4,4,48,384]{5,4,3,2,1,0:T(8,128)(2,1)}, bf16[2,4,4,4,48,384]{5,4,3,2,1,0:T(8,128)(2,1)}, f32[8,3072]{1,0:T(8,128)}, bf16[336,768]{1,0:T(8...) custom-call(s32[2]{0:T(128)} %ids.1, s32[2]{0:T(128)} %lens.1, ...), custom_call_target="tpu_custom_call" | custom-call | flops 6000000000 | bytes 50000000 | tf_op jit(solution)/shard_map/forward/pallas_call | solution.py:512
  87.5 89.2 %backward.1 = (f32[512,768]{1,0:T(8,128)}, bf16[33,64,512]{2,1,0:T(8,128)(2,1)}, f32[6,2304]{1,0:T(8,128)}, f32[6,768]{1,0:T(8,128)}, f32[6,3072]{1,0:T(8,128)},...) custom-call(bf16[2,9,4,4,48,384]{5,4,3,2,1,0:T(8,128)(2,1)} %get-tup, ...), custom_call_target="tpu_custom_call" | custom-call | flops 12000000000 | bytes 50000000 | tf_op jit(solution)/shard_map/backward/pallas_call | solution.py:963
  176.7 5.4 %results.1 = (bf16[32,64,512]{2,1,0:T(8,128)(2,1)}, f32[512,768]{1,0:T(8,128)}, f32[6,2304]{1,0:T(8,128)}, f32[6,768]{1,0:T(8,128)}, f32[6,3072]{1,0:T(8,128)}, ...) custom-call(s32[8,128]{1,0:T(8,128)} %get-tuple-element.63.inv, ...), custom_call_target="tpu_custom_call" | custom-call | tf_op jit(solution)/shard_map/results/pallas_call | solution.py:1011

commit v6 on v5

--- a/solution.py
+++ b/solution.py
@@ -990,17 +990,19 @@
 def k3_kernel(inv, arr, tg, *refs):
     n = len(refs) - 3
     small, (grid, tg_out, *outs), (gv, tv, sem) = refs[:13], refs[13:n], refs[n:]
-    ins = [pltpu.make_async_copy(tg, tv, sem.at[0])]
-    ins += [pltpu.make_async_copy(arr.at[inv[0, r]], gv.at[r], sem.at[1 + r]) for r in range(32)]
+    part = lambda i: pl.ds(128 * i, 128)
+    ins = [pltpu.make_async_copy(tg.at[part(i)], tv.at[part(i)], sem.at[i]) for i in range(4)]
+    ins += [pltpu.make_async_copy(arr.at[inv[0, r]], gv.at[r], sem.at[4 + r]) for r in range(32)]
     for cp in ins: cp.start()
     for a, b in zip(small, outs): b[...] = a[...]
-    back = [pltpu.make_async_copy(tv, tg_out, sem.at[33])]
-    back += [pltpu.make_async_copy(gv.at[pl.ds(8 * i, 8)], grid.at[pl.ds(8 * i, 8)], sem.at[34 + i]) for i in range(4)]
-    ins[0].wait()
-    back[0].start()
+    back = [pltpu.make_async_copy(tv.at[part(i)], tg_out.at[part(i)], sem.at[36 + i]) for i in range(4)]
+    back += [pltpu.make_async_copy(gv.at[pl.ds(4 * i, 4)], grid.at[pl.ds(4 * i, 4)], sem.at[40 + i]) for i in range(8)]
     for i in range(4):
-        for r in range(8): ins[1 + 8 * i + r].wait()
-        back[1 + i].start()
+        ins[i].wait()
+        back[i].start()
+    for i in range(8):
+        for r in range(4): ins[4 + 4 * i + r].wait()
+        back[4 + i].start()
     for cp in back: cp.wait()
 
 
@@ -1013,7 +1015,7 @@
         out_shape=(S((32, 64, 512), bf16), S((512, 768), f32)) + tuple(S(t.shape, t.dtype) for t in small),
         in_specs=[pl.BlockSpec(memory_space=pltpu.SMEM), anyspec, anyspec] + [vm] * 13,
         out_specs=[anyspec, anyspec] + [vm] * 13,
-        scratch_shapes=[pltpu.VMEM((32, 64, 512), bf16), pltpu.VMEM((512, 768), f32), pltpu.SemaphoreType.DMA((38,))],
+        scratch_shapes=[pltpu.VMEM((32, 64, 512), bf16), pltpu.VMEM((512, 768), f32), pltpu.SemaphoreType.DMA((48,))],
         name="results",
     )(inv, arr, tg, *small)
 

time: 183 us -> 183 us (level)
  no operation moved by 1% of the time
where the time goes in v6:
time: 183 us; the launch traced here: 182 us
  Pallas kernels  181 us (99%)
    pallas_call x1, Pallas kernels, k2_call(): pl.pallas_call(k2_kernel, out_shape=outs, in_specs=[anyspec] * 18 + [vm]...  89.2 us
    pallas_call x1, Pallas kernels, k1_call(): pl.pallas_call(k1_kernel, out_shape=outs, in_specs=[smem, smem] + [vm] *...  86.8 us
    pallas_call x1, Pallas kernels, k3_call(): pl.pallas_call(k3_kernel, out_shape=(S((32, 64, 512), bf16), S((512, 768)...  5.05 us

profile of v6, /device:TPU:1, one launch (start us, length us, event | category | flops | bytes accessed | tf_op | source)
XLA Modules:
  0.0 182.0 jit_solution(18200706521995568394)
XLA Ops:
  0.7 86.8 %forward.1 = (bf16[2,9,4,4,48,384]{5,4,3,2,1,0:T(8,128)(2,1)}, bf16[2,4,4,4,48,384]{5,4,3,2,1,0:T(8,128)(2,1)}, f32[8,3072]{1,0:T(8,128)}, bf16[336,768]{1,0:T(8...) custom-call(s32[2]{0:T(128)} %ids.1, s32[2]{0:T(128)} %lens.1, ...), custom_call_target="tpu_custom_call" | custom-call | flops 6000000000 | bytes 50000000 | tf_op jit(solution)/shard_map/forward/pallas_call | solution.py:512
  87.5 89.2 %backward.1 = (f32[512,768]{1,0:T(8,128)}, bf16[33,64,512]{2,1,0:T(8,128)(2,1)}, f32[6,2304]{1,0:T(8,128)}, f32[6,768]{1,0:T(8,128)}, f32[6,3072]{1,0:T(8,128)},...) custom-call(bf16[2,9,4,4,48,384]{5,4,3,2,1,0:T(8,128)(2,1)} %get-tup, ...), custom_call_target="tpu_custom_call" | custom-call | flops 12000000000 | bytes 50000000 | tf_op jit(solution)/shard_map/backward/pallas_call | solution.py:963
  176.7 5.1 %results.1 = (bf16[32,64,512]{2,1,0:T(8,128)(2,1)}, f32[512,768]{1,0:T(8,128)}, f32[6,2304]{1,0:T(8,128)}, f32[6,768]{1,0:T(8,128)}, f32[6,3072]{1,0:T(8,128)}, ...) custom-call(s32[8,128]{1,0:T(8,128)} %get-tuple-element.63.inv, ...), custom_call_target="tpu_custom_call" | custom-call | tf_op jit(solution)/shard_map/results/pallas_call | solution.py:1013
